TPU v7x, 32 devices: a whole 2x2x4 slice. The times are simulated.
32 devices in a mesh: inner: 8 (over y, x, core), outer: 4 (over z).
Axes of the slice: x: 2, y: 2, z: 4, core: 2. Of those that a mesh axis runs over, the one named last changes fastest.
Arguments:
- samples: bfloat16 [16384, 4096], P(('inner', 'outer')), may hold values from -6 to 6
- sketch_matrix: bfloat16 [4096, 128], P('inner'), may hold values from -0.09375 to 0.09375
Outputs:
- basis: float32 [16384, 128], P(('inner', 'outer'))
- projection: float32 [4096, 128], P('inner')
- row_error: float32 [16384], P(('inner', 'outer'))
All inputs are finite; a program needn't handle non-finite values.
Results may differ from a plain program's by a relative error of at most 0.0014.
Values may be sent and summed in bfloat16 or wider, within the bound.
No kernel may reach another device: no remote copies, remote signals or barrier semaphores. Data moves between devices by JAX's collectives and lax.ppermute only.
A program may use at most 64 MiB of HBM per device.

v0:
```python
import math

import jax
import jax.numpy as jnp
from jax import lax
from jax.sharding import PartitionSpec as P


def swapped(block, axis, stride):
    count = lax.axis_size(axis)
    route = []
    for low in range(count):
        high = low | 1 << stride
        if high != low and high < count:
            route += [(low, high), (high, low)]
    return lax.ppermute(block, axis, route)


def local(samples, sketch_matrix):
    local_rows = samples.shape[0]
    width = samples.shape[1]
    total_rows = local_rows * lax.axis_size("inner") * lax.axis_size("outer")
    columns = samples
    sketch = jnp.dot(
        columns,
        lax.all_gather(sketch_matrix, "inner", axis=0, tiled=True),
        preferred_element_type=jnp.float32,
    )
    gram_local = jnp.dot(sketch.T, sketch, precision=lax.Precision.HIGHEST)
    lower_factor = jnp.linalg.cholesky(gram_local)
    for level in range(lax.axis_size("inner").bit_length() - 1):
        partner = swapped(lower_factor, "inner", level)
        joined = jnp.dot(lower_factor, lower_factor.T, precision=lax.Precision.HIGHEST) + jnp.dot(
            partner, partner.T, precision=lax.Precision.HIGHEST
        )
        lower_factor = jnp.linalg.cholesky(joined)
    for level in range(lax.axis_size("outer").bit_length() - 1):
        partner = swapped(lower_factor, "outer", level)
        joined = jnp.dot(lower_factor, lower_factor.T, precision=lax.Precision.HIGHEST) + jnp.dot(
            partner, partner.T, precision=lax.Precision.HIGHEST
        )
        lower_factor = jnp.linalg.cholesky(joined)
    basis = lax.linalg.triangular_solve(
        lower_factor, sketch, left_side=False, lower=True, transpose_a=True
    )
    basis = basis * math.sqrt(total_rows)
    basis_low = basis.astype(jnp.bfloat16)
    columns = samples
    partial_rows = lax.psum_scatter(
        lax.dot_general(
            columns, basis_low, (((0,), (0,)), ((), ())), preferred_element_type=jnp.float32
        ),
        "inner",
        scatter_dimension=0,
        tiled=True,
    )
    summed = lax.psum(partial_rows, "outer")
    projection = summed * (math.sqrt(width) / total_rows)
    projection_low = projection.astype(jnp.bfloat16)
    columns = samples
    recon = lax.dot_general(
        basis_low,
        lax.all_gather(projection_low, "inner", axis=0, tiled=True),
        (((1,), (1,)), ((), ())),
        preferred_element_type=jnp.float32,
    ) / math.sqrt(width)
    diff = columns.astype(jnp.float32) - recon
    errors = jnp.sum(diff * diff, axis=1)
    return (basis, projection, errors / width)


def solution(mesh):
    placed = (P(("inner", "outer"), None), P("inner", None))
    return jax.shard_map(
        local,
        mesh=mesh,
        in_specs=placed,
        out_specs=(P(("inner", "outer"), None), P("inner", None), P(("inner", "outer"))),
        check_vma=False,
    )
```

profile of v0, /device:TPU:0, one launch (start us, length us, event | category | flops | bytes accessed | tf_op | source)
XLA Modules:
  0.0 271.8 jit_solution(10678209509113784983)
XLA Ops:
  7.2 0.7 all-gather.3.cloned.1.call-update
  7.9 28.2 %all-gather.3.cloned.1.call-done = bf16[4096,128]{1,0:T(8,128)(2,1)} async-done(((bf16[512,128]{1,0:T(8,128)(2,1)}), bf16[4096,128]{1,0:T(8,128)(2,1)}) %all-gather.3.cloned.1.call-update) | async-done | bytes 1048592 | tf_op jit(solution)/shard_map/all_gather | solution.py:26
  36.1 3.7 %fusion.21 = f32[512,128]{1,0:T(8,128)S(1)} fusion(bf16[512,4096]{1,0:T(8,128)(2,1)} %param.3, bf16[4096,128]{1,0:T(8,128)(2,1)} %all-gather.3.cloned.1.call-done), kind=kOutput, calls=%fused_computation.52 | convolution fusion | flops 536870912 | bytes 5505024 | tf_op jit(solution)/shard_map/dot_general | solution.py:24
  40.6 11.7 %cholesky.104 = f32[128,128]{1,0:T(8,128)S(1)} custom-call(f32[128,128]{1,0:T(8,128)S(1)} %fusion.7), custom_call_target="Cholesky" | custom-call | tf_op jit(solution)/shard_map/jit(cholesky)/cholesky | solution.py:30
  52.9 0.7 select_select_fusion.5
  54.2 0.7 collective-permute-done
  55.3 11.7 %cholesky.115 = f32[128,128]{1,0:T(8,128)S(1)} custom-call(f32[128,128]{1,0:T(8,128)S(1)} %fusion.6), custom_call_target="Cholesky" | custom-call | tf_op jit(solution)/shard_map/jit(cholesky)/cholesky | solution.py:36
  67.7 0.7 select_select_fusion.4
  68.4 1.5 collective-permute-start.1
  70.2 2.5 collective-permute-done.1
  73.1 11.9 %cholesky.126 = f32[128,128]{1,0:T(8,128)S(1)} custom-call(f32[128,128]{1,0:T(8,128)S(1)} %fusion.5), custom_call_target="Cholesky" | custom-call | tf_op jit(solution)/shard_map/jit(cholesky)/cholesky | solution.py:36
  85.7 0.7 select_select_fusion.3
  86.3 1.5 collective-permute-start.2
  88.1 2.6 collective-permute-done.2
  91.0 11.7 %cholesky.137 = f32[128,128]{1,0:T(8,128)S(1)} custom-call(f32[128,128]{1,0:T(8,128)S(1)} %fusion.4), custom_call_target="Cholesky" | custom-call | tf_op jit(solution)/shard_map/jit(cholesky)/cholesky | solution.py:36
  103.4 0.7 select_select_fusion.2
  104.1 1.6 collective-permute-start.3
  105.9 2.5 collective-permute-done.3
  108.8 11.7 %cholesky.148 = f32[128,128]{1,0:T(8,128)S(1)} custom-call(f32[128,128]{1,0:T(8,128)S(1)} %fusion.3), custom_call_target="Cholesky" | custom-call | tf_op jit(solution)/shard_map/jit(cholesky)/cholesky | solution.py:42
  121.2 0.7 select_select_fusion.1
  121.9 2.5 collective-permute-start.4
  124.6 2.5 collective-permute-done.4
  127.5 11.9 %cholesky.159 = f32[128,128]{1,0:T(8,128)S(1)} custom-call(f32[128,128]{1,0:T(8,128)S(1)} %fusion.2), custom_call_target="Cholesky" | custom-call | tf_op jit(solution)/shard_map/jit(cholesky)/cholesky | solution.py:42
  140.1 0.7 fusion
  140.7 9.8 %custom-call.5 = f32[1,128,128]{1,2,0:T(8,128)S(1)} custom-call(f32[1,128,128]{2,1,0:T(8,128)S(1)} %fusion), custom_call_target="InvertDiagBlocksLowerTriangular" | custom-call | tf_op jit(solution)/shard_map/triangular_solve | solution.py:43
  150.9 4.4 %convolution_bitcast_fusion = f32[4096,128]{0,1:T(8,128)} fusion(bf16[512,4096]{1,0:T(8,128)(2,1)} %param.3, f32[512,128]{1,0:T(8,128)S(1)} %convolution_multiply_fusion), kind=kOutput, calls=%fused_computation.1 | convolution fusion | flops 536936448 | bytes 6553600 | tf_op jit(solution)/shard_map/dot_general | solution.py:50
  155.4 42.0 %reduce-scatter.2.cloned.1.call-done = f32[512,128]{0,1:T(8,128)} async-done(((f32[4096,128]{0,1:T(8,128)}), f32[512,128]{0,1:T(8,128)}) %reduce-scatter.2.cloned.1.call-update) | async-done | bytes 262160 | tf_op jit(solution)/shard_map/reduce_scatter | solution.py:49
  197.5 37.8 %all-reduce.2.cloned.1.call-done = f32[512,128]{0,1:T(8,128)} async-done(((f32[512,128]{0,1:T(8,128)}), f32[512,128]{0,1:T(8,128)}) %all-reduce.2.cloned.1.call-update) | async-done | bytes 262160 | tf_op jit(solution)/shard_map/psum | solution.py:57
  235.2 1.6 fusion.20
  236.9 0.8 copy.21
  237.7 22.6 %all-gather.5.cloned.1.call-done = bf16[4096,128]{0,1:T(8,128)(2,1)} async-done(((bf16[512,128]{0,1:T(8,128)(2,1)}), bf16[4096,128]{0,1:T(8,128)(2,1)}) %all-gather.5.cloned.1.call-update) | async-done | bytes 1048592 | tf_op jit(solution)/shard_map/all_gather | solution.py:63
  260.4 4.3 %multiply_reduce_fusion = f32[512]{0:T(512)S(1)} fusion(bf16[512,4096]{1,0:T(8,128)(2,1)} %param.3, bf16[4096,128]{0,1:T(8,128)(2,1)} %all-gather.5.cloned.1.call-done, f32[512,128]{1,0:T(8,128)S(1)} %convolution_multiply_fusion), kind=kOutput, calls=%fused_computation | convolution fusion | flops 547421696 | bytes 5507072 | tf_op jit(solution)/shard_map/dot_general | solution.py:61
  (47 shorter events, 9.4 us)
Async XLA Ops:
  7.2 28.9 %all-gather.3.cloned.1.call-start = ((), (), s32[]{:S(2)}) async-start(), calls=%async_computation.1 | async-start | bytes 1179648 | tf_op jit(solution)/shard_map/all_gather | solution.py:26
  7.9 189.5 %reduce-scatter.2.cloned.1.call-start = ((), (), s32[]{:S(2)}) async-start(), calls=%async_computation.2 | async-start | bytes 2359296 | tf_op jit(solution)/shard_map/reduce_scatter | solution.py:49
  53.6 1.3 collective-permute-start
  68.4 4.3 %collective-permute-start.1 = (f32[128,128]{1,0:T(8,128)S(1)}, f32[128,128]{1,0:T(8,128)S(1)}, u32[]{:S(2)}, u32[]{:S(2)}) collective-permute-start(f32[128,128]{1,0:T(8,128)S(1)} %select_select_fusion.4), channel_id=1, source_target_pairs={{0,8},{8,0},{4,12},{12,4},{16,24},{24,16},{20,28},{28,20},{1,9},{9... | collective-permute-start | bytes 196616 | tf_op jit(solution)/shard_map/ppermute | solution.py:16
  86.3 4.3 %collective-permute-start.2 = (f32[128,128]{1,0:T(8,128)S(1)}, f32[128,128]{1,0:T(8,128)S(1)}, u32[]{:S(2)}, u32[]{:S(2)}) collective-permute-start(f32[128,128]{1,0:T(8,128)S(1)} %select_select_fusion.3), channel_id=1, source_target_pairs={{0,16},{16,0},{4,20},{20,4},{8,24},{24,8},{12,28},{28,12},{1,17},{... | collective-permute-start | bytes 196616 | tf_op jit(solution)/shard_map/ppermute | solution.py:16
  104.1 4.3 %collective-permute-start.3 = (f32[128,128]{1,0:T(8,128)S(1)}, f32[128,128]{1,0:T(8,128)S(1)}, u32[]{:S(2)}, u32[]{:S(2)}) collective-permute-start(f32[128,128]{1,0:T(8,128)S(1)} %select_select_fusion.2), channel_id=1, source_target_pairs={{0,1},{1,0},{2,3},{3,2},{4,5},{5,4},{6,7},{7,6},{8,9},{9,8},{10,11... | collective-permute-start | bytes 196616 | tf_op jit(solution)/shard_map/ppermute | solution.py:16
  121.9 5.2 %collective-permute-start.4 = (f32[128,128]{1,0:T(8,128)S(1)}, f32[128,128]{1,0:T(8,128)S(1)}, u32[]{:S(2)}, u32[]{:S(2)}) collective-permute-start(f32[128,128]{1,0:T(8,128)S(1)} %select_select_fusion.1), channel_id=1, source_target_pairs={{0,2},{2,0},{1,3},{3,1},{4,6},{6,4},{5,7},{7,5},{8,10},{10,8},{9,1... | collective-permute-start | bytes 196616 | tf_op jit(solution)/shard_map/ppermute | solution.py:16
  150.9 109.4 %copy-start = (f32[512,128]{1,0:T(8,128)}, f32[512,128]{1,0:T(8,128)S(1)}, u32[]{:S(2)}) copy-start(f32[512,128]{1,0:T(8,128)S(1)} %convolution_multiply_fusion) | copy-start | bytes 786436
  155.3 79.9 %all-reduce.2.cloned.1.call-start = ((), (), s32[]{:S(2)}) async-start(), calls=%async_computation.3 | async-start | bytes 524288 | tf_op jit(solution)/shard_map/psum | solution.py:57
  197.4 62.9 %all-gather.5.cloned.1.call-start = ((), (), s32[]{:S(2)}) async-start(), calls=%async_computation.4 | async-start | bytes 1179648 | tf_op jit(solution)/shard_map/all_gather | solution.py:63
Sparse Core Ops, SparseCore 0:
  9.9 26.1 all-gather.2
  155.5 41.9 reduce-scatter.1
  199.9 35.3 all-reduce.1
  237.0 23.2 all-gather.4
where the time goes:
time: 272 us
  waiting for transfers between devices  142 us (52%)
  other arithmetic  90.7 us (33%)
  matrix products  16 us (6%)
  between operations  14 us (5%)
  starting transfers between devices  7.54 us (3%)
    another operation x15, other arithmetic, local(): lower_factor = jnp.linalg.cholesky(joined)  62.3 us
    reduce_scatter x1, waiting for transfers between devices, local(): lax.psum_scatter(lax.dot_general(columns, basis_low, (((0,), (0,)), ((),...  42 us
    psum x1, waiting for transfers between devices, local(): summed = lax.psum(partial_rows, 'outer')  37.8 us
    all_gather x1, waiting for transfers between devices, local(): lax.all_gather(sketch_matrix, 'inner', axis=0, tiled=True)  28.2 us
    all_gather x1, waiting for transfers between devices, local(): lax.all_gather(projection_low, 'inner', axis=0, tiled=True)  22.6 us
    another operation x3, other arithmetic, local(): lower_factor = jnp.linalg.cholesky(gram_local)  12.4 us
    ppermute x5, waiting for transfers between devices, swapped(): return lax.ppermute(block, axis, route)  10.8 us
    another operation x2, other arithmetic, local(): lax.linalg.triangular_solve(lower_factor, sketch, left_side=False, lower=...  10.5 us
  transfers between devices with their start and end apart: 9, of which 9 were waited for; matrix products, arithmetic and copies ran while one was open for 1% of the time, Pallas kernels for 0%

commit v1 on v0

v1 whole, which is shorter than its diff:
```python
import math

import jax
import jax.numpy as jnp
from jax import lax
from jax.sharding import PartitionSpec as P


def flipped(block, axis, mask):
    count = lax.axis_size(axis)
    return lax.ppermute(block, axis, [(low, low ^ mask) for low in range(count)])


def exact_dot(a, b, contract):
    return lax.dot_general(
        a, b, (contract, ((), ())), precision=lax.Precision.HIGHEST, preferred_element_type=jnp.float32
    )


def summed_over(value, axis):
    for level in range(lax.axis_size(axis).bit_length() - 1):
        value = value + flipped(value, axis, 1 << level)
    return value


def local(samples, sketch_matrix):
    inner = lax.axis_size("inner")
    outer = lax.axis_size("outer")
    rows, width = samples.shape
    rank = sketch_matrix.shape[1]
    total_rows = rows * inner * outer
    me = lax.axis_index("inner")
    mine = lax.axis_index("outer")
    piece = width // inner
    part = piece // outer
    evens = range(2, inner, 2)

    got = {0: sketch_matrix}
    for mask in reversed(evens):
        got[mask] = flipped(sketch_matrix, "inner", mask)
    even = jnp.concatenate([got[mask] for mask in range(0, inner, 2)])
    odd = flipped(even, "inner", 1)

    def columns(masks):
        return jnp.concatenate(
            [lax.dynamic_slice_in_dim(samples, (me ^ mask) * piece, piece, 1) for mask in masks], axis=1
        )

    even_columns = columns(range(0, inner, 2))
    odd_columns = columns(range(1, inner, 2))
    sketch = jnp.dot(even_columns, even, preferred_element_type=jnp.float32)
    sketch = sketch + jnp.dot(odd_columns, odd, preferred_element_type=jnp.float32)

    gram = exact_dot(sketch, sketch, ((0,), (0,)))
    high = sketch.astype(jnp.bfloat16)
    low = (sketch - high.astype(jnp.float32)).astype(jnp.bfloat16)
    both = jnp.concatenate([high, low], axis=1)

    def products(side):
        twice = lax.dot_general(side, both, (((0,), (0,)), ((), ())), preferred_element_type=jnp.float32)
        return twice[:, :rank] + twice[:, rank:]

    pieces = products(even_columns) + flipped(products(odd_columns), "inner", 1)
    pieces = pieces.reshape(inner // 2, piece, rank)
    own = pieces[0]
    for mask in reversed(evens):
        own = own + flipped(pieces[mask // 2], "inner", mask)
    share = lax.dynamic_slice_in_dim(own, mine * part, part, 0)
    for mask in range(1, outer):
        share = share + flipped(
            lax.dynamic_slice_in_dim(own, (mine ^ mask) * part, part, 0), "outer", mask
        )

    gram = summed_over(summed_over(gram, "inner"), "outer")
    lower_factor = jnp.linalg.cholesky(gram)
    inverse = lax.linalg.triangular_solve(
        lower_factor, jnp.eye(rank, dtype=jnp.float32), left_side=False, lower=True, transpose_a=True
    )

    basis = exact_dot(sketch, inverse * math.sqrt(total_rows), ((1,), (0,)))
    basis_low = basis.astype(jnp.bfloat16)

    share = exact_dot(share, inverse * (math.sqrt(width) / math.sqrt(total_rows)), ((1,), (0,)))
    projection = jnp.zeros((piece, rank), jnp.float32)
    projection = lax.dynamic_update_slice_in_dim(projection, share, mine * part, 0)
    for mask in range(1, outer):
        projection = lax.dynamic_update_slice_in_dim(
            projection, flipped(share, "outer", mask), (mine ^ mask) * part, 0
        )
    projection_low = projection.astype(jnp.bfloat16)

    got = {0: projection_low}
    for mask in reversed(evens):
        got[mask] = flipped(projection_low, "inner", mask)
    even = jnp.concatenate([got[mask] for mask in range(0, inner, 2)])
    odd = flipped(even, "inner", 1)

    def errors(side, factor):
        recon = lax.dot_general(
            basis_low, factor, (((1,), (1,)), ((), ())), preferred_element_type=jnp.float32
        ) * (1.0 / math.sqrt(width))
        diff = side.astype(jnp.float32) - recon
        return jnp.sum(diff * diff, axis=1)

    row_error = (errors(even_columns, even) + errors(odd_columns, odd)) / width
    return (basis, projection, row_error)


def solution(mesh):
    placed = (P(("inner", "outer"), None), P("inner", None))
    return jax.shard_map(
        local,
        mesh=mesh,
        in_specs=placed,
        out_specs=(P(("inner", "outer"), None), P("inner", None), P(("inner", "outer"))),
        check_vma=False,
    )
```

time: 272 us -> 106 us (0.39)
  waiting for transfers between devices: 142 us -> 29.5 us
  other arithmetic: 90.7 us -> 27.6 us
  starting transfers between devices: 7.54 us -> 29.2 us
  between operations: 14 us -> 1.24 us
  local copies, waits for them, and re-layouts: 1.4 us -> 5.21 us
  matrix products: 16 us -> 12.7 us
    another operation x20 -> x5, other arithmetic: 85.2 us -> 23.7 us  [the longest x3 13.2 us: local(): lower_factor = jnp.linalg.cholesky(gram)]
    all_gather x2 -> x0, waiting for transfers between devices: 50.8 us -> none  [the longest x1 28.2 us: local(): lax.all_gather(sketch_matrix, 'inner', axis=0, tiled=True)]
    reduce_scatter x1 -> x0, waiting for transfers between devices: 42 us -> none  [local(): lax.psum_scatter(lax.dot_general(columns, basis_low, (((0,), (0,)), ((),...]
    psum x1 -> x0, waiting for transfers between devices: 37.8 us -> none  [local(): summed = lax.psum(partial_rows, 'outer')]
    ppermute x5 -> x23, starting transfers between devices: 7.38 us -> 29.2 us  [flipped(): lax.ppermute(block, axis, [(low, low ^ mask) for low in range(count)])]
    ppermute x5 -> x23, waiting for transfers between devices: 10.8 us -> 29.5 us  [flipped(): lax.ppermute(block, axis, [(low, low ^ mask) for low in range(count)])]
    select_n x5 -> x0, other arithmetic: 3.28 us -> none  [the longest x4 2.63 us: local(): lower_factor = jnp.linalg.cholesky(joined)]
    dot_general x14 -> x9, matrix products: 15.6 us -> 12.5 us  [the longest x2 6.23 us: errors(): lax.dot_general(basis_low, factor, (((1,), (1,)), ((), ())), preferred_el...]
  transfers between devices with their start and end apart: 9 -> 23, of which waited for: 9 -> 13; matrix products, arithmetic and copies ran while one was open for 1% -> 35% of each run, Pallas kernels for 0% -> 0%
where the time goes in v1:
time: 106 us
  waiting for transfers between devices  29.5 us (28%)
  starting transfers between devices  29.2 us (28%)
  other arithmetic  27.6 us (26%)
  matrix products  12.7 us (12%)
  local copies, waits for them, and re-layouts  5.21 us (5%)
  between operations  1.24 us (1%)
    ppermute x23, waiting for transfers between devices, flipped(): lax.ppermute(block, axis, [(low, low ^ mask) for low in range(count)])  29.5 us
    ppermute x23, starting transfers between devices, flipped(): lax.ppermute(block, axis, [(low, low ^ mask) for low in range(count)])  29.2 us
    another operation x3, other arithmetic, local(): lower_factor = jnp.linalg.cholesky(gram)  13.2 us
    another operation x2, other arithmetic, local(): lax.linalg.triangular_solve(lower_factor, jnp.eye(rank, dtype=jnp.float32...  10.5 us
    dot_general x2, matrix products, errors(): lax.dot_general(basis_low, factor, (((1,), (1,)), ((), ())), preferred_el...  6.23 us
    dot_general x2, matrix products, products(): lax.dot_general(side, both, (((0,), (0,)), ((), ())), preferred_element_t...  3.05 us
    dynamic_slice x1, local copies, waits for them, and re-layouts, columns(): lax.dynamic_slice_in_dim(samples, (me ^ mask) * piece, piece, 1)  2.47 us
  transfers between devices with their start and end apart: 23, of which 13 were waited for; matrix products, arithmetic and copies ran while one was open for 35% of the time, Pallas kernels for 0%

profile of v1, /device:TPU:0, one launch (start us, length us, event | category | flops | bytes accessed | tf_op | source)
XLA Modules:
  0.0 105.5 jit_solution(12599548174691982203)
XLA Ops:
  0.6 3.0 %collective-permute-start = (bf16[512,128]{1,0:T(8,128)(2,1)}, bf16[512,128]{1,0:T(8,128)(2,1)S(1)}, u32[]{:S(2)}, u32[]{:S(2)}) collective-permute-start(bf16[512,128]{1,0:T(8,128)(2,1)} %param.3), channel_id=1, source_target_pairs={{0,8},{4,12},{8,0},{12,4},{16,24},{20,28},{24,16},{28,20},{1,9},{5... | collective-permute-start | bytes 393224 | tf_op jit(solution)/shard_map/ppermute | solution.py:11
  3.6 1.5 %collective-permute-start.1 = (bf16[512,128]{1,0:T(8,128)(2,1)}, bf16[512,128]{1,0:T(8,128)(2,1)S(1)}, u32[]{:S(2)}, u32[]{:S(2)}) collective-permute-start(bf16[512,128]{1,0:T(8,128)(2,1)} %param.3), channel_id=1, source_target_pairs={{0,16},{4,20},{8,24},{12,28},{16,0},{20,4},{24,8},{28,12},{1,17},{... | collective-permute-start | bytes 393224 | tf_op jit(solution)/shard_map/ppermute | solution.py:11
  6.1 1.7 %collective-permute-done = bf16[512,128]{1,0:T(8,128)(2,1)S(1)} collective-permute-done((bf16[512,128]{1,0:T(8,128)(2,1)}, bf16[512,128]{1,0:T(8,128)(2,1)S(1)}, u32[]{:S(2)}, u32[]{:S(2)}) %collective-permute-start) | collective-permute-done | bytes 131104 | tf_op jit(solution)/shard_map/ppermute | solution.py:11
  7.9 3.7 %collective-permute-done.1 = bf16[512,128]{1,0:T(8,128)(2,1)S(1)} collective-permute-done((bf16[512,128]{1,0:T(8,128)(2,1)}, bf16[512,128]{1,0:T(8,128)(2,1)S(1)}, u32[]{:S(2)}, u32[]{:S(2)}) %collective-permute-start.1) | collective-permute-done | bytes 131104 | tf_op jit(solution)/shard_map/ppermute | solution.py:11
  11.8 2.5 %constant_dynamic-slice_fusion.10 = (bf16[512,512]{1,0:T(8,128)(2,1)S(1)}, bf16[512,512]{1,0:T(8,128)(2,1)S(1)}, bf16[512,512]{1,0:T(8,128)(2,1)S(1)}, bf16[512,...) fusion(bf16[512,4096]{1,0:T(8,128)(2,1)} %param.2, ...), kind=kLoop, calls=%fused_computation.56 | loop fusion | bytes 8388640 | tf_op jit(solution)/shard_map/dynamic_slice | solution.py:46
  15.4 1.0 fusion.28
  19.0 1.9 %collective-permute-done.4 = f32[128,128]{0,1:T(8,128)S(1)} collective-permute-done((f32[128,128]{0,1:T(8,128)S(1)}, f32[128,128]{0,1:T(8,128)S(1)}, u32[]{:S(2)}, u32[]{:S(2)}) %collective-permute-start.4) | collective-permute-done | bytes 65568 | tf_op jit(solution)/shard_map/ppermute | solution.py:11
  20.9 1.3 %collective-permute-start.5 = (f32[128,128]{0,1:T(8,128)S(1)}, f32[128,128]{0,1:T(8,128)S(1)}, u32[]{:S(2)}, u32[]{:S(2)}) collective-permute-start(f32[128,128]{0,1:T(8,128)S(1)} %add.108), channel_id=1, source_target_pairs={{0,8},{4,12},{8,0},{12,4},{16,24},{20,28},{24,16},{28,20},{1,9},{5... | collective-permute-start | bytes 196616 | tf_op jit(solution)/shard_map/ppermute | solution.py:11
  22.2 3.2 %collective-permute-done.5 = f32[128,128]{0,1:T(8,128)S(1)} collective-permute-done((f32[128,128]{0,1:T(8,128)S(1)}, f32[128,128]{0,1:T(8,128)S(1)}, u32[]{:S(2)}, u32[]{:S(2)}) %collective-permute-start.5) | collective-permute-done | bytes 65568 | tf_op jit(solution)/shard_map/ppermute | solution.py:11
  25.3 1.6 %collective-permute-start.6 = (f32[128,128]{0,1:T(8,128)S(1)}, f32[128,128]{0,1:T(8,128)S(1)}, u32[]{:S(2)}, u32[]{:S(2)}) collective-permute-start(f32[128,128]{0,1:T(8,128)S(1)} %add.109), channel_id=1, source_target_pairs={{0,16},{4,20},{8,24},{12,28},{16,0},{20,4},{24,8},{28,12},{1,17},{... | collective-permute-start | bytes 196616 | tf_op jit(solution)/shard_map/ppermute | solution.py:11
  26.9 2.8 %collective-permute-done.6 = f32[128,128]{0,1:T(8,128)S(1)} collective-permute-done((f32[128,128]{0,1:T(8,128)S(1)}, f32[128,128]{0,1:T(8,128)S(1)}, u32[]{:S(2)}, u32[]{:S(2)}) %collective-permute-start.6) | collective-permute-done | bytes 65568 | tf_op jit(solution)/shard_map/ppermute | solution.py:11
  29.7 1.6 %collective-permute-start.7 = (f32[128,128]{0,1:T(8,128)S(1)}, f32[128,128]{0,1:T(8,128)S(1)}, u32[]{:S(2)}, u32[]{:S(2)}) collective-permute-start(f32[128,128]{0,1:T(8,128)S(1)} %add.110), channel_id=1, source_target_pairs={{0,1},{1,0},{2,3},{3,2},{4,5},{5,4},{6,7},{7,6},{8,9},{9,8},{10,11... | collective-permute-start | bytes 196616 | tf_op jit(solution)/shard_map/ppermute | solution.py:11
  31.3 2.7 %collective-permute-done.7 = f32[128,128]{0,1:T(8,128)S(1)} collective-permute-done((f32[128,128]{0,1:T(8,128)S(1)}, f32[128,128]{0,1:T(8,128)S(1)}, u32[]{:S(2)}, u32[]{:S(2)}) %collective-permute-start.7) | collective-permute-done | bytes 65568 | tf_op jit(solution)/shard_map/ppermute | solution.py:11
  34.0 2.9 %collective-permute-start.8 = (f32[128,128]{0,1:T(8,128)S(1)}, f32[128,128]{0,1:T(8,128)S(1)}, u32[]{:S(2)}, u32[]{:S(2)}) collective-permute-start(f32[128,128]{0,1:T(8,128)S(1)} %add.111), channel_id=1, source_target_pairs={{0,2},{1,3},{2,0},{3,1},{4,6},{5,7},{6,4},{7,5},{8,10},{9,11},{10,... | collective-permute-start | bytes 196616 | tf_op jit(solution)/shard_map/ppermute | solution.py:11
  36.9 2.3 %fusion.4 = f32[2048,256]{1,0:T(8,128)S(1)} fusion(bf16[512,128]{0,1:T(8,128)(2,1)} %copy-done.18, bf16[512,128]{0,1:T(8,128)(2,1)S(1)} %get-tuple-element.17, bf16[512,512]{1,0:T(8,128)(2,1)} %copy-done.11, bf16[512,512]{1,0:T(8,128)(2,1)} %copy-done.13, bf16[512,512]{1,0:T(8,128)(2,1)} %copy-done.15, bf16[512,512]{1,0:T(8,128)(2,1)} %copy-done.9), kind=kOutput, calls=%fused_computation.15 | convolution fusion | flops 545783808 | bytes 4456448 | tf_op jit(solution)/shard_map/dot_general | solution.py:60
  40.0 12.5 %cholesky.14 = f32[128,128]{1,0:T(8,128)S(1)} custom-call(f32[128,128]{1,0:T(8,128)} %fusion.8), custom_call_target="Cholesky" | custom-call | tf_op jit(solution)/shard_map/jit(cholesky)/cholesky | solution.py:75
  52.6 1.4 %fusion = f32[2048,128]{1,0:T(8,128)S(1)} fusion(f32[2048,128]{1,0:T(8,128)} %collective-permute-done.9, f32[2048,256]{1,0:T(8,128)S(1)} %fusion.4), kind=kLoop, calls=%fused_computation.7 | loop fusion | flops 524288 | bytes 4194304 | tf_op jit(solution)/shard_map/add | solution.py:63
  54.9 1.2 %collective-permute-start.12 = (f32[512,128]{1,0:T(8,128)}, f32[512,128]{1,0:T(8,128)}, u32[]{:S(2)}, u32[]{:S(2)}) collective-permute-start(f32[512,128]{1,0:T(8,128)} %get-tuple-element.12), channel_id=1, source_target_pairs={{0,8},{4,12},{8,0},{12,4},{16,24},{20,28},{24,16},{28,20},{1,9},{5... | collective-permute-start | bytes 786440 | tf_op jit(solution)/shard_map/ppermute | solution.py:11
  56.9 1.4 %collective-permute-start.10 = (f32[512,128]{1,0:T(8,128)}, f32[512,128]{1,0:T(8,128)}, u32[]{:S(2)}, u32[]{:S(2)}) collective-permute-start(f32[512,128]{1,0:T(8,128)} %get-tuple-element.11), channel_id=1, source_target_pairs={{0,24},{4,28},{8,16},{12,20},{16,8},{20,12},{24,0},{28,4},{1,25},{... | collective-permute-start | bytes 786440 | tf_op jit(solution)/shard_map/ppermute | solution.py:11
  59.7 9.8 %custom-call.6 = f32[1,128,128]{1,2,0:T(8,128)S(1)} custom-call(f32[1,128,128]{2,1,0:T(8,128)S(1)} %fusion.5), custom_call_target="InvertDiagBlocksLowerTriangular" | custom-call | tf_op jit(solution)/shard_map/triangular_solve | solution.py:76
  69.5 1.2 %fusion.2 = f32[512,128]{1,0:T(8,128)S(1)} fusion(f32[512,128]{1,0:T(8,128)} %collective-permute-done.12, f32[512,128]{1,0:T(8,128)} %collective-permute-done.11, f32[512,128]{1,0:T(8,128)} %collective-permute-done.10, f32[2048,128]{1,0:T(8,128)S(1)} %fusion), kind=kLoop, calls=%fused_computation.11 | loop fusion | flops 196608 | bytes 1310720 | tf_op jit(solution)/shard_map/add | solution.py:67
  70.7 4.4 %collective-permute-start.15 = (f32[128,128]{1,0:T(8,128)S(1)}, f32[128,128]{1,0:T(8,128)S(1)}, u32[]{:S(2)}, u32[]{:S(2)}) collective-permute-start(f32[128,128]{1,0:T(8,128)S(1)} %get-tuple-element.15), channel_id=1, source_target_pairs={{0,3},{1,2},{2,1},{3,0},{4,7},{5,6},{6,5},{7,4},{8,11},{9,10},{10,... | collective-permute-start | bytes 196616 | tf_op jit(solution)/shard_map/ppermute | solution.py:11
  75.9 1.5 %collective-permute-done.15 = f32[128,128]{1,0:T(8,128)S(1)} collective-permute-done((f32[128,128]{1,0:T(8,128)S(1)}, f32[128,128]{1,0:T(8,128)S(1)}, u32[]{:S(2)}, u32[]{:S(2)}) %collective-permute-start.15) | collective-permute-done | bytes 65568 | tf_op jit(solution)/shard_map/ppermute | solution.py:11
  77.4 5.0 %collective-permute-done.14 = f32[128,128]{1,0:T(8,128)S(1)} collective-permute-done((f32[128,128]{1,0:T(8,128)S(1)}, f32[128,128]{1,0:T(8,128)S(1)}, u32[]{:S(2)}, u32[]{:S(2)}) %collective-permute-start.14) | collective-permute-done | bytes 65568 | tf_op jit(solution)/shard_map/ppermute | solution.py:11
  82.9 4.2 %collective-permute-start.18 = (f32[128,128]{1,0:T(8,128)S(1)}, f32[128,128]{1,0:T(8,128)S(1)}, u32[]{:S(2)}, u32[]{:S(2)}) collective-permute-start(f32[128,128]{1,0:T(8,128)S(1)} %get-tuple-element.21), channel_id=1, source_target_pairs={{0,3},{1,2},{2,1},{3,0},{4,7},{5,6},{6,5},{7,4},{8,11},{9,10},{10,... | collective-permute-start | bytes 196616 | tf_op jit(solution)/shard_map/ppermute | solution.py:11
  88.0 2.1 %collective-permute-done.18 = f32[128,128]{1,0:T(8,128)S(1)} collective-permute-done((f32[128,128]{1,0:T(8,128)S(1)}, f32[128,128]{1,0:T(8,128)S(1)}, u32[]{:S(2)}, u32[]{:S(2)}) %collective-permute-start.18) | collective-permute-done | bytes 65568 | tf_op jit(solution)/shard_map/ppermute | solution.py:11
  90.1 1.5 %collective-permute-start.21 = (bf16[512,128]{1,0:T(8,128)(2,1)S(1)}, bf16[512,128]{1,0:T(8,128)(2,1)S(1)}, u32[]{:S(2)}, u32[]{:S(2)}) collective-permute-start(bf16[512,128]{1,0:T(8,128)(2,1)S(1)} %convert_element_type.27), channel_id=1, source_target_pairs={{0,24},{4,28},{8,16},{12,20},{16,8},{20,12},{24,0},{28,4},{1,25},{... | collective-permute-start | bytes 393224 | tf_op jit(solution)/shard_map/ppermute | solution.py:11
  91.7 1.2 %collective-permute-start.20 = (bf16[512,128]{1,0:T(8,128)(2,1)S(1)}, bf16[512,128]{1,0:T(8,128)(2,1)S(1)}, u32[]{:S(2)}, u32[]{:S(2)}) collective-permute-start(bf16[512,128]{1,0:T(8,128)(2,1)S(1)} %convert_element_type.27), channel_id=1, source_target_pairs={{0,16},{4,20},{8,24},{12,28},{16,0},{20,4},{24,8},{28,12},{1,17},{... | collective-permute-start | bytes 393224 | tf_op jit(solution)/shard_map/ppermute | solution.py:11
  93.7 2.5 %collective-permute-done.21 = bf16[512,128]{1,0:T(8,128)(2,1)S(1)} collective-permute-done((bf16[512,128]{1,0:T(8,128)(2,1)S(1)}, bf16[512,128]{1,0:T(8,128)(2,1)S(1)}, u32[]{:S(2)}, u32[]{:S(2)}) %collective-permute-start.21) | collective-permute-done | bytes 131104 | tf_op jit(solution)/shard_map/ppermute | solution.py:11
  96.1 1.3 %collective-permute-done.20 = bf16[512,128]{1,0:T(8,128)(2,1)S(1)} collective-permute-done((bf16[512,128]{1,0:T(8,128)(2,1)S(1)}, bf16[512,128]{1,0:T(8,128)(2,1)S(1)}, u32[]{:S(2)}, u32[]{:S(2)}) %collective-permute-start.20) | collective-permute-done | bytes 131104 | tf_op jit(solution)/shard_map/ppermute | solution.py:11
  98.6 5.1 %multiply_reduce_fusion.1 = f32[512]{0:T(512)S(1)} fusion(f32[512,128]{1,0:T(8,128)S(1)} %fusion.17, bf16[512,128]{1,0:T(8,128)(2,1)S(1)} %collective-permute-done.21, bf16[512,128]{1,0:T(8,128)(2,1)S(1)} %collective-permute-done.20, bf16[512,128]{1,0:T(8,128)(2,1)S(1)} %collective-permute-done.19, bf16[512,128]{1,0:T(8,128)(2,1)S(1)} %convert_element_type.27, ...), kind=kOutput, calls=%fused_computation.1 | convolution fusion | flops 283180544 | bytes 2885632 | tf_op jit(solution)/shard_map/dot_general | solution.py:99
  103.7 1.2 %multiply_reduce_fusion = f32[512]{0:T(512)S(1)} fusion(bf16[2048,128]{1,0:T(8,128)(2,1)S(1)} %collective-permute-done.22, f32[512,128]{1,0:T(8,128)S(1)} %fusion.17, bf16[512,512]{1,0:T(8,128)(2,1)S(1)} %copy-done.6, bf16[512,512]{1,0:T(8,128)(2,1)S(1)} %copy-done.8, bf16[512,512]{1,0:T(8,128)(2,1)S(1)} %copy-done.2, bf16[512,512]{1,0:T(8,128)(2,1)S(1)} %copy-done.4), kind=kOutput, calls=%fused_computation | convolution fusion | flops 281083392 | bytes 2885632 | tf_op jit(solution)/shard_map/dot_general | solution.py:99
  (91 shorter events, 13.3 us)
Async XLA Ops:
  0.6 7.2 %collective-permute-start = (bf16[512,128]{1,0:T(8,128)(2,1)}, bf16[512,128]{1,0:T(8,128)(2,1)S(1)}, u32[]{:S(2)}, u32[]{:S(2)}) collective-permute-start(bf16[512,128]{1,0:T(8,128)(2,1)} %param.3), channel_id=1, source_target_pairs={{0,8},{4,12},{8,0},{12,4},{16,24},{20,28},{24,16},{28,20},{1,9},{5... | collective-permute-start | bytes 393224 | tf_op jit(solution)/shard_map/ppermute | solution.py:11
  3.6 8.0 %collective-permute-start.1 = (bf16[512,128]{1,0:T(8,128)(2,1)}, bf16[512,128]{1,0:T(8,128)(2,1)S(1)}, u32[]{:S(2)}, u32[]{:S(2)}) collective-permute-start(bf16[512,128]{1,0:T(8,128)(2,1)} %param.3), channel_id=1, source_target_pairs={{0,16},{4,20},{8,24},{12,28},{16,0},{20,4},{24,8},{28,12},{1,17},{... | collective-permute-start | bytes 393224 | tf_op jit(solution)/shard_map/ppermute | solution.py:11
  5.2 6.5 %collective-permute-start.2 = (bf16[512,128]{1,0:T(8,128)(2,1)}, bf16[512,128]{1,0:T(8,128)(2,1)S(1)}, u32[]{:S(2)}, u32[]{:S(2)}) collective-permute-start(bf16[512,128]{1,0:T(8,128)(2,1)} %param.3), channel_id=1, source_target_pairs={{0,24},{4,28},{8,16},{12,20},{16,8},{20,12},{24,0},{28,4},{1,25},{... | collective-permute-start | bytes 393224 | tf_op jit(solution)/shard_map/ppermute | solution.py:11
  11.7 2.7 %collective-permute-start.3 = (bf16[2048,128]{1,0:T(8,128)(2,1)S(1)}, bf16[2048,128]{1,0:T(8,128)(2,1)S(1)}, u32[]{:S(2)}, u32[]{:S(2)}) collective-permute-start(bf16[2048,128]{1,0:T(8,128)(2,1)S(1)} %constant_dynamic-update-slice_fusion), channel_id=1, source_target_pairs={{0,4},{4,0},{8,12},{12,8},{16,20},{20,16},{24,28},{28,24},{1,5},{5... | collective-permute-start | bytes 1572872 | tf_op jit(solution)/shard_map/ppermute | solution.py:11
  18.0 34.6 %collective-permute-start.9 = (f32[2048,128]{1,0:T(8,128)S(1)}, f32[2048,128]{1,0:T(8,128)}, u32[]{:S(2)}, u32[]{:S(2)}) collective-permute-start(f32[2048,128]{1,0:T(8,128)S(1)} %slice_add_fusion), channel_id=1, source_target_pairs={{0,4},{4,0},{8,12},{12,8},{16,20},{20,16},{24,28},{28,24},{1,5},{5... | collective-permute-start | bytes 3145736 | tf_op jit(solution)/shard_map/ppermute | solution.py:11
  18.9 2.0 %collective-permute-start.4 = (f32[128,128]{0,1:T(8,128)S(1)}, f32[128,128]{0,1:T(8,128)S(1)}, u32[]{:S(2)}, u32[]{:S(2)}) collective-permute-start(f32[128,128]{0,1:T(8,128)S(1)} %fusion.29), channel_id=1, source_target_pairs={{0,4},{4,0},{8,12},{12,8},{16,20},{20,16},{24,28},{28,24},{1,5},{5... | collective-permute-start | bytes 196616 | tf_op jit(solution)/shard_map/ppermute | solution.py:11
  20.9 4.4 %collective-permute-start.5 = (f32[128,128]{0,1:T(8,128)S(1)}, f32[128,128]{0,1:T(8,128)S(1)}, u32[]{:S(2)}, u32[]{:S(2)}) collective-permute-start(f32[128,128]{0,1:T(8,128)S(1)} %add.108), channel_id=1, source_target_pairs={{0,8},{4,12},{8,0},{12,4},{16,24},{20,28},{24,16},{28,20},{1,9},{5... | collective-permute-start | bytes 196616 | tf_op jit(solution)/shard_map/ppermute | solution.py:11
  25.3 4.3 %collective-permute-start.6 = (f32[128,128]{0,1:T(8,128)S(1)}, f32[128,128]{0,1:T(8,128)S(1)}, u32[]{:S(2)}, u32[]{:S(2)}) collective-permute-start(f32[128,128]{0,1:T(8,128)S(1)} %add.109), channel_id=1, source_target_pairs={{0,16},{4,20},{8,24},{12,28},{16,0},{20,4},{24,8},{28,12},{1,17},{... | collective-permute-start | bytes 196616 | tf_op jit(solution)/shard_map/ppermute | solution.py:11
  29.7 4.3 %collective-permute-start.7 = (f32[128,128]{0,1:T(8,128)S(1)}, f32[128,128]{0,1:T(8,128)S(1)}, u32[]{:S(2)}, u32[]{:S(2)}) collective-permute-start(f32[128,128]{0,1:T(8,128)S(1)} %add.110), channel_id=1, source_target_pairs={{0,1},{1,0},{2,3},{3,2},{4,5},{5,4},{6,7},{7,6},{8,9},{9,8},{10,11... | collective-permute-start | bytes 196616 | tf_op jit(solution)/shard_map/ppermute | solution.py:11
  34.0 5.2 %collective-permute-start.8 = (f32[128,128]{0,1:T(8,128)S(1)}, f32[128,128]{0,1:T(8,128)S(1)}, u32[]{:S(2)}, u32[]{:S(2)}) collective-permute-start(f32[128,128]{0,1:T(8,128)S(1)} %add.111), channel_id=1, source_target_pairs={{0,2},{1,3},{2,0},{3,1},{4,6},{5,7},{6,4},{7,5},{8,10},{9,11},{10,... | collective-permute-start | bytes 196616 | tf_op jit(solution)/shard_map/ppermute | solution.py:11
  54.0 44.5 %copy-start.10 = (bf16[512,512]{1,0:T(8,128)(2,1)S(1)}, bf16[512,512]{1,0:T(8,128)(2,1)}, u32[]{:S(2)}) copy-start(bf16[512,512]{1,0:T(8,128)(2,1)} %copy-done.9) | copy-start | bytes 1572868
  54.0 44.5 %copy-start.12 = (bf16[512,512]{1,0:T(8,128)(2,1)S(1)}, bf16[512,512]{1,0:T(8,128)(2,1)}, u32[]{:S(2)}) copy-start(bf16[512,512]{1,0:T(8,128)(2,1)} %copy-done.11) | copy-start | bytes 1572868
  54.0 44.5 %copy-start.14 = (bf16[512,512]{1,0:T(8,128)(2,1)S(1)}, bf16[512,512]{1,0:T(8,128)(2,1)}, u32[]{:S(2)}) copy-start(bf16[512,512]{1,0:T(8,128)(2,1)} %copy-done.13) | copy-start | bytes 1572868
  54.0 44.5 %copy-start.16 = (bf16[512,512]{1,0:T(8,128)(2,1)S(1)}, bf16[512,512]{1,0:T(8,128)(2,1)}, u32[]{:S(2)}) copy-start(bf16[512,512]{1,0:T(8,128)(2,1)} %copy-done.15) | copy-start | bytes 1572868
  54.9 14.6 %collective-permute-start.12 = (f32[512,128]{1,0:T(8,128)}, f32[512,128]{1,0:T(8,128)}, u32[]{:S(2)}, u32[]{:S(2)}) collective-permute-start(f32[512,128]{1,0:T(8,128)} %get-tuple-element.12), channel_id=1, source_target_pairs={{0,8},{4,12},{8,0},{12,4},{16,24},{20,28},{24,16},{28,20},{1,9},{5... | collective-permute-start | bytes 786440 | tf_op jit(solution)/shard_map/ppermute | solution.py:11
  56.1 13.4 %collective-permute-start.11 = (f32[512,128]{1,0:T(8,128)}, f32[512,128]{1,0:T(8,128)}, u32[]{:S(2)}, u32[]{:S(2)}) collective-permute-start(f32[512,128]{1,0:T(8,128)} %get-tuple-element.13), channel_id=1, source_target_pairs={{0,16},{4,20},{8,24},{12,28},{16,0},{20,4},{24,8},{28,12},{1,17},{... | collective-permute-start | bytes 786440 | tf_op jit(solution)/shard_map/ppermute | solution.py:11
  56.9 12.6 %collective-permute-start.10 = (f32[512,128]{1,0:T(8,128)}, f32[512,128]{1,0:T(8,128)}, u32[]{:S(2)}, u32[]{:S(2)}) collective-permute-start(f32[512,128]{1,0:T(8,128)} %get-tuple-element.11), channel_id=1, source_target_pairs={{0,24},{4,28},{8,16},{12,20},{16,8},{20,12},{24,0},{28,4},{1,25},{... | collective-permute-start | bytes 786440 | tf_op jit(solution)/shard_map/ppermute | solution.py:11
  70.7 6.7 %collective-permute-start.15 = (f32[128,128]{1,0:T(8,128)S(1)}, f32[128,128]{1,0:T(8,128)S(1)}, u32[]{:S(2)}, u32[]{:S(2)}) collective-permute-start(f32[128,128]{1,0:T(8,128)S(1)} %get-tuple-element.15), channel_id=1, source_target_pairs={{0,3},{1,2},{2,1},{3,0},{4,7},{5,6},{6,5},{7,4},{8,11},{9,10},{10,... | collective-permute-start | bytes 196616 | tf_op jit(solution)/shard_map/ppermute | solution.py:11
  75.1 7.3 %collective-permute-start.14 = (f32[128,128]{1,0:T(8,128)S(1)}, f32[128,128]{1,0:T(8,128)S(1)}, u32[]{:S(2)}, u32[]{:S(2)}) collective-permute-start(f32[128,128]{1,0:T(8,128)S(1)} %get-tuple-element.16), channel_id=1, source_target_pairs={{0,2},{1,3},{2,0},{3,1},{4,6},{5,7},{6,4},{7,5},{8,10},{9,11},{10,... | collective-permute-start | bytes 196616 | tf_op jit(solution)/shard_map/ppermute | solution.py:11
  75.1 7.3 %collective-permute-start.13 = (f32[128,128]{1,0:T(8,128)S(1)}, f32[128,128]{1,0:T(8,128)S(1)}, u32[]{:S(2)}, u32[]{:S(2)}) collective-permute-start(f32[128,128]{1,0:T(8,128)S(1)} %get-tuple-element.14), channel_id=1, source_target_pairs={{0,1},{1,0},{2,3},{3,2},{4,5},{5,4},{6,7},{7,6},{8,9},{9,8},{10,11... | collective-permute-start | bytes 196616 | tf_op jit(solution)/shard_map/ppermute | solution.py:11
  82.7 4.5 %collective-permute-start.16 = (f32[128,128]{1,0:T(8,128)S(1)}, f32[128,128]{1,0:T(8,128)S(1)}, u32[]{:S(2)}, u32[]{:S(2)}) collective-permute-start(f32[128,128]{1,0:T(8,128)S(1)} %get-tuple-element.21), channel_id=1, source_target_pairs={{0,1},{1,0},{2,3},{3,2},{4,5},{5,4},{6,7},{7,6},{8,9},{9,8},{10,11... | collective-permute-start | bytes 196616 | tf_op jit(solution)/shard_map/ppermute | solution.py:11
  82.7 5.2 %collective-permute-start.17 = (f32[128,128]{1,0:T(8,128)S(1)}, f32[128,128]{1,0:T(8,128)S(1)}, u32[]{:S(2)}, u32[]{:S(2)}) collective-permute-start(f32[128,128]{1,0:T(8,128)S(1)} %get-tuple-element.21), channel_id=1, source_target_pairs={{0,2},{1,3},{2,0},{3,1},{4,6},{5,7},{6,4},{7,5},{8,10},{9,11},{10,... | collective-permute-start | bytes 196616 | tf_op jit(solution)/shard_map/ppermute | solution.py:11
  82.9 7.1 %collective-permute-start.18 = (f32[128,128]{1,0:T(8,128)S(1)}, f32[128,128]{1,0:T(8,128)S(1)}, u32[]{:S(2)}, u32[]{:S(2)}) collective-permute-start(f32[128,128]{1,0:T(8,128)S(1)} %get-tuple-element.21), channel_id=1, source_target_pairs={{0,3},{1,2},{2,1},{3,0},{4,7},{5,6},{6,5},{7,4},{8,11},{9,10},{10,... | collective-permute-start | bytes 196616 | tf_op jit(solution)/shard_map/ppermute | solution.py:11
  90.1 13.6 %copy-start = (f32[512,128]{1,0:T(8,128)}, f32[512,128]{1,0:T(8,128)S(1)}, u32[]{:S(2)}) copy-start(f32[512,128]{1,0:T(8,128)S(1)} %constant_dynamic-update-slice_fusion.4) | copy-start | bytes 786436
  90.1 6.0 %collective-permute-start.21 = (bf16[512,128]{1,0:T(8,128)(2,1)S(1)}, bf16[512,128]{1,0:T(8,128)(2,1)S(1)}, u32[]{:S(2)}, u32[]{:S(2)}) collective-permute-start(bf16[512,128]{1,0:T(8,128)(2,1)S(1)} %convert_element_type.27), channel_id=1, source_target_pairs={{0,24},{4,28},{8,16},{12,20},{16,8},{20,12},{24,0},{28,4},{1,25},{... | collective-permute-start | bytes 393224 | tf_op jit(solution)/shard_map/ppermute | solution.py:11
  91.7 5.8 %collective-permute-start.20 = (bf16[512,128]{1,0:T(8,128)(2,1)S(1)}, bf16[512,128]{1,0:T(8,128)(2,1)S(1)}, u32[]{:S(2)}, u32[]{:S(2)}) collective-permute-start(bf16[512,128]{1,0:T(8,128)(2,1)S(1)} %convert_element_type.27), channel_id=1, source_target_pairs={{0,16},{4,20},{8,24},{12,28},{16,0},{20,4},{24,8},{28,12},{1,17},{... | collective-permute-start | bytes 393224 | tf_op jit(solution)/shard_map/ppermute | solution.py:11
  92.8 5.0 %collective-permute-start.19 = (bf16[512,128]{1,0:T(8,128)(2,1)S(1)}, bf16[512,128]{1,0:T(8,128)(2,1)S(1)}, u32[]{:S(2)}, u32[]{:S(2)}) collective-permute-start(bf16[512,128]{1,0:T(8,128)(2,1)S(1)} %convert_element_type.27), channel_id=1, source_target_pairs={{0,8},{4,12},{8,0},{12,4},{16,24},{20,28},{24,16},{28,20},{1,9},{5... | collective-permute-start | bytes 393224 | tf_op jit(solution)/shard_map/ppermute | solution.py:11
  97.8 5.8 %collective-permute-start.22 = (bf16[2048,128]{1,0:T(8,128)(2,1)S(1)}, bf16[2048,128]{1,0:T(8,128)(2,1)S(1)}, u32[]{:S(2)}, u32[]{:S(2)}) collective-permute-start(bf16[2048,128]{1,0:T(8,128)(2,1)S(1)} %pad_maximum_fusion.2), channel_id=1, source_target_pairs={{0,4},{4,0},{8,12},{12,8},{16,20},{20,16},{24,28},{28,24},{1,5},{5... | collective-permute-start | bytes 1572872 | tf_op jit(solution)/shard_map/ppermute | solution.py:11
  98.6 5.1 %copy-start.17 = (f32[512,128]{1,0:T(8,128)}, f32[512,128]{1,0:T(8,128)S(1)}, u32[]{:S(2)}) copy-start(f32[512,128]{1,0:T(8,128)S(1)} %fusion.17) | copy-start | bytes 786436
  98.6 5.1 %copy-start.2 = (bf16[512,512]{1,0:T(8,128)(2,1)S(1)}, bf16[512,512]{1,0:T(8,128)(2,1)}, u32[]{:S(2)}) copy-start(bf16[512,512]{1,0:T(8,128)(2,1)} %copy-done.1) | copy-start | bytes 1572868
  98.6 5.1 %copy-start.4 = (bf16[512,512]{1,0:T(8,128)(2,1)S(1)}, bf16[512,512]{1,0:T(8,128)(2,1)}, u32[]{:S(2)}) copy-start(bf16[512,512]{1,0:T(8,128)(2,1)} %copy-done.3) | copy-start | bytes 1572868
  98.6 5.1 %copy-start.6 = (bf16[512,512]{1,0:T(8,128)(2,1)S(1)}, bf16[512,512]{1,0:T(8,128)(2,1)}, u32[]{:S(2)}) copy-start(bf16[512,512]{1,0:T(8,128)(2,1)} %copy-done.5) | copy-start | bytes 1572868
  (10 other events, 25.9 us)

commit v2 on v1

--- a/solution.py
+++ b/solution.py
@@ -1,8 +1,11 @@
+import functools
 import math
 
 import jax
 import jax.numpy as jnp
 from jax import lax
+from jax.experimental import pallas as pl
+from jax.experimental.pallas import tpu as pltpu
 from jax.sharding import PartitionSpec as P
 
 
@@ -17,10 +20,55 @@
     )
 
 
-def summed_over(value, axis):
-    for level in range(lax.axis_size(axis).bit_length() - 1):
-        value = value + flipped(value, axis, 1 << level)
-    return value
+def terms(value):
+    high = value.astype(jnp.bfloat16).astype(jnp.float32)
+    rest = value - high
+    middle = rest.astype(jnp.bfloat16).astype(jnp.float32)
+    return high, middle, rest - middle
+
+
+def factor_kernel(block, gram_ref, out_ref, work, lines):
+    n = gram_ref.shape[0]
+    work[:, :n] = gram_ref[...]
+    down = lax.broadcasted_iota(jnp.int32, (n, n), 0)
+    across = lax.broadcasted_iota(jnp.int32, (n, n), 1)
+    work[:, n:] = jnp.where(down == across, 1.0, 0.0)
+    for top in range(0, n, block):
+        line = [work[top + i : top + i + 1, :] for i in range(block)]
+        corner = {}
+        for i in range(block):
+            for j in range(i + 1):
+                corner[i, j] = jnp.broadcast_to(line[i][:, top + j : top + j + 1], (1, n))
+        for j in range(block):
+            scale = lax.rsqrt(corner[j, j])
+            line[j] = line[j] * jnp.concatenate([scale, scale], axis=1)
+            lines[j : j + 1, :] = line[j]
+            for i in range(j + 1, block):
+                corner[i, j] = corner[i, j] * scale
+            for i in range(j + 1, block):
+                for m in range(j + 1, i + 1):
+                    corner[i, m] = corner[i, m] - corner[i, j] * corner[m, j]
+                line[i] = line[i] - jnp.concatenate([corner[i, j]] * 2, axis=1) * line[j]
+        done = lines[...]
+        out_ref[top : top + block, :] = done[:, n:]
+        if top + block < n:
+            high, middle, small = terms(done)
+            left = jnp.concatenate([high, high, middle, high, small, middle])[:, :n].astype(jnp.bfloat16)
+            right = jnp.concatenate([high, middle, high, small, high, middle]).astype(jnp.bfloat16)
+            work[...] -= lax.dot_general(
+                left, right, (((0,), (0,)), ((), ())), preferred_element_type=jnp.float32
+            )
+
+
+def inverse_factor(gram, block=16):
+    n = gram.shape[0]
+    return pl.pallas_call(
+        functools.partial(factor_kernel, block),
+        out_shape=jax.ShapeDtypeStruct((n, n), jnp.float32),
+        scratch_shapes=[pltpu.VMEM((n, 2 * n), jnp.float32), pltpu.VMEM((block, 2 * n), jnp.float32)],
+        cost_estimate=pl.CostEstimate(flops=6_000_000_000, bytes_accessed=131072, transcendentals=128),
+        name="inverse_factor",
+    )(gram)
 
 
 def local(samples, sketch_matrix):
@@ -39,7 +87,6 @@
     for mask in reversed(evens):
         got[mask] = flipped(sketch_matrix, "inner", mask)
     even = jnp.concatenate([got[mask] for mask in range(0, inner, 2)])
-    odd = flipped(even, "inner", 1)
 
     def columns(masks):
         return jnp.concatenate(
@@ -48,12 +95,15 @@
 
     even_columns = columns(range(0, inner, 2))
     odd_columns = columns(range(1, inner, 2))
+    even, even_columns, odd_columns = lax.optimization_barrier((even, even_columns, odd_columns))
+    odd = flipped(even, "inner", 1)
     sketch = jnp.dot(even_columns, even, preferred_element_type=jnp.float32)
     sketch = sketch + jnp.dot(odd_columns, odd, preferred_element_type=jnp.float32)
 
     gram = exact_dot(sketch, sketch, ((0,), (0,)))
-    high = sketch.astype(jnp.bfloat16)
-    low = (sketch - high.astype(jnp.float32)).astype(jnp.bfloat16)
+    rounded = lax.reduce_precision(sketch, 8, 7)
+    high = rounded.astype(jnp.bfloat16)
+    low = (sketch - rounded).astype(jnp.bfloat16)
     both = jnp.concatenate([high, low], axis=1)
 
     def products(side):
@@ -61,26 +111,30 @@
         return twice[:, :rank] + twice[:, rank:]
 
     pieces = products(even_columns) + flipped(products(odd_columns), "inner", 1)
+    gram = gram + flipped(gram, "inner", 1)
     pieces = pieces.reshape(inner // 2, piece, rank)
-    own = pieces[0]
-    for mask in reversed(evens):
-        own = own + flipped(pieces[mask // 2], "inner", mask)
+    gram = gram + flipped(gram, "inner", 2)
+    gram, near = lax.optimization_barrier((gram, pieces[1]))
+    for level in range(2, inner.bit_length() - 1):
+        gram = gram + flipped(gram, "inner", 1 << level)
+    gram, *rest = lax.optimization_barrier((gram, *[pieces[mask // 2] for mask in reversed(evens[1:])]))
+    own = pieces[0] + flipped(near, "inner", 2)
+    for mask, block in zip(reversed(evens[1:]), rest):
+        own = own + flipped(block, "inner", mask)
+    for level in range(outer.bit_length() - 1):
+        gram = gram + flipped(gram, "outer", 1 << level)
+    gram, _ = lax.optimization_barrier((gram, own))
     share = lax.dynamic_slice_in_dim(own, mine * part, part, 0)
     for mask in range(1, outer):
         share = share + flipped(
             lax.dynamic_slice_in_dim(own, (mine ^ mask) * part, part, 0), "outer", mask
         )
 
-    gram = summed_over(summed_over(gram, "inner"), "outer")
-    lower_factor = jnp.linalg.cholesky(gram)
-    inverse = lax.linalg.triangular_solve(
-        lower_factor, jnp.eye(rank, dtype=jnp.float32), left_side=False, lower=True, transpose_a=True
-    )
-
-    basis = exact_dot(sketch, inverse * math.sqrt(total_rows), ((1,), (0,)))
+    inverse = inverse_factor(gram)
+    basis = exact_dot(sketch, inverse * math.sqrt(total_rows), ((1,), (1,)))
     basis_low = basis.astype(jnp.bfloat16)
 
-    share = exact_dot(share, inverse * (math.sqrt(width) / math.sqrt(total_rows)), ((1,), (0,)))
+    share = exact_dot(share, inverse * (math.sqrt(width) / math.sqrt(total_rows)), ((1,), (1,)))
     projection = jnp.zeros((piece, rank), jnp.float32)
     projection = lax.dynamic_update_slice_in_dim(projection, share, mine * part, 0)
     for mask in range(1, outer):

time: 106 us -> 77 us (0.73)
  other arithmetic: 27.6 us -> 3.38 us
  Pallas kernels: 0 us -> 6.31 us
  matrix products: 12.7 us -> 7.34 us
  waiting for transfers between devices: 29.5 us -> 24.8 us
    another operation x5 -> x0, other arithmetic: 23.7 us -> none  [the longest x3 13.2 us: local(): lower_factor = jnp.linalg.cholesky(gram)]
    pallas_call x0 -> x1, Pallas kernels: none -> 6.31 us  [inverse_factor(): pl.pallas_call(functools.partial(factor_kernel, block), out_shape=jax.Sha...]
    ppermute x23, waiting for transfers between devices: 29.5 us -> 24.8 us  [flipped(): lax.ppermute(block, axis, [(low, low ^ mask) for low in range(count)])]
    dot_general x2, matrix products: 6.23 us -> 1.87 us  [errors(): lax.dot_general(basis_low, factor, (((1,), (1,)), ((), ())), preferred_el...]
    dot_general x2, matrix products: 3.05 us -> 1.53 us  [products(): lax.dot_general(side, both, (((0,), (0,)), ((), ())), preferred_element_t...]
    add x1, other arithmetic: 1.36 us -> 0.14 us  [local(): pieces = products(even_columns) + flipped(products(odd_columns), 'inner', 1)]
    dot_general x3, matrix products: 1.18 us -> 2.25 us  [exact_dot(): lax.dot_general(a, b, (contract, ((), ())), precision=lax.Precision.HIGHE...]
  transfers between devices with their start and end apart: 23 -> 23, of which waited for: 13 -> 14; matrix products, arithmetic and copies ran while one was open for 35% -> 10% of each run, Pallas kernels for 0% -> 8%
where the time goes in v2:
time: 77 us; the launch traced here: 76.8 us
  starting transfers between devices  29.8 us (39%)
  waiting for transfers between devices  24.8 us (32%)
  matrix products  7.34 us (10%)
  Pallas kernels  6.31 us (8%)
  local copies, waits for them, and re-layouts  4.31 us (6%)
  other arithmetic  3.38 us (4%)
  between operations  0.88 us (1%)
    ppermute x23, starting transfers between devices, flipped(): lax.ppermute(block, axis, [(low, low ^ mask) for low in range(count)])  29.8 us
    ppermute x23, waiting for transfers between devices, flipped(): lax.ppermute(block, axis, [(low, low ^ mask) for low in range(count)])  24.8 us
    pallas_call x1, Pallas kernels, inverse_factor(): pl.pallas_call(functools.partial(factor_kernel, block), out_shape=jax.Sha...  6.31 us
    dynamic_slice x1, local copies, waits for them, and re-layouts, columns(): lax.dynamic_slice_in_dim(samples, (me ^ mask) * piece, piece, 1)  2.63 us
    dot_general x3, matrix products, exact_dot(): lax.dot_general(a, b, (contract, ((), ())), precision=lax.Precision.HIGHE...  2.25 us
    dot_general x2, matrix products, errors(): lax.dot_general(basis_low, factor, (((1,), (1,)), ((), ())), preferred_el...  1.87 us
  transfers between devices with their start and end apart: 23, of which 14 were waited for; matrix products, arithmetic and copies ran while one was open for 10% of the time, Pallas kernels for 8%

profile of v2, /device:TPU:0, one launch (start us, length us, event | category | flops | bytes accessed | tf_op | source)
XLA Modules:
  0.0 76.8 jit_solution(8858348867336341988)
XLA Ops:
  0.6 4.0 %collective-permute-start.2 = (bf16[512,128]{1,0:T(8,128)(2,1)}, bf16[512,128]{1,0:T(8,128)(2,1)S(1)}, u32[]{:S(2)}, u32[]{:S(2)}) collective-permute-start(bf16[512,128]{1,0:T(8,128)(2,1)} %param.3), channel_id=1, source_target_pairs={{0,24},{4,28},{8,16},{12,20},{16,8},{20,12},{24,0},{28,4},{1,25},{... | collective-permute-start | bytes 393224 | tf_op jit(solution)/shard_map/ppermute | solution.py:14
  5.2 2.6 %constant_dynamic-slice_fusion.6 = (bf16[512,512]{1,0:T(8,128)(2,1)S(1)}, bf16[512,512]{1,0:T(8,128)(2,1)S(1)}, bf16[512,512]{1,0:T(8,128)(2,1)S(1)}, bf16[512,5...) fusion(bf16[512,4096]{1,0:T(8,128)(2,1)} %param.2, ...), kind=kLoop, calls=%fused_computation.42 | loop fusion | bytes 8388640 | tf_op jit(solution)/shard_map/dynamic_slice | solution.py:93
  8.8 2.3 %collective-permute-done.1 = bf16[512,128]{1,0:T(8,128)(2,1)S(1)} collective-permute-done((bf16[512,128]{1,0:T(8,128)(2,1)}, bf16[512,128]{1,0:T(8,128)(2,1)S(1)}, u32[]{:S(2)}, u32[]{:S(2)}) %collective-permute-start.1) | collective-permute-done | bytes 131104 | tf_op jit(solution)/shard_map/ppermute | solution.py:14
  11.5 0.8 %fusion.24 = f32[512,128]{0,1:T(8,128)S(1)} fusion(bf16[512,2048]{1,0:T(8,128)(2,1)S(1)} %get-tuple-element.12, bf16[2048,128]{1,0:T(8,128)(2,1)S(1)} %pad_maximum_fusion.2), kind=kOutput, calls=%fused_computation.53 | convolution fusion | flops 268435456 | bytes 2883584 | tf_op jit(solution)/shard_map/dot_general | solution.py:100
  12.3 1.1 %collective-permute-done.3 = bf16[2048,128]{1,0:T(8,128)(2,1)S(1)} collective-permute-done((bf16[2048,128]{1,0:T(8,128)(2,1)S(1)}, bf16[2048,128]{1,0:T(8,128)(2,1)S(1)}, u32[]{:S(2)}, u32[]{:S(2)}) %collective-permute-start.3) | collective-permute-done | bytes 524320 | tf_op jit(solution)/shard_map/ppermute | solution.py:14
  13.4 0.8 %reduce-precision_convert_fusion = (bf16[512,128]{0,1:T(8,128)(2,1)S(1)}, bf16[512,128]{0,1:T(8,128)(2,1)S(1)}, f32[512,128]{0,1:T(8,128)S(1)}) fusion(f32[512,128]{0,1:T(8,128)S(1)} %fusion.24, bf16[512,2048]{1,0:T(8,128)(2,1)S(1)} %get-tuple-element.14, bf16[2048,128]{1,0:T(8,128)(2,1)S(1)} %collective-permute-done.3), kind=kOutput, calls=%fused_computation.11 | convolution fusion | flops 268763136 | bytes 3407872 | tf_op jit(solution)/shard_map/dot_general | solution.py:101
  16.1 1.8 %collective-permute-done.4 = f32[128,128]{1,0:T(8,128)S(1)} collective-permute-done((f32[128,128]{1,0:T(8,128)S(1)}, f32[128,128]{1,0:T(8,128)S(1)}, u32[]{:S(2)}, u32[]{:S(2)}) %collective-permute-start.4) | collective-permute-done | bytes 65568 | tf_op jit(solution)/shard_map/ppermute | solution.py:14
  17.9 1.6 %collective-permute-start.5 = (f32[128,128]{1,0:T(8,128)S(1)}, f32[128,128]{1,0:T(8,128)S(1)}, u32[]{:S(2)}, u32[]{:S(2)}) collective-permute-start(f32[128,128]{1,0:T(8,128)S(1)} %add.97), channel_id=1, source_target_pairs={{0,8},{4,12},{8,0},{12,4},{16,24},{20,28},{24,16},{28,20},{1,9},{5... | collective-permute-start | bytes 196616 | tf_op jit(solution)/shard_map/ppermute | solution.py:14
  20.3 1.9 %collective-permute-done.5 = f32[128,128]{1,0:T(8,128)S(1)} collective-permute-done((f32[128,128]{1,0:T(8,128)S(1)}, f32[128,128]{1,0:T(8,128)S(1)}, u32[]{:S(2)}, u32[]{:S(2)}) %collective-permute-start.5) | collective-permute-done | bytes 65568 | tf_op jit(solution)/shard_map/ppermute | solution.py:14
  22.5 0.9 %fusion.23 = (f32[512,128]{1,0:T(8,128)}, f32[512,128]{1,0:T(8,128)}, f32[512,128]{1,0:T(8,128)}) fusion(f32[2048,128]{1,0:T(8,128)S(1)} %fusion), kind=kLoop, calls=%fused_computation.52 | loop fusion | bytes 1572864 | tf_op jit(solution)/shard_map/slice | solution.py:120
  23.3 1.5 %collective-permute-start.7 = (f32[128,128]{1,0:T(8,128)S(1)}, f32[128,128]{1,0:T(8,128)S(1)}, u32[]{:S(2)}, u32[]{:S(2)}) collective-permute-start(f32[128,128]{1,0:T(8,128)S(1)} %add.98), channel_id=1, source_target_pairs={{0,16},{4,20},{8,24},{12,28},{16,0},{20,4},{24,8},{28,12},{1,17},{... | collective-permute-start | bytes 196616 | tf_op jit(solution)/shard_map/ppermute | solution.py:14
  25.5 2.1 %collective-permute-done.7 = f32[128,128]{1,0:T(8,128)S(1)} collective-permute-done((f32[128,128]{1,0:T(8,128)S(1)}, f32[128,128]{1,0:T(8,128)S(1)}, u32[]{:S(2)}, u32[]{:S(2)}) %collective-permute-start.7) | collective-permute-done | bytes 65568 | tf_op jit(solution)/shard_map/ppermute | solution.py:14
  27.6 1.5 %collective-permute-start.12 = (f32[512,128]{1,0:T(8,128)}, f32[512,128]{1,0:T(8,128)}, u32[]{:S(2)}, u32[]{:S(2)}) collective-permute-start(f32[512,128]{1,0:T(8,128)} %get-tuple-element.19), channel_id=1, source_target_pairs={{0,16},{4,20},{8,24},{12,28},{16,0},{20,4},{24,8},{28,12},{1,17},{... | collective-permute-start | bytes 786440 | tf_op jit(solution)/shard_map/ppermute | solution.py:14
  29.2 1.5 %collective-permute-start.11 = (f32[512,128]{1,0:T(8,128)}, f32[512,128]{1,0:T(8,128)}, u32[]{:S(2)}, u32[]{:S(2)}) collective-permute-start(f32[512,128]{1,0:T(8,128)} %get-tuple-element.18), channel_id=1, source_target_pairs={{0,24},{4,28},{8,16},{12,20},{16,8},{20,12},{24,0},{28,4},{1,25},{... | collective-permute-start | bytes 786440 | tf_op jit(solution)/shard_map/ppermute | solution.py:14
  30.7 1.6 %collective-permute-start.8 = (f32[128,128]{1,0:T(8,128)S(1)}, f32[128,128]{1,0:T(8,128)S(1)}, u32[]{:S(2)}, u32[]{:S(2)}) collective-permute-start(f32[128,128]{1,0:T(8,128)S(1)} %add.102), channel_id=1, source_target_pairs={{0,1},{1,0},{2,3},{3,2},{4,5},{5,4},{6,7},{7,6},{8,9},{9,8},{10,11... | collective-permute-start | bytes 196616 | tf_op jit(solution)/shard_map/ppermute | solution.py:14
  32.3 2.7 %collective-permute-done.8 = f32[128,128]{1,0:T(8,128)S(1)} collective-permute-done((f32[128,128]{1,0:T(8,128)S(1)}, f32[128,128]{1,0:T(8,128)S(1)}, u32[]{:S(2)}, u32[]{:S(2)}) %collective-permute-start.8) | collective-permute-done | bytes 65568 | tf_op jit(solution)/shard_map/ppermute | solution.py:14
  35.0 3.1 %collective-permute-start.9 = (f32[128,128]{1,0:T(8,128)S(1)}, f32[128,128]{1,0:T(8,128)S(1)}, u32[]{:S(2)}, u32[]{:S(2)}) collective-permute-start(f32[128,128]{1,0:T(8,128)S(1)} %add.103), channel_id=1, source_target_pairs={{0,2},{1,3},{2,0},{3,1},{4,6},{5,7},{6,4},{7,5},{8,10},{9,11},{10,... | collective-permute-start | bytes 196616 | tf_op jit(solution)/shard_map/ppermute | solution.py:14
  38.1 2.2 %collective-permute-done.9 = f32[128,128]{1,0:T(8,128)S(1)} collective-permute-done((f32[128,128]{1,0:T(8,128)S(1)}, f32[128,128]{1,0:T(8,128)S(1)}, u32[]{:S(2)}, u32[]{:S(2)}) %collective-permute-start.9) | collective-permute-done | bytes 65568 | tf_op jit(solution)/shard_map/ppermute | solution.py:14
  41.0 1.2 %fusion.3 = f32[512,128]{1,0:T(8,128)S(1)} fusion(f32[512,128]{1,0:T(8,128)} %collective-permute-done.12, f32[512,128]{1,0:T(8,128)} %collective-permute-done.11, f32[512,128]{1,0:T(8,128)} %collective-permute-done.10, f32[2048,128]{1,0:T(8,128)S(1)} %fusion), kind=kLoop, calls=%fused_computation.15 | loop fusion | flops 196608 | bytes 1310720 | tf_op jit(solution)/shard_map/add | solution.py:123
  42.9 4.2 %collective-permute-start.15 = (f32[128,128]{1,0:T(8,128)S(1)}, f32[128,128]{1,0:T(8,128)S(1)}, u32[]{:S(2)}, u32[]{:S(2)}) collective-permute-start(f32[128,128]{1,0:T(8,128)S(1)} %get-tuple-element.33), channel_id=1, source_target_pairs={{0,3},{1,2},{2,1},{3,0},{4,7},{5,6},{6,5},{7,4},{8,11},{9,10},{10,... | collective-permute-start | bytes 196616 | tf_op jit(solution)/shard_map/ppermute | solution.py:14
  47.7 6.3 %inverse_factor.1 = f32[128,128]{1,0:T(8,128)} custom-call(f32[128,128]{1,0:T(8,128)} %add.104.gram_ref), custom_call_target="tpu_custom_call" | custom-call | flops 6000000000 | bytes 131072 | tf_op jit(solution)/shard_map/inverse_factor/pallas_call | solution.py:65
  54.1 1.3 %constant_dynamic-update-slice_fusion.3 = (f32[512,128]{1,0:T(8,128)S(1)}, f32[128,128]{1,0:T(8,128)S(1)}) fusion(f32[512,128]{1,0:T(8,128)S(1)} %broadcast_in_dim.3, s32[]{:T(128)S(6)} %select_n.48, f32[128,128]{1,0:T(8,128)} %inverse_factor.1, f32[128,128]{1,0:T(8,128)S(1)} %collective-permute-done.15, f32[128,128]{1,0:T(8,128)S(1)} %collective-permute-done.14, ...), kind=kOutput, calls=%fused_computation.34 | convolution fusion | flops 25231360 | bytes 459776 | tf_op jit(solution)/shard_map/dot_general | solution.py:18
  55.4 1.4 %collective-permute-start.16 = (f32[128,128]{1,0:T(8,128)S(1)}, f32[128,128]{1,0:T(8,128)S(1)}, u32[]{:S(2)}, u32[]{:S(2)}) collective-permute-start(f32[128,128]{1,0:T(8,128)S(1)} %get-tuple-element.39), channel_id=1, source_target_pairs={{0,1},{1,0},{2,3},{3,2},{4,5},{5,4},{6,7},{7,6},{8,9},{9,8},{10,11... | collective-permute-start | bytes 196616 | tf_op jit(solution)/shard_map/ppermute | solution.py:14
  56.8 2.9 %collective-permute-start.17 = (f32[128,128]{1,0:T(8,128)S(1)}, f32[128,128]{1,0:T(8,128)S(1)}, u32[]{:S(2)}, u32[]{:S(2)}) collective-permute-start(f32[128,128]{1,0:T(8,128)S(1)} %get-tuple-element.39), channel_id=1, source_target_pairs={{0,2},{1,3},{2,0},{3,1},{4,6},{5,7},{6,4},{7,5},{8,10},{9,11},{10,... | collective-permute-start | bytes 196616 | tf_op jit(solution)/shard_map/ppermute | solution.py:14
  59.9 2.8 %collective-permute-done.17 = f32[128,128]{1,0:T(8,128)S(1)} collective-permute-done((f32[128,128]{1,0:T(8,128)S(1)}, f32[128,128]{1,0:T(8,128)S(1)}, u32[]{:S(2)}, u32[]{:S(2)}) %collective-permute-start.17) | collective-permute-done | bytes 65568 | tf_op jit(solution)/shard_map/ppermute | solution.py:14
  62.7 3.1 %collective-permute-done.18 = f32[128,128]{1,0:T(8,128)S(1)} collective-permute-done((f32[128,128]{1,0:T(8,128)S(1)}, f32[128,128]{1,0:T(8,128)S(1)}, u32[]{:S(2)}, u32[]{:S(2)}) %collective-permute-start.18) | collective-permute-done | bytes 65568 | tf_op jit(solution)/shard_map/ppermute | solution.py:14
  65.9 1.5 %collective-permute-start.21 = (bf16[512,128]{1,0:T(8,128)(2,1)S(1)}, bf16[512,128]{1,0:T(8,128)(2,1)S(1)}, u32[]{:S(2)}, u32[]{:S(2)}) collective-permute-start(bf16[512,128]{1,0:T(8,128)(2,1)S(1)} %convert_element_type.22), channel_id=1, source_target_pairs={{0,24},{4,28},{8,16},{12,20},{16,8},{20,12},{24,0},{28,4},{1,25},{... | collective-permute-start | bytes 393224 | tf_op jit(solution)/shard_map/ppermute | solution.py:14
  67.9 1.5 %collective-permute-start.19 = (bf16[512,128]{1,0:T(8,128)(2,1)S(1)}, bf16[512,128]{1,0:T(8,128)(2,1)S(1)}, u32[]{:S(2)}, u32[]{:S(2)}) collective-permute-start(bf16[512,128]{1,0:T(8,128)(2,1)S(1)} %convert_element_type.22), channel_id=1, source_target_pairs={{0,8},{4,12},{8,0},{12,4},{16,24},{20,28},{24,16},{28,20},{1,9},{5... | collective-permute-start | bytes 393224 | tf_op jit(solution)/shard_map/ppermute | solution.py:14
  69.4 2.5 %collective-permute-done.21 = bf16[512,128]{1,0:T(8,128)(2,1)S(1)} collective-permute-done((bf16[512,128]{1,0:T(8,128)(2,1)S(1)}, bf16[512,128]{1,0:T(8,128)(2,1)S(1)}, u32[]{:S(2)}, u32[]{:S(2)}) %collective-permute-start.21) | collective-permute-done | bytes 131104 | tf_op jit(solution)/shard_map/ppermute | solution.py:14
  71.9 1.3 %collective-permute-done.20 = bf16[512,128]{1,0:T(8,128)(2,1)S(1)} collective-permute-done((bf16[512,128]{1,0:T(8,128)(2,1)S(1)}, bf16[512,128]{1,0:T(8,128)(2,1)S(1)}, u32[]{:S(2)}, u32[]{:S(2)}) %collective-permute-start.20) | collective-permute-done | bytes 131104 | tf_op jit(solution)/shard_map/ppermute | solution.py:14
  74.0 0.9 %multiply_reduce_fusion.1 = f32[512]{0:T(512)S(1)} fusion(bf16[512,2048]{1,0:T(8,128)(2,1)S(1)} %copy-done.1, f32[512,128]{1,0:T(8,128)S(1)} %fusion.14, bf16[512,128]{1,0:T(8,128)(2,1)S(1)} %collective-permute-done.21, bf16[512,128]{1,0:T(8,128)(2,1)S(1)} %collective-permute-done.20, bf16[512,128]{1,0:T(8,128)(2,1)S(1)} %collective-permute-done.19, ...), kind=kOutput, calls=%fused_computation.1 | convolution fusion | flops 275840512 | bytes 2885632 | tf_op jit(solution)/shard_map/dot_general | solution.py:153
  75.2 0.9 %multiply_reduce_fusion = f32[512]{0:T(512)S(1)} fusion(bf16[512,2048]{1,0:T(8,128)(2,1)S(1)} %get-tuple-element.14, bf16[2048,128]{1,0:T(8,128)(2,1)S(1)} %collective-permute-done.22, f32[512,128]{1,0:T(8,128)S(1)} %fusion.14), kind=kOutput, calls=%fused_computation | convolution fusion | flops 273743360 | bytes 2885632 | tf_op jit(solution)/shard_map/dot_general | solution.py:153
  (58 shorter events, 9.8 us)
Async XLA Ops:
  0.6 8.2 %collective-permute-start.2 = (bf16[512,128]{1,0:T(8,128)(2,1)}, bf16[512,128]{1,0:T(8,128)(2,1)S(1)}, u32[]{:S(2)}, u32[]{:S(2)}) collective-permute-start(bf16[512,128]{1,0:T(8,128)(2,1)} %param.3), channel_id=1, source_target_pairs={{0,24},{4,28},{8,16},{12,20},{16,8},{20,12},{24,0},{28,4},{1,25},{... | collective-permute-start | bytes 393224 | tf_op jit(solution)/shard_map/ppermute | solution.py:14
  4.6 6.5 %collective-permute-start.1 = (bf16[512,128]{1,0:T(8,128)(2,1)}, bf16[512,128]{1,0:T(8,128)(2,1)S(1)}, u32[]{:S(2)}, u32[]{:S(2)}) collective-permute-start(bf16[512,128]{1,0:T(8,128)(2,1)} %param.3), channel_id=1, source_target_pairs={{0,16},{4,20},{8,24},{12,28},{16,0},{20,4},{24,8},{28,12},{1,17},{... | collective-permute-start | bytes 393224 | tf_op jit(solution)/shard_map/ppermute | solution.py:14
  5.1 6.3 %collective-permute-start = (bf16[512,128]{1,0:T(8,128)(2,1)}, bf16[512,128]{1,0:T(8,128)(2,1)S(1)}, u32[]{:S(2)}, u32[]{:S(2)}) collective-permute-start(bf16[512,128]{1,0:T(8,128)(2,1)} %param.3), channel_id=1, source_target_pairs={{0,8},{4,12},{8,0},{12,4},{16,24},{20,28},{24,16},{28,20},{1,9},{5... | collective-permute-start | bytes 393224 | tf_op jit(solution)/shard_map/ppermute | solution.py:14
  7.9 3.5 %copy-start.6 = (bf16[512,128]{1,0:T(8,128)(2,1)S(1)}, bf16[512,128]{1,0:T(8,128)(2,1)}, u32[]{:S(2)}) copy-start(bf16[512,128]{1,0:T(8,128)(2,1)} %param.3) | copy-start | bytes 393220
  8.5 11.0 %copy-start = (bf16[512,2048]{1,0:T(8,128)(2,1)}, bf16[512,2048]{1,0:T(8,128)(2,1)S(1)}, u32[]{:S(2)}) copy-start(bf16[512,2048]{1,0:T(8,128)(2,1)S(1)} %get-tuple-element.12) | copy-start | bytes 6291460
  11.4 2.0 %collective-permute-start.3 = (bf16[2048,128]{1,0:T(8,128)(2,1)S(1)}, bf16[2048,128]{1,0:T(8,128)(2,1)S(1)}, u32[]{:S(2)}, u32[]{:S(2)}) collective-permute-start(bf16[2048,128]{1,0:T(8,128)(2,1)S(1)} %pad_maximum_fusion.2), channel_id=1, source_target_pairs={{0,4},{4,0},{8,12},{12,8},{16,20},{20,16},{24,28},{28,24},{1,5},{5... | collective-permute-start | bytes 1572872 | tf_op jit(solution)/shard_map/ppermute | solution.py:14
  15.1 7.2 %collective-permute-start.6 = (f32[2048,128]{1,0:T(8,128)S(1)}, f32[2048,128]{1,0:T(8,128)S(1)}, u32[]{:S(2)}, u32[]{:S(2)}) collective-permute-start(f32[2048,128]{1,0:T(8,128)S(1)} %slice_add_fusion), channel_id=1, source_target_pairs={{0,4},{4,0},{8,12},{12,8},{16,20},{20,16},{24,28},{28,24},{1,5},{5... | collective-permute-start | bytes 3145736 | tf_op jit(solution)/shard_map/ppermute | solution.py:14
  15.7 2.2 %collective-permute-start.4 = (f32[128,128]{1,0:T(8,128)S(1)}, f32[128,128]{1,0:T(8,128)S(1)}, u32[]{:S(2)}, u32[]{:S(2)}) collective-permute-start(f32[128,128]{1,0:T(8,128)S(1)} %fusion.25), channel_id=1, source_target_pairs={{0,4},{4,0},{8,12},{12,8},{16,20},{20,16},{24,28},{28,24},{1,5},{5... | collective-permute-start | bytes 196616 | tf_op jit(solution)/shard_map/ppermute | solution.py:14
  17.9 4.3 %collective-permute-start.5 = (f32[128,128]{1,0:T(8,128)S(1)}, f32[128,128]{1,0:T(8,128)S(1)}, u32[]{:S(2)}, u32[]{:S(2)}) collective-permute-start(f32[128,128]{1,0:T(8,128)S(1)} %add.97), channel_id=1, source_target_pairs={{0,8},{4,12},{8,0},{12,4},{16,24},{20,28},{24,16},{28,20},{1,9},{5... | collective-permute-start | bytes 196616 | tf_op jit(solution)/shard_map/ppermute | solution.py:14
  23.3 4.3 %collective-permute-start.7 = (f32[128,128]{1,0:T(8,128)S(1)}, f32[128,128]{1,0:T(8,128)S(1)}, u32[]{:S(2)}, u32[]{:S(2)}) collective-permute-start(f32[128,128]{1,0:T(8,128)S(1)} %add.98), channel_id=1, source_target_pairs={{0,16},{4,20},{8,24},{12,28},{16,0},{20,4},{24,8},{28,12},{1,17},{... | collective-permute-start | bytes 196616 | tf_op jit(solution)/shard_map/ppermute | solution.py:14
  24.8 16.2 %collective-permute-start.10 = (f32[512,128]{1,0:T(8,128)}, f32[512,128]{1,0:T(8,128)}, u32[]{:S(2)}, u32[]{:S(2)}) collective-permute-start(f32[512,128]{1,0:T(8,128)} %get-tuple-element.17), channel_id=1, source_target_pairs={{0,8},{4,12},{8,0},{12,4},{16,24},{20,28},{24,16},{28,20},{1,9},{5... | collective-permute-start | bytes 786440 | tf_op jit(solution)/shard_map/ppermute | solution.py:14
  27.6 13.4 %collective-permute-start.12 = (f32[512,128]{1,0:T(8,128)}, f32[512,128]{1,0:T(8,128)}, u32[]{:S(2)}, u32[]{:S(2)}) collective-permute-start(f32[512,128]{1,0:T(8,128)} %get-tuple-element.19), channel_id=1, source_target_pairs={{0,16},{4,20},{8,24},{12,28},{16,0},{20,4},{24,8},{28,12},{1,17},{... | collective-permute-start | bytes 786440 | tf_op jit(solution)/shard_map/ppermute | solution.py:14
  29.2 11.8 %collective-permute-start.11 = (f32[512,128]{1,0:T(8,128)}, f32[512,128]{1,0:T(8,128)}, u32[]{:S(2)}, u32[]{:S(2)}) collective-permute-start(f32[512,128]{1,0:T(8,128)} %get-tuple-element.18), channel_id=1, source_target_pairs={{0,24},{4,28},{8,16},{12,20},{16,8},{20,12},{24,0},{28,4},{1,25},{... | collective-permute-start | bytes 786440 | tf_op jit(solution)/shard_map/ppermute | solution.py:14
  30.7 4.3 %collective-permute-start.8 = (f32[128,128]{1,0:T(8,128)S(1)}, f32[128,128]{1,0:T(8,128)S(1)}, u32[]{:S(2)}, u32[]{:S(2)}) collective-permute-start(f32[128,128]{1,0:T(8,128)S(1)} %add.102), channel_id=1, source_target_pairs={{0,1},{1,0},{2,3},{3,2},{4,5},{5,4},{6,7},{7,6},{8,9},{9,8},{10,11... | collective-permute-start | bytes 196616 | tf_op jit(solution)/shard_map/ppermute | solution.py:14
  35.0 5.4 %collective-permute-start.9 = (f32[128,128]{1,0:T(8,128)S(1)}, f32[128,128]{1,0:T(8,128)S(1)}, u32[]{:S(2)}, u32[]{:S(2)}) collective-permute-start(f32[128,128]{1,0:T(8,128)S(1)} %add.103), channel_id=1, source_target_pairs={{0,2},{1,3},{2,0},{3,1},{4,6},{5,7},{6,4},{7,5},{8,10},{9,11},{10,... | collective-permute-start | bytes 196616 | tf_op jit(solution)/shard_map/ppermute | solution.py:14
  42.2 0.7 copy-start.2
  42.9 11.2 %collective-permute-start.15 = (f32[128,128]{1,0:T(8,128)S(1)}, f32[128,128]{1,0:T(8,128)S(1)}, u32[]{:S(2)}, u32[]{:S(2)}) collective-permute-start(f32[128,128]{1,0:T(8,128)S(1)} %get-tuple-element.33), channel_id=1, source_target_pairs={{0,3},{1,2},{2,1},{3,0},{4,7},{5,6},{6,5},{7,4},{8,11},{9,10},{10,... | collective-permute-start | bytes 196616 | tf_op jit(solution)/shard_map/ppermute | solution.py:14
  47.1 7.0 %collective-permute-start.14 = (f32[128,128]{1,0:T(8,128)S(1)}, f32[128,128]{1,0:T(8,128)S(1)}, u32[]{:S(2)}, u32[]{:S(2)}) collective-permute-start(f32[128,128]{1,0:T(8,128)S(1)} %get-tuple-element.34), channel_id=1, source_target_pairs={{0,2},{1,3},{2,0},{3,1},{4,6},{5,7},{6,4},{7,5},{8,10},{9,11},{10,... | collective-permute-start | bytes 196616 | tf_op jit(solution)/shard_map/ppermute | solution.py:14
  47.1 7.0 %collective-permute-start.13 = (f32[128,128]{1,0:T(8,128)S(1)}, f32[128,128]{1,0:T(8,128)S(1)}, u32[]{:S(2)}, u32[]{:S(2)}) collective-permute-start(f32[128,128]{1,0:T(8,128)S(1)} %get-tuple-element.32), channel_id=1, source_target_pairs={{0,1},{1,0},{2,3},{3,2},{4,5},{5,4},{6,7},{7,6},{8,9},{9,8},{10,11... | collective-permute-start | bytes 196616 | tf_op jit(solution)/shard_map/ppermute | solution.py:14
  54.1 19.3 %copy-start.4 = (f32[128,128]{1,0:T(8,128)S(1)}, f32[128,128]{1,0:T(8,128)}, u32[]{:S(2)}) copy-start(f32[128,128]{1,0:T(8,128)} %inverse_factor.1) | copy-start | bytes 196612
  54.1 19.9 %copy-start.1 = (bf16[512,2048]{1,0:T(8,128)(2,1)S(1)}, bf16[512,2048]{1,0:T(8,128)(2,1)}, u32[]{:S(2)}) copy-start(bf16[512,2048]{1,0:T(8,128)(2,1)} %copy-done) | copy-start | bytes 6291460
  55.4 4.5 %collective-permute-start.16 = (f32[128,128]{1,0:T(8,128)S(1)}, f32[128,128]{1,0:T(8,128)S(1)}, u32[]{:S(2)}, u32[]{:S(2)}) collective-permute-start(f32[128,128]{1,0:T(8,128)S(1)} %get-tuple-element.39), channel_id=1, source_target_pairs={{0,1},{1,0},{2,3},{3,2},{4,5},{5,4},{6,7},{7,6},{8,9},{9,8},{10,11... | collective-permute-start | bytes 196616 | tf_op jit(solution)/shard_map/ppermute | solution.py:14
  56.8 5.9 %collective-permute-start.17 = (f32[128,128]{1,0:T(8,128)S(1)}, f32[128,128]{1,0:T(8,128)S(1)}, u32[]{:S(2)}, u32[]{:S(2)}) collective-permute-start(f32[128,128]{1,0:T(8,128)S(1)} %get-tuple-element.39), channel_id=1, source_target_pairs={{0,2},{1,3},{2,0},{3,1},{4,6},{5,7},{6,4},{7,5},{8,10},{9,11},{10,... | collective-permute-start | bytes 196616 | tf_op jit(solution)/shard_map/ppermute | solution.py:14
  59.8 6.1 %collective-permute-start.18 = (f32[128,128]{1,0:T(8,128)S(1)}, f32[128,128]{1,0:T(8,128)S(1)}, u32[]{:S(2)}, u32[]{:S(2)}) collective-permute-start(f32[128,128]{1,0:T(8,128)S(1)} %get-tuple-element.39), channel_id=1, source_target_pairs={{0,3},{1,2},{2,1},{3,0},{4,7},{5,6},{6,5},{7,4},{8,11},{9,10},{10,... | collective-permute-start | bytes 196616 | tf_op jit(solution)/shard_map/ppermute | solution.py:14
  65.8 9.1 %copy-start.3 = (f32[512,128]{1,0:T(8,128)}, f32[512,128]{1,0:T(8,128)S(1)}, u32[]{:S(2)}) copy-start(f32[512,128]{1,0:T(8,128)S(1)} %constant_dynamic-update-slice_fusion) | copy-start | bytes 786436
  65.9 6.0 %collective-permute-start.21 = (bf16[512,128]{1,0:T(8,128)(2,1)S(1)}, bf16[512,128]{1,0:T(8,128)(2,1)S(1)}, u32[]{:S(2)}, u32[]{:S(2)}) collective-permute-start(bf16[512,128]{1,0:T(8,128)(2,1)S(1)} %convert_element_type.22), channel_id=1, source_target_pairs={{0,24},{4,28},{8,16},{12,20},{16,8},{20,12},{24,0},{28,4},{1,25},{... | collective-permute-start | bytes 393224 | tf_op jit(solution)/shard_map/ppermute | solution.py:14
  67.3 5.9 %collective-permute-start.20 = (bf16[512,128]{1,0:T(8,128)(2,1)S(1)}, bf16[512,128]{1,0:T(8,128)(2,1)S(1)}, u32[]{:S(2)}, u32[]{:S(2)}) collective-permute-start(bf16[512,128]{1,0:T(8,128)(2,1)S(1)} %convert_element_type.22), channel_id=1, source_target_pairs={{0,16},{4,20},{8,24},{12,28},{16,0},{20,4},{24,8},{28,12},{1,17},{... | collective-permute-start | bytes 393224 | tf_op jit(solution)/shard_map/ppermute | solution.py:14
  67.9 5.3 %collective-permute-start.19 = (bf16[512,128]{1,0:T(8,128)(2,1)S(1)}, bf16[512,128]{1,0:T(8,128)(2,1)S(1)}, u32[]{:S(2)}, u32[]{:S(2)}) collective-permute-start(bf16[512,128]{1,0:T(8,128)(2,1)S(1)} %convert_element_type.22), channel_id=1, source_target_pairs={{0,8},{4,12},{8,0},{12,4},{16,24},{20,28},{24,16},{28,20},{1,9},{5... | collective-permute-start | bytes 393224 | tf_op jit(solution)/shard_map/ppermute | solution.py:14
  73.3 2.0 %collective-permute-start.22 = (bf16[2048,128]{1,0:T(8,128)(2,1)S(1)}, bf16[2048,128]{1,0:T(8,128)(2,1)S(1)}, u32[]{:S(2)}, u32[]{:S(2)}) collective-permute-start(bf16[2048,128]{1,0:T(8,128)(2,1)S(1)} %pad_maximum_fusion.3), channel_id=1, source_target_pairs={{0,4},{4,0},{8,12},{12,8},{16,20},{20,16},{24,28},{28,24},{1,5},{5... | collective-permute-start | bytes 1572872 | tf_op jit(solution)/shard_map/ppermute | solution.py:14
  74.0 1.3 %copy-start.5 = (f32[512,128]{1,0:T(8,128)}, f32[512,128]{1,0:T(8,128)S(1)}, u32[]{:S(2)}) copy-start(f32[512,128]{1,0:T(8,128)S(1)} %fusion.14) | copy-start | bytes 786436

commit v3 on v2

--- a/solution.py
+++ b/solution.py
@@ -110,37 +110,34 @@
         twice = lax.dot_general(side, both, (((0,), (0,)), ((), ())), preferred_element_type=jnp.float32)
         return twice[:, :rank] + twice[:, rank:]
 
-    pieces = products(even_columns) + flipped(products(odd_columns), "inner", 1)
-    gram = gram + flipped(gram, "inner", 1)
+    gram, both = lax.optimization_barrier((gram, both))
+    gram, odd_pieces = lax.optimization_barrier((gram + flipped(gram, "inner", 1), products(odd_columns)))
+    pieces = products(even_columns) + flipped(odd_pieces, "inner", 1)
     pieces = pieces.reshape(inner // 2, piece, rank)
+    gram = gram + flipped(gram, "outer", 1)
+    gram = gram + flipped(gram, "outer", 2)
+    own = pieces[0] + flipped(pieces[3], "inner", 6)+ flipped(pieces[1], "inner", 2)+ flipped(pieces[2], "inner", 4)
+    gram, own = lax.optimization_barrier((gram, own))
     gram = gram + flipped(gram, "inner", 2)
-    gram, near = lax.optimization_barrier((gram, pieces[1]))
-    for level in range(2, inner.bit_length() - 1):
-        gram = gram + flipped(gram, "inner", 1 << level)
-    gram, *rest = lax.optimization_barrier((gram, *[pieces[mask // 2] for mask in reversed(evens[1:])]))
-    own = pieces[0] + flipped(near, "inner", 2)
-    for mask, block in zip(reversed(evens[1:]), rest):
-        own = own + flipped(block, "inner", mask)
-    for level in range(outer.bit_length() - 1):
-        gram = gram + flipped(gram, "outer", 1 << level)
-    gram, _ = lax.optimization_barrier((gram, own))
+    gram = gram + flipped(gram, "inner", 4)
     share = lax.dynamic_slice_in_dim(own, mine * part, part, 0)
     for mask in range(1, outer):
         share = share + flipped(
             lax.dynamic_slice_in_dim(own, (mine ^ mask) * part, part, 0), "outer", mask
         )
+    gram, share = lax.optimization_barrier((gram, share))
+
+    summed = jnp.zeros((piece, rank), jnp.float32)
+    summed = lax.dynamic_update_slice_in_dim(summed, share, mine * part, 0)
+    for mask in range(1, outer):
+        summed = lax.dynamic_update_slice_in_dim(
+            summed, flipped(share, "outer", mask), (mine ^ mask) * part, 0
+        )
 
     inverse = inverse_factor(gram)
     basis = exact_dot(sketch, inverse * math.sqrt(total_rows), ((1,), (1,)))
     basis_low = basis.astype(jnp.bfloat16)
-
-    share = exact_dot(share, inverse * (math.sqrt(width) / math.sqrt(total_rows)), ((1,), (1,)))
-    projection = jnp.zeros((piece, rank), jnp.float32)
-    projection = lax.dynamic_update_slice_in_dim(projection, share, mine * part, 0)
-    for mask in range(1, outer):
-        projection = lax.dynamic_update_slice_in_dim(
-            projection, flipped(share, "outer", mask), (mine ^ mask) * part, 0
-        )
+    projection = exact_dot(summed, inverse * (math.sqrt(width) / math.sqrt(total_rows)), ((1,), (1,)))
     projection_low = projection.astype(jnp.bfloat16)
 
     got = {0: projection_low}

time: 77 us -> 72.4 us (0.940)
  waiting for transfers between devices: 24.8 us -> 20.6 us
  starting transfers between devices: 29.8 us -> 27.5 us
  other arithmetic: 3.38 us -> 5.08 us
    ppermute x23, waiting for transfers between devices: 24.8 us -> 20.6 us  [flipped(): lax.ppermute(block, axis, [(low, low ^ mask) for low in range(count)])]
    ppermute x23, starting transfers between devices: 29.8 us -> 27.5 us  [flipped(): lax.ppermute(block, axis, [(low, low ^ mask) for low in range(count)])]
    add x6 -> x7, other arithmetic: 1.96 us -> 3.66 us  [the longest x1 1.16 us: local(): pieces[0] + flipped(pieces[3], 'inner', 6) + flipped(pieces[1], 'inner', 2)]
  transfers between devices with their start and end apart: 23 -> 23, of which waited for: 14 -> 14; matrix products, arithmetic and copies ran while one was open for 10% -> 13% of each run, Pallas kernels for 8% -> 9%
where the time goes in v3:
time: 72.4 us; the launch traced here: 72.1 us
  starting transfers between devices  27.5 us (38%)
  waiting for transfers between devices  20.6 us (28%)
  matrix products  8.09 us (11%)
  Pallas kernels  6.31 us (9%)
  other arithmetic  5.08 us (7%)
  local copies, waits for them, and re-layouts  3.63 us (5%)
  between operations  0.91 us (1%)
    ppermute x23, starting transfers between devices, flipped(): lax.ppermute(block, axis, [(low, low ^ mask) for low in range(count)])  27.5 us
    ppermute x23, waiting for transfers between devices, flipped(): lax.ppermute(block, axis, [(low, low ^ mask) for low in range(count)])  20.6 us
    pallas_call x1, Pallas kernels, inverse_factor(): pl.pallas_call(functools.partial(factor_kernel, block), out_shape=jax.Sha...  6.31 us
    dot_general x3, matrix products, exact_dot(): lax.dot_general(a, b, (contract, ((), ())), precision=lax.Precision.HIGHE...  3.02 us
    dynamic_slice x1, local copies, waits for them, and re-layouts, columns(): lax.dynamic_slice_in_dim(samples, (me ^ mask) * piece, piece, 1)  2.63 us
    dot_general x2, matrix products, errors(): lax.dot_general(basis_low, factor, (((1,), (1,)), ((), ())), preferred_el...  1.87 us
    dot_general x2, matrix products, products(): lax.dot_general(side, both, (((0,), (0,)), ((), ())), preferred_element_t...  1.52 us
  transfers between devices with their start and end apart: 23, of which 14 were waited for; matrix products, arithmetic and copies ran while one was open for 13% of the time, Pallas kernels for 9%

profile of v3, /device:TPU:0, one launch (start us, length us, event | category | flops | bytes accessed | tf_op | source)
XLA Modules:
  0.0 72.1 jit_solution(2164113004204384045)
XLA Ops:
  0.6 4.0 %collective-permute-start.2 = (bf16[512,128]{1,0:T(8,128)(2,1)}, bf16[512,128]{1,0:T(8,128)(2,1)S(1)}, u32[]{:S(2)}, u32[]{:S(2)}) collective-permute-start(bf16[512,128]{1,0:T(8,128)(2,1)} %param.3), channel_id=1, source_target_pairs={{0,24},{4,28},{8,16},{12,20},{16,8},{20,12},{24,0},{28,4},{1,25},{... | collective-permute-start | bytes 393224 | tf_op jit(solution)/shard_map/ppermute | solution.py:14
  5.2 2.6 %constant_dynamic-slice_fusion.6 = (bf16[512,512]{1,0:T(8,128)(2,1)S(1)}, bf16[512,512]{1,0:T(8,128)(2,1)S(1)}, bf16[512,512]{1,0:T(8,128)(2,1)S(1)}, bf16[512,5...) fusion(bf16[512,4096]{1,0:T(8,128)(2,1)} %param.2, ...), kind=kLoop, calls=%fused_computation.36 | loop fusion | bytes 8388640 | tf_op jit(solution)/shard_map/dynamic_slice | solution.py:93
  8.8 2.3 %collective-permute-done.1 = bf16[512,128]{1,0:T(8,128)(2,1)S(1)} collective-permute-done((bf16[512,128]{1,0:T(8,128)(2,1)}, bf16[512,128]{1,0:T(8,128)(2,1)S(1)}, u32[]{:S(2)}, u32[]{:S(2)}) %collective-permute-start.1) | collective-permute-done | bytes 131104 | tf_op jit(solution)/shard_map/ppermute | solution.py:14
  11.5 0.8 %fusion.16 = f32[512,128]{0,1:T(8,128)S(1)} fusion(bf16[512,2048]{1,0:T(8,128)(2,1)S(1)} %get-tuple-element.14, bf16[2048,128]{1,0:T(8,128)(2,1)S(1)} %pad_maximum_fusion.2), kind=kOutput, calls=%fused_computation.46 | convolution fusion | flops 268435456 | bytes 2883584 | tf_op jit(solution)/shard_map/dot_general | solution.py:100
  12.3 1.1 %collective-permute-done.3 = bf16[2048,128]{1,0:T(8,128)(2,1)S(1)} collective-permute-done((bf16[2048,128]{1,0:T(8,128)(2,1)S(1)}, bf16[2048,128]{1,0:T(8,128)(2,1)S(1)}, u32[]{:S(2)}, u32[]{:S(2)}) %collective-permute-start.3) | collective-permute-done | bytes 524320 | tf_op jit(solution)/shard_map/ppermute | solution.py:14
  13.4 0.8 %reduce-precision_convert_fusion = (bf16[512,128]{0,1:T(8,128)(2,1)S(1)}, bf16[512,128]{0,1:T(8,128)(2,1)S(1)}, f32[512,128]{0,1:T(8,128)S(1)}) fusion(f32[512,128]{0,1:T(8,128)S(1)} %fusion.16, bf16[512,2048]{1,0:T(8,128)(2,1)S(1)} %get-tuple-element.16, bf16[2048,128]{1,0:T(8,128)(2,1)S(1)} %collective-permute-done.3), kind=kOutput, calls=%fused_computation.11 | convolution fusion | flops 268763136 | bytes 3407872 | tf_op jit(solution)/shard_map/dot_general | solution.py:101
  17.0 1.7 %collective-permute-done.7 = f32[2048,128]{1,0:T(8,128)S(1)} collective-permute-done((f32[2048,128]{1,0:T(8,128)S(1)}, f32[2048,128]{1,0:T(8,128)S(1)}, u32[]{:S(2)}, u32[]{:S(2)}) %collective-permute-start.7) | collective-permute-done | bytes 1048608 | tf_op jit(solution)/shard_map/ppermute | solution.py:14
  18.8 0.9 %fusion.14 = (f32[512,128]{1,0:T(8,128)}, f32[512,128]{1,0:T(8,128)}, f32[512,128]{1,0:T(8,128)}) fusion(f32[2048,128]{1,0:T(8,128)S(1)} %fusion), kind=kLoop, calls=%fused_computation.44 | loop fusion | bytes 1572864 | tf_op jit(solution)/shard_map/slice | solution.py:119
  19.7 1.5 %collective-permute-start.10 = (f32[512,128]{1,0:T(8,128)}, f32[512,128]{1,0:T(8,128)}, u32[]{:S(2)}, u32[]{:S(2)}) collective-permute-start(f32[512,128]{1,0:T(8,128)} %get-tuple-element.34), channel_id=1, source_target_pairs={{0,16},{4,20},{8,24},{12,28},{16,0},{20,4},{24,8},{28,12},{1,17},{... | collective-permute-start | bytes 786440 | tf_op jit(solution)/shard_map/ppermute | solution.py:14
  21.9 1.3 %collective-permute-start.8 = (f32[512,128]{1,0:T(8,128)}, f32[512,128]{1,0:T(8,128)}, u32[]{:S(2)}, u32[]{:S(2)}) collective-permute-start(f32[512,128]{1,0:T(8,128)} %get-tuple-element.33), channel_id=1, source_target_pairs={{0,24},{4,28},{8,16},{12,20},{16,8},{20,12},{24,0},{28,4},{1,25},{... | collective-permute-start | bytes 786440 | tf_op jit(solution)/shard_map/ppermute | solution.py:14
  23.2 1.6 %collective-permute-start.5 = (f32[128,128]{1,0:T(8,128)S(1)}, f32[128,128]{1,0:T(8,128)S(1)}, u32[]{:S(2)}, u32[]{:S(2)}) collective-permute-start(f32[128,128]{1,0:T(8,128)S(1)} %add.97), channel_id=1, source_target_pairs={{0,1},{1,0},{2,3},{3,2},{4,5},{5,4},{6,7},{7,6},{8,9},{9,8},{10,11... | collective-permute-start | bytes 196616 | tf_op jit(solution)/shard_map/ppermute | solution.py:14
  24.8 2.7 %collective-permute-done.5 = f32[128,128]{1,0:T(8,128)S(1)} collective-permute-done((f32[128,128]{1,0:T(8,128)S(1)}, f32[128,128]{1,0:T(8,128)S(1)}, u32[]{:S(2)}, u32[]{:S(2)}) %collective-permute-start.5) | collective-permute-done | bytes 65568 | tf_op jit(solution)/shard_map/ppermute | solution.py:14
  27.5 2.7 %collective-permute-start.6 = (f32[128,128]{1,0:T(8,128)S(1)}, f32[128,128]{1,0:T(8,128)}, u32[]{:S(2)}, u32[]{:S(2)}) collective-permute-start(f32[128,128]{1,0:T(8,128)S(1)} %add.99), channel_id=1, source_target_pairs={{0,2},{1,3},{2,0},{3,1},{4,6},{5,7},{6,4},{7,5},{8,10},{9,11},{10,... | collective-permute-start | bytes 196616 | tf_op jit(solution)/shard_map/ppermute | solution.py:14
  30.2 2.7 %collective-permute-done.6 = f32[128,128]{1,0:T(8,128)} collective-permute-done((f32[128,128]{1,0:T(8,128)S(1)}, f32[128,128]{1,0:T(8,128)}, u32[]{:S(2)}, u32[]{:S(2)}) %collective-permute-start.6) | collective-permute-done | bytes 65568 | tf_op jit(solution)/shard_map/ppermute | solution.py:14
  32.8 0.8 %add.100 = f32[128,128]{1,0:T(8,128)S(1)} add(f32[128,128]{1,0:T(8,128)S(1)} %add.99, f32[128,128]{1,0:T(8,128)} %collective-permute-done.6) | non-fusion elementwise | flops 16384 | bytes 196608 | tf_op jit(solution)/shard_map/add | solution.py:118
  33.7 1.5 %collective-permute-done.8 = f32[512,128]{1,0:T(8,128)} collective-permute-done((f32[512,128]{1,0:T(8,128)}, f32[512,128]{1,0:T(8,128)}, u32[]{:S(2)}, u32[]{:S(2)}) %collective-permute-start.8) | collective-permute-done | bytes 262176 | tf_op jit(solution)/shard_map/ppermute | solution.py:14
  35.2 1.2 %fusion.3 = f32[512,128]{1,0:T(8,128)S(1)} fusion(f32[512,128]{1,0:T(8,128)} %collective-permute-done.10, f32[512,128]{1,0:T(8,128)} %collective-permute-done.9, f32[512,128]{1,0:T(8,128)} %collective-permute-done.8, f32[2048,128]{1,0:T(8,128)S(1)} %fusion), kind=kLoop, calls=%fused_computation.15 | loop fusion | flops 196608 | bytes 1310720 | tf_op jit(solution)/shard_map/add | solution.py:119
  36.4 1.6 %collective-permute-start.11 = (f32[128,128]{1,0:T(8,128)S(1)}, f32[128,128]{1,0:T(8,128)S(1)}, u32[]{:S(2)}, u32[]{:S(2)}) collective-permute-start(f32[128,128]{1,0:T(8,128)S(1)} %add.100), channel_id=1, source_target_pairs={{0,8},{4,12},{8,0},{12,4},{16,24},{20,28},{24,16},{28,20},{1,9},{5... | collective-permute-start | bytes 196616 | tf_op jit(solution)/shard_map/ppermute | solution.py:14
  38.0 3.7 %collective-permute-start.15 = (f32[128,128]{1,0:T(8,128)S(1)}, f32[128,128]{1,0:T(8,128)S(1)}, u32[]{:S(2)}, u32[]{:S(2)}) collective-permute-start(f32[128,128]{1,0:T(8,128)S(1)} %get-tuple-element.37), channel_id=1, source_target_pairs={{0,3},{1,2},{2,1},{3,0},{4,7},{5,6},{6,5},{7,4},{8,11},{9,10},{10,... | collective-permute-start | bytes 196616 | tf_op jit(solution)/shard_map/ppermute | solution.py:14
  43.1 1.0 %collective-permute-done.15 = f32[128,128]{1,0:T(8,128)S(1)} collective-permute-done((f32[128,128]{1,0:T(8,128)S(1)}, f32[128,128]{1,0:T(8,128)S(1)}, u32[]{:S(2)}, u32[]{:S(2)}) %collective-permute-start.15) | collective-permute-done | bytes 65568 | tf_op jit(solution)/shard_map/ppermute | solution.py:14
  44.2 2.7 %collective-permute-done.14 = f32[128,128]{1,0:T(8,128)S(1)} collective-permute-done((f32[128,128]{1,0:T(8,128)S(1)}, f32[128,128]{1,0:T(8,128)S(1)}, u32[]{:S(2)}, u32[]{:S(2)}) %collective-permute-start.14) | collective-permute-done | bytes 65568 | tf_op jit(solution)/shard_map/ppermute | solution.py:14
  46.9 0.9 %add_add_fusion = f32[128,128]{1,0:T(8,128)S(1)} fusion(f32[128,128]{1,0:T(8,128)S(1)} %collective-permute-done.15, f32[128,128]{1,0:T(8,128)S(1)} %collective-permute-done.14, f32[128,128]{1,0:T(8,128)S(1)} %collective-permute-done.13, f32[512,128]{1,0:T(8,128)} %copy-done.2, s32[]{:T(128)S(6)} %select_n.48), kind=kLoop, calls=%fused_computation.23 | loop fusion | flops 49152 | bytes 327684 | tf_op jit(solution)/shard_map/add | solution.py:125
  48.9 2.7 %collective-permute-start.17 = (f32[128,128]{1,0:T(8,128)S(1)}, f32[128,128]{1,0:T(8,128)S(1)}, u32[]{:S(2)}, u32[]{:S(2)}) collective-permute-start(f32[128,128]{1,0:T(8,128)S(1)} %add_add_fusion), channel_id=1, source_target_pairs={{0,2},{1,3},{2,0},{3,1},{4,6},{5,7},{6,4},{7,5},{8,10},{9,11},{10,... | collective-permute-start | bytes 196616 | tf_op jit(solution)/shard_map/ppermute | solution.py:14
  51.6 1.2 %collective-permute-start.18 = (f32[128,128]{1,0:T(8,128)S(1)}, f32[128,128]{1,0:T(8,128)S(1)}, u32[]{:S(2)}, u32[]{:S(2)}) collective-permute-start(f32[128,128]{1,0:T(8,128)S(1)} %add_add_fusion), channel_id=1, source_target_pairs={{0,3},{1,2},{2,1},{3,0},{4,7},{5,6},{6,5},{7,4},{8,11},{9,10},{10,... | collective-permute-start | bytes 196616 | tf_op jit(solution)/shard_map/ppermute | solution.py:14
  52.8 6.3 %inverse_factor.1 = f32[128,128]{1,0:T(8,128)} custom-call(f32[128,128]{1,0:T(8,128)} %add.107.gram_ref), custom_call_target="tpu_custom_call" | custom-call | flops 6000000000 | bytes 131072 | tf_op jit(solution)/shard_map/inverse_factor/pallas_call | solution.py:65
  59.3 2.1 %fusion.15 = (bf16[512,128]{1,0:T(8,128)(2,1)S(1)}, f32[512,128]{1,0:T(8,128)}) fusion(f32[512,128]{1,0:T(8,128)S(1)} %constant_dynamic-update-slice_fusion, f32[128,128]{1,0:T(8,128)} %inverse_factor.1), kind=kOutput, calls=%fused_computation.45 | convolution fusion | flops 100745216 | bytes 720896 | tf_op jit(solution)/shard_map/dot_general | solution.py:18
  61.3 1.4 %collective-permute-start.21 = (bf16[512,128]{1,0:T(8,128)(2,1)S(1)}, bf16[512,128]{1,0:T(8,128)(2,1)S(1)}, u32[]{:S(2)}, u32[]{:S(2)}) collective-permute-start(bf16[512,128]{1,0:T(8,128)(2,1)S(1)} %get-tuple-element.42), channel_id=1, source_target_pairs={{0,24},{4,28},{8,16},{12,20},{16,8},{20,12},{24,0},{28,4},{1,25},{... | collective-permute-start | bytes 393224 | tf_op jit(solution)/shard_map/ppermute | solution.py:14
  63.5 1.3 %collective-permute-start.19 = (bf16[512,128]{1,0:T(8,128)(2,1)S(1)}, bf16[512,128]{1,0:T(8,128)(2,1)S(1)}, u32[]{:S(2)}, u32[]{:S(2)}) collective-permute-start(bf16[512,128]{1,0:T(8,128)(2,1)S(1)} %get-tuple-element.42), channel_id=1, source_target_pairs={{0,8},{4,12},{8,0},{12,4},{16,24},{20,28},{24,16},{28,20},{1,9},{5... | collective-permute-start | bytes 393224 | tf_op jit(solution)/shard_map/ppermute | solution.py:14
  64.8 2.5 %collective-permute-done.21 = bf16[512,128]{1,0:T(8,128)(2,1)S(1)} collective-permute-done((bf16[512,128]{1,0:T(8,128)(2,1)S(1)}, bf16[512,128]{1,0:T(8,128)(2,1)S(1)}, u32[]{:S(2)}, u32[]{:S(2)}) %collective-permute-start.21) | collective-permute-done | bytes 131104 | tf_op jit(solution)/shard_map/ppermute | solution.py:14
  67.3 1.3 %collective-permute-done.20 = bf16[512,128]{1,0:T(8,128)(2,1)S(1)} collective-permute-done((bf16[512,128]{1,0:T(8,128)(2,1)S(1)}, bf16[512,128]{1,0:T(8,128)(2,1)S(1)}, u32[]{:S(2)}, u32[]{:S(2)}) %collective-permute-start.20) | collective-permute-done | bytes 131104 | tf_op jit(solution)/shard_map/ppermute | solution.py:14
  69.3 0.9 %multiply_reduce_fusion.1 = f32[512]{0:T(512)S(1)} fusion(bf16[512,2048]{1,0:T(8,128)(2,1)S(1)} %copy-done.1, f32[512,128]{1,0:T(8,128)S(1)} %fusion.8, bf16[512,128]{1,0:T(8,128)(2,1)S(1)} %collective-permute-done.21, bf16[512,128]{1,0:T(8,128)(2,1)S(1)} %collective-permute-done.20, bf16[512,128]{1,0:T(8,128)(2,1)S(1)} %collective-permute-done.19, ...), kind=kOutput, calls=%fused_computation.1 | convolution fusion | flops 275840512 | bytes 2885632 | tf_op jit(solution)/shard_map/dot_general | solution.py:150
  70.6 0.9 %multiply_reduce_fusion = f32[512]{0:T(512)S(1)} fusion(bf16[512,2048]{1,0:T(8,128)(2,1)S(1)} %get-tuple-element.16, bf16[2048,128]{1,0:T(8,128)(2,1)S(1)} %collective-permute-done.22, f32[512,128]{1,0:T(8,128)S(1)} %fusion.8), kind=kOutput, calls=%fused_computation | convolution fusion | flops 273743360 | bytes 2885632 | tf_op jit(solution)/shard_map/dot_general | solution.py:150
  (58 shorter events, 10.6 us)
Async XLA Ops:
  0.6 8.2 %collective-permute-start.2 = (bf16[512,128]{1,0:T(8,128)(2,1)}, bf16[512,128]{1,0:T(8,128)(2,1)S(1)}, u32[]{:S(2)}, u32[]{:S(2)}) collective-permute-start(bf16[512,128]{1,0:T(8,128)(2,1)} %param.3), channel_id=1, source_target_pairs={{0,24},{4,28},{8,16},{12,20},{16,8},{20,12},{24,0},{28,4},{1,25},{... | collective-permute-start | bytes 393224 | tf_op jit(solution)/shard_map/ppermute | solution.py:14
  4.6 6.5 %collective-permute-start.1 = (bf16[512,128]{1,0:T(8,128)(2,1)}, bf16[512,128]{1,0:T(8,128)(2,1)S(1)}, u32[]{:S(2)}, u32[]{:S(2)}) collective-permute-start(bf16[512,128]{1,0:T(8,128)(2,1)} %param.3), channel_id=1, source_target_pairs={{0,16},{4,20},{8,24},{12,28},{16,0},{20,4},{24,8},{28,12},{1,17},{... | collective-permute-start | bytes 393224 | tf_op jit(solution)/shard_map/ppermute | solution.py:14
  5.1 6.3 %collective-permute-start = (bf16[512,128]{1,0:T(8,128)(2,1)}, bf16[512,128]{1,0:T(8,128)(2,1)S(1)}, u32[]{:S(2)}, u32[]{:S(2)}) collective-permute-start(bf16[512,128]{1,0:T(8,128)(2,1)} %param.3), channel_id=1, source_target_pairs={{0,8},{4,12},{8,0},{12,4},{16,24},{20,28},{24,16},{28,20},{1,9},{5... | collective-permute-start | bytes 393224 | tf_op jit(solution)/shard_map/ppermute | solution.py:14
  7.9 3.5 %copy-start.5 = (bf16[512,128]{1,0:T(8,128)(2,1)S(1)}, bf16[512,128]{1,0:T(8,128)(2,1)}, u32[]{:S(2)}) copy-start(bf16[512,128]{1,0:T(8,128)(2,1)} %param.3) | copy-start | bytes 393220
  8.5 7.7 %copy-start = (bf16[512,2048]{1,0:T(8,128)(2,1)}, bf16[512,2048]{1,0:T(8,128)(2,1)S(1)}, u32[]{:S(2)}) copy-start(bf16[512,2048]{1,0:T(8,128)(2,1)S(1)} %get-tuple-element.14) | copy-start | bytes 6291460
  11.4 2.0 %collective-permute-start.3 = (bf16[2048,128]{1,0:T(8,128)(2,1)S(1)}, bf16[2048,128]{1,0:T(8,128)(2,1)S(1)}, u32[]{:S(2)}, u32[]{:S(2)}) collective-permute-start(bf16[2048,128]{1,0:T(8,128)(2,1)S(1)} %pad_maximum_fusion.2), channel_id=1, source_target_pairs={{0,4},{4,0},{8,12},{12,8},{16,20},{20,16},{24,28},{28,24},{1,5},{5... | collective-permute-start | bytes 1572872 | tf_op jit(solution)/shard_map/ppermute | solution.py:14
  14.6 1.3 %collective-permute-start.4 = (f32[128,128]{1,0:T(8,128)S(1)}, f32[128,128]{1,0:T(8,128)S(1)}, u32[]{:S(2)}, u32[]{:S(2)}) collective-permute-start(f32[128,128]{1,0:T(8,128)S(1)} %fusion.17), channel_id=1, source_target_pairs={{0,4},{4,0},{8,12},{12,8},{16,20},{20,16},{24,28},{28,24},{1,5},{5... | collective-permute-start | bytes 196616 | tf_op jit(solution)/shard_map/ppermute | solution.py:14
  16.0 2.7 %collective-permute-start.7 = (f32[2048,128]{1,0:T(8,128)S(1)}, f32[2048,128]{1,0:T(8,128)S(1)}, u32[]{:S(2)}, u32[]{:S(2)}) collective-permute-start(f32[2048,128]{1,0:T(8,128)S(1)} %slice_add_fusion.1), channel_id=1, source_target_pairs={{0,4},{4,0},{8,12},{12,8},{16,20},{20,16},{24,28},{28,24},{1,5},{5... | collective-permute-start | bytes 3145736 | tf_op jit(solution)/shard_map/ppermute | solution.py:14
  19.7 14.0 %collective-permute-start.10 = (f32[512,128]{1,0:T(8,128)}, f32[512,128]{1,0:T(8,128)}, u32[]{:S(2)}, u32[]{:S(2)}) collective-permute-start(f32[512,128]{1,0:T(8,128)} %get-tuple-element.34), channel_id=1, source_target_pairs={{0,16},{4,20},{8,24},{12,28},{16,0},{20,4},{24,8},{28,12},{1,17},{... | collective-permute-start | bytes 786440 | tf_op jit(solution)/shard_map/ppermute | solution.py:14
  21.2 12.5 %collective-permute-start.9 = (f32[512,128]{1,0:T(8,128)}, f32[512,128]{1,0:T(8,128)}, u32[]{:S(2)}, u32[]{:S(2)}) collective-permute-start(f32[512,128]{1,0:T(8,128)} %get-tuple-element.35), channel_id=1, source_target_pairs={{0,8},{4,12},{8,0},{12,4},{16,24},{20,28},{24,16},{28,20},{1,9},{5... | collective-permute-start | bytes 786440 | tf_op jit(solution)/shard_map/ppermute | solution.py:14
  21.9 13.3 %collective-permute-start.8 = (f32[512,128]{1,0:T(8,128)}, f32[512,128]{1,0:T(8,128)}, u32[]{:S(2)}, u32[]{:S(2)}) collective-permute-start(f32[512,128]{1,0:T(8,128)} %get-tuple-element.33), channel_id=1, source_target_pairs={{0,24},{4,28},{8,16},{12,20},{16,8},{20,12},{24,0},{28,4},{1,25},{... | collective-permute-start | bytes 786440 | tf_op jit(solution)/shard_map/ppermute | solution.py:14
  23.2 4.3 %collective-permute-start.5 = (f32[128,128]{1,0:T(8,128)S(1)}, f32[128,128]{1,0:T(8,128)S(1)}, u32[]{:S(2)}, u32[]{:S(2)}) collective-permute-start(f32[128,128]{1,0:T(8,128)S(1)} %add.97), channel_id=1, source_target_pairs={{0,1},{1,0},{2,3},{3,2},{4,5},{5,4},{6,7},{7,6},{8,9},{9,8},{10,11... | collective-permute-start | bytes 196616 | tf_op jit(solution)/shard_map/ppermute | solution.py:14
  27.5 5.3 %collective-permute-start.6 = (f32[128,128]{1,0:T(8,128)S(1)}, f32[128,128]{1,0:T(8,128)}, u32[]{:S(2)}, u32[]{:S(2)}) collective-permute-start(f32[128,128]{1,0:T(8,128)S(1)} %add.99), channel_id=1, source_target_pairs={{0,2},{1,3},{2,0},{3,1},{4,6},{5,7},{6,4},{7,5},{8,10},{9,11},{10,... | collective-permute-start | bytes 196616 | tf_op jit(solution)/shard_map/ppermute | solution.py:14
  36.4 1.6 %copy-start.2 = (f32[512,128]{1,0:T(8,128)}, f32[512,128]{1,0:T(8,128)S(1)}, u32[]{:S(2)}) copy-start(f32[512,128]{1,0:T(8,128)S(1)} %fusion.3) | copy-start | bytes 786436
  36.4 6.1 %collective-permute-start.11 = (f32[128,128]{1,0:T(8,128)S(1)}, f32[128,128]{1,0:T(8,128)S(1)}, u32[]{:S(2)}, u32[]{:S(2)}) collective-permute-start(f32[128,128]{1,0:T(8,128)S(1)} %add.100), channel_id=1, source_target_pairs={{0,8},{4,12},{8,0},{12,4},{16,24},{20,28},{24,16},{28,20},{1,9},{5... | collective-permute-start | bytes 196616 | tf_op jit(solution)/shard_map/ppermute | solution.py:14
  38.0 6.1 %collective-permute-start.15 = (f32[128,128]{1,0:T(8,128)S(1)}, f32[128,128]{1,0:T(8,128)S(1)}, u32[]{:S(2)}, u32[]{:S(2)}) collective-permute-start(f32[128,128]{1,0:T(8,128)S(1)} %get-tuple-element.37), channel_id=1, source_target_pairs={{0,3},{1,2},{2,1},{3,0},{4,7},{5,6},{6,5},{7,4},{8,11},{9,10},{10,... | collective-permute-start | bytes 196616 | tf_op jit(solution)/shard_map/ppermute | solution.py:14
  41.7 5.2 %collective-permute-start.14 = (f32[128,128]{1,0:T(8,128)S(1)}, f32[128,128]{1,0:T(8,128)S(1)}, u32[]{:S(2)}, u32[]{:S(2)}) collective-permute-start(f32[128,128]{1,0:T(8,128)S(1)} %get-tuple-element.38), channel_id=1, source_target_pairs={{0,2},{1,3},{2,0},{3,1},{4,6},{5,7},{6,4},{7,5},{8,10},{9,11},{10,... | collective-permute-start | bytes 196616 | tf_op jit(solution)/shard_map/ppermute | solution.py:14
  41.7 5.2 %collective-permute-start.13 = (f32[128,128]{1,0:T(8,128)S(1)}, f32[128,128]{1,0:T(8,128)S(1)}, u32[]{:S(2)}, u32[]{:S(2)}) collective-permute-start(f32[128,128]{1,0:T(8,128)S(1)} %get-tuple-element.36), channel_id=1, source_target_pairs={{0,1},{1,0},{2,3},{3,2},{4,5},{5,4},{6,7},{7,6},{8,9},{9,8},{10,11... | collective-permute-start | bytes 196616 | tf_op jit(solution)/shard_map/ppermute | solution.py:14
  42.5 5.3 %collective-permute-start.12 = (f32[128,128]{1,0:T(8,128)S(1)}, f32[128,128]{1,0:T(8,128)S(1)}, u32[]{:S(2)}, u32[]{:S(2)}) collective-permute-start(f32[128,128]{1,0:T(8,128)S(1)} %add.106), channel_id=1, source_target_pairs={{0,16},{4,20},{8,24},{12,28},{16,0},{20,4},{24,8},{28,12},{1,17},{... | collective-permute-start | bytes 196616 | tf_op jit(solution)/shard_map/ppermute | solution.py:14
  48.4 10.7 %collective-permute-start.16 = (f32[128,128]{1,0:T(8,128)S(1)}, f32[128,128]{1,0:T(8,128)S(1)}, u32[]{:S(2)}, u32[]{:S(2)}) collective-permute-start(f32[128,128]{1,0:T(8,128)S(1)} %add_add_fusion), channel_id=1, source_target_pairs={{0,1},{1,0},{2,3},{3,2},{4,5},{5,4},{6,7},{7,6},{8,9},{9,8},{10,11... | collective-permute-start | bytes 196616 | tf_op jit(solution)/shard_map/ppermute | solution.py:14
  48.9 10.3 %collective-permute-start.17 = (f32[128,128]{1,0:T(8,128)S(1)}, f32[128,128]{1,0:T(8,128)S(1)}, u32[]{:S(2)}, u32[]{:S(2)}) collective-permute-start(f32[128,128]{1,0:T(8,128)S(1)} %add_add_fusion), channel_id=1, source_target_pairs={{0,2},{1,3},{2,0},{3,1},{4,6},{5,7},{6,4},{7,5},{8,10},{9,11},{10,... | collective-permute-start | bytes 196616 | tf_op jit(solution)/shard_map/ppermute | solution.py:14
  51.6 7.6 %collective-permute-start.18 = (f32[128,128]{1,0:T(8,128)S(1)}, f32[128,128]{1,0:T(8,128)S(1)}, u32[]{:S(2)}, u32[]{:S(2)}) collective-permute-start(f32[128,128]{1,0:T(8,128)S(1)} %add_add_fusion), channel_id=1, source_target_pairs={{0,3},{1,2},{2,1},{3,0},{4,7},{5,6},{6,5},{7,4},{8,11},{9,10},{10,... | collective-permute-start | bytes 196616 | tf_op jit(solution)/shard_map/ppermute | solution.py:14
  59.1 9.6 %copy-start.4 = (f32[128,128]{1,0:T(8,128)S(1)}, f32[128,128]{1,0:T(8,128)}, u32[]{:S(2)}) copy-start(f32[128,128]{1,0:T(8,128)} %inverse_factor.1) | copy-start | bytes 196612
  59.1 10.2 %copy-start.1 = (bf16[512,2048]{1,0:T(8,128)(2,1)S(1)}, bf16[512,2048]{1,0:T(8,128)(2,1)}, u32[]{:S(2)}) copy-start(bf16[512,2048]{1,0:T(8,128)(2,1)} %copy-done) | copy-start | bytes 6291460
  61.3 6.0 %collective-permute-start.21 = (bf16[512,128]{1,0:T(8,128)(2,1)S(1)}, bf16[512,128]{1,0:T(8,128)(2,1)S(1)}, u32[]{:S(2)}, u32[]{:S(2)}) collective-permute-start(bf16[512,128]{1,0:T(8,128)(2,1)S(1)} %get-tuple-element.42), channel_id=1, source_target_pairs={{0,24},{4,28},{8,16},{12,20},{16,8},{20,12},{24,0},{28,4},{1,25},{... | collective-permute-start | bytes 393224 | tf_op jit(solution)/shard_map/ppermute | solution.py:14
  62.7 5.9 %collective-permute-start.20 = (bf16[512,128]{1,0:T(8,128)(2,1)S(1)}, bf16[512,128]{1,0:T(8,128)(2,1)S(1)}, u32[]{:S(2)}, u32[]{:S(2)}) collective-permute-start(bf16[512,128]{1,0:T(8,128)(2,1)S(1)} %get-tuple-element.42), channel_id=1, source_target_pairs={{0,16},{4,20},{8,24},{12,28},{16,0},{20,4},{24,8},{28,12},{1,17},{... | collective-permute-start | bytes 393224 | tf_op jit(solution)/shard_map/ppermute | solution.py:14
  63.5 5.1 %collective-permute-start.19 = (bf16[512,128]{1,0:T(8,128)(2,1)S(1)}, bf16[512,128]{1,0:T(8,128)(2,1)S(1)}, u32[]{:S(2)}, u32[]{:S(2)}) collective-permute-start(bf16[512,128]{1,0:T(8,128)(2,1)S(1)} %get-tuple-element.42), channel_id=1, source_target_pairs={{0,8},{4,12},{8,0},{12,4},{16,24},{20,28},{24,16},{28,20},{1,9},{5... | collective-permute-start | bytes 393224 | tf_op jit(solution)/shard_map/ppermute | solution.py:14
  68.6 2.0 %collective-permute-start.22 = (bf16[2048,128]{1,0:T(8,128)(2,1)S(1)}, bf16[2048,128]{1,0:T(8,128)(2,1)S(1)}, u32[]{:S(2)}, u32[]{:S(2)}) collective-permute-start(bf16[2048,128]{1,0:T(8,128)(2,1)S(1)} %pad_maximum_fusion.3), channel_id=1, source_target_pairs={{0,4},{4,0},{8,12},{12,8},{16,20},{20,16},{24,28},{28,24},{1,5},{5... | collective-permute-start | bytes 1572872 | tf_op jit(solution)/shard_map/ppermute | solution.py:14
  69.3 1.3 %copy-start.3 = (f32[512,128]{1,0:T(8,128)}, f32[512,128]{1,0:T(8,128)S(1)}, u32[]{:S(2)}) copy-start(f32[512,128]{1,0:T(8,128)S(1)} %fusion.8) | copy-start | bytes 786436

commit v4 on v3

--- a/solution.py
+++ b/solution.py
@@ -27,31 +27,63 @@
     return high, middle, rest - middle
 
 
-def factor_kernel(block, gram_ref, out_ref, work, lines):
-    n = gram_ref.shape[0]
-    work[:, :n] = gram_ref[...]
+def twice(value):
+    return jnp.concatenate([value, value], axis=1)
+
+
+def eliminate(line, corner, store, side=None, rest=None):
+    for j in range(8):
+        scale = lax.rsqrt(corner[j, j])
+        line[j] = line[j] * twice(scale)
+        store(j, line[j][:1])
+        for i in range(j + 1, 8):
+            corner[i, j] = corner[i, j] * scale
+        if side is not None:
+            side[j] = side[j] * scale
+        for i in range(j + 1, 8):
+            for m in range(j + 1, i + 1):
+                corner[i, m] = corner[i, m] - corner[i, j] * corner[m, j]
+            line[i] = line[i] - twice(corner[i, j]) * line[j]
+            if side is not None:
+                side[i] = side[i] - corner[i, j] * side[j]
+        if side is not None:
+            rest = rest - twice(side[j]) * line[j]
+    return rest
+
+
+def factor_kernel(gram_ref, other_ref, out_ref, work, lines):
+    n = out_ref.shape[0]
+    work[:, :n] = gram_ref[...] + other_ref[...]
     down = lax.broadcasted_iota(jnp.int32, (n, n), 0)
     across = lax.broadcasted_iota(jnp.int32, (n, n), 1)
     work[:, n:] = jnp.where(down == across, 1.0, 0.0)
-    for top in range(0, n, block):
-        line = [work[top + i : top + i + 1, :] for i in range(block)]
-        corner = {}
-        for i in range(block):
-            for j in range(i + 1):
-                corner[i, j] = jnp.broadcast_to(line[i][:, top + j : top + j + 1], (1, n))
-        for j in range(block):
-            scale = lax.rsqrt(corner[j, j])
-            line[j] = line[j] * jnp.concatenate([scale, scale], axis=1)
-            lines[j : j + 1, :] = line[j]
-            for i in range(j + 1, block):
-                corner[i, j] = corner[i, j] * scale
-            for i in range(j + 1, block):
-                for m in range(j + 1, i + 1):
-                    corner[i, m] = corner[i, m] - corner[i, j] * corner[m, j]
-                line[i] = line[i] - jnp.concatenate([corner[i, j]] * 2, axis=1) * line[j]
+
+    def spread(ref, top):
+        return [jnp.broadcast_to(ref[top + i : top + i + 1, :], (8, 2 * n)) for i in range(8)]
+
+    def corner_of(line, left):
+        return {
+            (i, j): jnp.broadcast_to(line[i][:, left + j : left + j + 1], (8, n))
+            for i in range(8)
+            for j in range(i + 1)
+        }
+
+    def store_at(top):
+        def store(j, value):
+            lines[top + j : top + j + 1, :] = value
+
+        return store
+
+    for top in range(0, n, 16):
+        line = spread(work, top)
+        below = work[top + 8 : top + 16, :]
+        side = [jnp.broadcast_to(below[:, top + j : top + j + 1], (8, n)) for j in range(8)]
+        lines[8:, :] = eliminate(line, corner_of(line, top), store_at(0), side, below)
+        line = spread(lines, 8)
+        eliminate(line, corner_of(line, top + 8), store_at(8))
         done = lines[...]
-        out_ref[top : top + block, :] = done[:, n:]
-        if top + block < n:
+        out_ref[top : top + 16, :] = done[:, n:]
+        if top + 16 < n:
             high, middle, small = terms(done)
             left = jnp.concatenate([high, high, middle, high, small, middle])[:, :n].astype(jnp.bfloat16)
             right = jnp.concatenate([high, middle, high, small, high, middle]).astype(jnp.bfloat16)
@@ -60,15 +92,16 @@
             )
 
 
-def inverse_factor(gram, block=16):
-    n = gram.shape[0]
+def inverse_factor(*grams):
+    n = grams[0].shape[0]
     return pl.pallas_call(
-        functools.partial(factor_kernel, block),
+        factor_kernel,
         out_shape=jax.ShapeDtypeStruct((n, n), jnp.float32),
-        scratch_shapes=[pltpu.VMEM((n, 2 * n), jnp.float32), pltpu.VMEM((block, 2 * n), jnp.float32)],
+        out_specs=pl.BlockSpec(memory_space=pltpu.VMEM),
+        scratch_shapes=[pltpu.VMEM((n, 2 * n), jnp.float32), pltpu.VMEM((16, 2 * n), jnp.float32)],
         cost_estimate=pl.CostEstimate(flops=6_000_000_000, bytes_accessed=131072, transcendentals=128),
         name="inverse_factor",
-    )(gram)
+    )(*grams)
 
 
 def local(samples, sketch_matrix):
@@ -119,13 +152,13 @@
     own = pieces[0] + flipped(pieces[3], "inner", 6)+ flipped(pieces[1], "inner", 2)+ flipped(pieces[2], "inner", 4)
     gram, own = lax.optimization_barrier((gram, own))
     gram = gram + flipped(gram, "inner", 2)
-    gram = gram + flipped(gram, "inner", 4)
+    last = flipped(gram, "inner", 4)
     share = lax.dynamic_slice_in_dim(own, mine * part, part, 0)
     for mask in range(1, outer):
         share = share + flipped(
             lax.dynamic_slice_in_dim(own, (mine ^ mask) * part, part, 0), "outer", mask
         )
-    gram, share = lax.optimization_barrier((gram, share))
+    gram, last, share = lax.optimization_barrier((gram, last, share))
 
     summed = jnp.zeros((piece, rank), jnp.float32)
     summed = lax.dynamic_update_slice_in_dim(summed, share, mine * part, 0)
@@ -134,10 +167,11 @@
             summed, flipped(share, "outer", mask), (mine ^ mask) * part, 0
         )
 
-    inverse = inverse_factor(gram)
+    inverse = inverse_factor(gram, last)
     basis = exact_dot(sketch, inverse * math.sqrt(total_rows), ((1,), (1,)))
     basis_low = basis.astype(jnp.bfloat16)
     projection = exact_dot(summed, inverse * (math.sqrt(width) / math.sqrt(total_rows)), ((1,), (1,)))
+    projection = lax.optimization_barrier(projection)
     projection_low = projection.astype(jnp.bfloat16)
 
     got = {0: projection_low}

time: 72.4 us -> 70.3 us (0.971)
  Pallas kernels: 6.31 us -> 5.38 us
    pallas_call x1, Pallas kernels: 6.31 us -> 5.38 us  [inverse_factor(): pl.pallas_call(factor_kernel, out_shape=jax.ShapeDtypeStruct((n, n), jnp....]
  transfers between devices with their start and end apart: 23 -> 23, of which waited for: 14 -> 14; matrix products, arithmetic and copies ran while one was open for 13% -> 13% of each run, Pallas kernels for 9% -> 8%
where the time goes in v4:
time: 70.3 us; the launch traced here: 70 us
  starting transfers between devices  27.6 us (39%)
  waiting for transfers between devices  20.6 us (29%)
  matrix products  7.38 us (10%)
  Pallas kernels  5.38 us (8%)
  other arithmetic  4.46 us (6%)
  local copies, waits for them, and re-layouts  3.66 us (5%)
  between operations  0.95 us (1%)
    ppermute x23, starting transfers between devices, flipped(): lax.ppermute(block, axis, [(low, low ^ mask) for low in range(count)])  27.6 us
    ppermute x23, waiting for transfers between devices, flipped(): lax.ppermute(block, axis, [(low, low ^ mask) for low in range(count)])  20.6 us
    pallas_call x1, Pallas kernels, inverse_factor(): pl.pallas_call(factor_kernel, out_shape=jax.ShapeDtypeStruct((n, n), jnp....  5.38 us
    dynamic_slice x1, local copies, waits for them, and re-layouts, columns(): lax.dynamic_slice_in_dim(samples, (me ^ mask) * piece, piece, 1)  2.63 us
    dot_general x3, matrix products, exact_dot(): lax.dot_general(a, b, (contract, ((), ())), precision=lax.Precision.HIGHE...  2.31 us
    dot_general x2, matrix products, errors(): lax.dot_general(basis_low, factor, (((1,), (1,)), ((), ())), preferred_el...  1.88 us
    dot_general x2, matrix products, products(): lax.dot_general(side, both, (((0,), (0,)), ((), ())), preferred_element_t...  1.52 us
  transfers between devices with their start and end apart: 23, of which 14 were waited for; matrix products, arithmetic and copies ran while one was open for 13% of the time, Pallas kernels for 8%

profile of v4, /device:TPU:0, one launch (start us, length us, event | category | flops | bytes accessed | tf_op | source)
XLA Modules:
  0.0 70.0 jit_solution(7460225245319430993)
XLA Ops:
  0.6 4.0 %collective-permute-start.2 = (bf16[512,128]{1,0:T(8,128)(2,1)}, bf16[512,128]{1,0:T(8,128)(2,1)S(1)}, u32[]{:S(2)}, u32[]{:S(2)}) collective-permute-start(bf16[512,128]{1,0:T(8,128)(2,1)} %param.3), channel_id=1, source_target_pairs={{0,24},{4,28},{8,16},{12,20},{16,8},{20,12},{24,0},{28,4},{1,25},{... | collective-permute-start | bytes 393224 | tf_op jit(solution)/shard_map/ppermute | solution.py:14
  5.2 2.6 %constant_dynamic-slice_fusion.6 = (bf16[512,512]{1,0:T(8,128)(2,1)S(1)}, bf16[512,512]{1,0:T(8,128)(2,1)S(1)}, bf16[512,512]{1,0:T(8,128)(2,1)S(1)}, bf16[512,5...) fusion(bf16[512,4096]{1,0:T(8,128)(2,1)} %param.2, ...), kind=kLoop, calls=%fused_computation.36 | loop fusion | bytes 8388640 | tf_op jit(solution)/shard_map/dynamic_slice | solution.py:126
  8.8 2.3 %collective-permute-done.1 = bf16[512,128]{1,0:T(8,128)(2,1)S(1)} collective-permute-done((bf16[512,128]{1,0:T(8,128)(2,1)}, bf16[512,128]{1,0:T(8,128)(2,1)S(1)}, u32[]{:S(2)}, u32[]{:S(2)}) %collective-permute-start.1) | collective-permute-done | bytes 131104 | tf_op jit(solution)/shard_map/ppermute | solution.py:14
  11.5 0.8 %fusion.15 = f32[512,128]{0,1:T(8,128)S(1)} fusion(bf16[512,2048]{1,0:T(8,128)(2,1)S(1)} %get-tuple-element.15, bf16[2048,128]{1,0:T(8,128)(2,1)S(1)} %pad_maximum_fusion.2), kind=kOutput, calls=%fused_computation.45 | convolution fusion | flops 268435456 | bytes 2883584 | tf_op jit(solution)/shard_map/dot_general | solution.py:133
  12.3 1.1 %collective-permute-done.3 = bf16[2048,128]{1,0:T(8,128)(2,1)S(1)} collective-permute-done((bf16[2048,128]{1,0:T(8,128)(2,1)S(1)}, bf16[2048,128]{1,0:T(8,128)(2,1)S(1)}, u32[]{:S(2)}, u32[]{:S(2)}) %collective-permute-start.3) | collective-permute-done | bytes 524320 | tf_op jit(solution)/shard_map/ppermute | solution.py:14
  13.4 0.8 %reduce-precision_convert_fusion = (bf16[512,128]{0,1:T(8,128)(2,1)S(1)}, bf16[512,128]{0,1:T(8,128)(2,1)S(1)}, f32[512,128]{0,1:T(8,128)S(1)}) fusion(f32[512,128]{0,1:T(8,128)S(1)} %fusion.15, bf16[512,2048]{1,0:T(8,128)(2,1)S(1)} %get-tuple-element.17, bf16[2048,128]{1,0:T(8,128)(2,1)S(1)} %collective-permute-done.3), kind=kOutput, calls=%fused_computation.11 | convolution fusion | flops 268763136 | bytes 3407872 | tf_op jit(solution)/shard_map/dot_general | solution.py:134
  17.0 1.7 %collective-permute-done.7 = f32[2048,128]{1,0:T(8,128)S(1)} collective-permute-done((f32[2048,128]{1,0:T(8,128)S(1)}, f32[2048,128]{1,0:T(8,128)S(1)}, u32[]{:S(2)}, u32[]{:S(2)}) %collective-permute-start.7) | collective-permute-done | bytes 1048608 | tf_op jit(solution)/shard_map/ppermute | solution.py:14
  18.8 0.9 %fusion.14 = (f32[512,128]{1,0:T(8,128)}, f32[512,128]{1,0:T(8,128)}, f32[512,128]{1,0:T(8,128)}) fusion(f32[2048,128]{1,0:T(8,128)S(1)} %fusion), kind=kLoop, calls=%fused_computation.44 | loop fusion | bytes 1572864 | tf_op jit(solution)/shard_map/slice | solution.py:152
  19.7 1.5 %collective-permute-start.10 = (f32[512,128]{1,0:T(8,128)}, f32[512,128]{1,0:T(8,128)}, u32[]{:S(2)}, u32[]{:S(2)}) collective-permute-start(f32[512,128]{1,0:T(8,128)} %get-tuple-element.36), channel_id=1, source_target_pairs={{0,16},{4,20},{8,24},{12,28},{16,0},{20,4},{24,8},{28,12},{1,17},{... | collective-permute-start | bytes 786440 | tf_op jit(solution)/shard_map/ppermute | solution.py:14
  21.9 1.3 %collective-permute-start.8 = (f32[512,128]{1,0:T(8,128)}, f32[512,128]{1,0:T(8,128)}, u32[]{:S(2)}, u32[]{:S(2)}) collective-permute-start(f32[512,128]{1,0:T(8,128)} %get-tuple-element.35), channel_id=1, source_target_pairs={{0,24},{4,28},{8,16},{12,20},{16,8},{20,12},{24,0},{28,4},{1,25},{... | collective-permute-start | bytes 786440 | tf_op jit(solution)/shard_map/ppermute | solution.py:14
  23.2 1.6 %collective-permute-start.5 = (f32[128,128]{1,0:T(8,128)S(1)}, f32[128,128]{1,0:T(8,128)S(1)}, u32[]{:S(2)}, u32[]{:S(2)}) collective-permute-start(f32[128,128]{1,0:T(8,128)S(1)} %add.94), channel_id=1, source_target_pairs={{0,1},{1,0},{2,3},{3,2},{4,5},{5,4},{6,7},{7,6},{8,9},{9,8},{10,11... | collective-permute-start | bytes 196616 | tf_op jit(solution)/shard_map/ppermute | solution.py:14
  24.8 2.7 %collective-permute-done.5 = f32[128,128]{1,0:T(8,128)S(1)} collective-permute-done((f32[128,128]{1,0:T(8,128)S(1)}, f32[128,128]{1,0:T(8,128)S(1)}, u32[]{:S(2)}, u32[]{:S(2)}) %collective-permute-start.5) | collective-permute-done | bytes 65568 | tf_op jit(solution)/shard_map/ppermute | solution.py:14
  27.5 2.7 %collective-permute-start.6 = (f32[128,128]{1,0:T(8,128)S(1)}, f32[128,128]{1,0:T(8,128)}, u32[]{:S(2)}, u32[]{:S(2)}) collective-permute-start(f32[128,128]{1,0:T(8,128)S(1)} %add.96), channel_id=1, source_target_pairs={{0,2},{1,3},{2,0},{3,1},{4,6},{5,7},{6,4},{7,5},{8,10},{9,11},{10,... | collective-permute-start | bytes 196616 | tf_op jit(solution)/shard_map/ppermute | solution.py:14
  30.2 2.7 %collective-permute-done.6 = f32[128,128]{1,0:T(8,128)} collective-permute-done((f32[128,128]{1,0:T(8,128)S(1)}, f32[128,128]{1,0:T(8,128)}, u32[]{:S(2)}, u32[]{:S(2)}) %collective-permute-start.6) | collective-permute-done | bytes 65568 | tf_op jit(solution)/shard_map/ppermute | solution.py:14
  32.8 0.8 %add.97 = f32[128,128]{1,0:T(8,128)S(1)} add(f32[128,128]{1,0:T(8,128)S(1)} %add.96, f32[128,128]{1,0:T(8,128)} %collective-permute-done.6) | non-fusion elementwise | flops 16384 | bytes 196608 | tf_op jit(solution)/shard_map/add | solution.py:151
  33.7 1.5 %collective-permute-done.8 = f32[512,128]{1,0:T(8,128)} collective-permute-done((f32[512,128]{1,0:T(8,128)}, f32[512,128]{1,0:T(8,128)}, u32[]{:S(2)}, u32[]{:S(2)}) %collective-permute-start.8) | collective-permute-done | bytes 262176 | tf_op jit(solution)/shard_map/ppermute | solution.py:14
  35.2 1.2 %fusion.3 = f32[512,128]{1,0:T(8,128)S(1)} fusion(f32[512,128]{1,0:T(8,128)} %collective-permute-done.10, f32[512,128]{1,0:T(8,128)} %collective-permute-done.9, f32[512,128]{1,0:T(8,128)} %collective-permute-done.8, f32[2048,128]{1,0:T(8,128)S(1)} %fusion), kind=kLoop, calls=%fused_computation.15 | loop fusion | flops 196608 | bytes 1310720 | tf_op jit(solution)/shard_map/add | solution.py:152
  36.4 1.6 %collective-permute-start.11 = (f32[128,128]{1,0:T(8,128)S(1)}, f32[128,128]{1,0:T(8,128)S(1)}, u32[]{:S(2)}, u32[]{:S(2)}) collective-permute-start(f32[128,128]{1,0:T(8,128)S(1)} %add.97), channel_id=1, source_target_pairs={{0,8},{4,12},{8,0},{12,4},{16,24},{20,28},{24,16},{28,20},{1,9},{5... | collective-permute-start | bytes 196616 | tf_op jit(solution)/shard_map/ppermute | solution.py:14
  38.0 3.7 %collective-permute-start.15 = (f32[128,128]{1,0:T(8,128)S(1)}, f32[128,128]{1,0:T(8,128)S(1)}, u32[]{:S(2)}, u32[]{:S(2)}) collective-permute-start(f32[128,128]{1,0:T(8,128)S(1)} %get-tuple-element.39), channel_id=1, source_target_pairs={{0,3},{1,2},{2,1},{3,0},{4,7},{5,6},{6,5},{7,4},{8,11},{9,10},{10,... | collective-permute-start | bytes 196616 | tf_op jit(solution)/shard_map/ppermute | solution.py:14
  43.2 1.0 %collective-permute-done.15 = f32[128,128]{1,0:T(8,128)S(1)} collective-permute-done((f32[128,128]{1,0:T(8,128)S(1)}, f32[128,128]{1,0:T(8,128)S(1)}, u32[]{:S(2)}, u32[]{:S(2)}) %collective-permute-start.15) | collective-permute-done | bytes 65568 | tf_op jit(solution)/shard_map/ppermute | solution.py:14
  44.2 2.7 %collective-permute-done.14 = f32[128,128]{1,0:T(8,128)S(1)} collective-permute-done((f32[128,128]{1,0:T(8,128)S(1)}, f32[128,128]{1,0:T(8,128)S(1)}, u32[]{:S(2)}, u32[]{:S(2)}) %collective-permute-start.14) | collective-permute-done | bytes 65568 | tf_op jit(solution)/shard_map/ppermute | solution.py:14
  46.9 0.9 %add_add_fusion = f32[128,128]{1,0:T(8,128)S(1)} fusion(f32[128,128]{1,0:T(8,128)S(1)} %collective-permute-done.15, f32[128,128]{1,0:T(8,128)S(1)} %collective-permute-done.14, f32[128,128]{1,0:T(8,128)S(1)} %collective-permute-done.13, f32[512,128]{1,0:T(8,128)} %copy-done.2, s32[]{:T(128)S(6)} %select_n.48), kind=kLoop, calls=%fused_computation.23 | loop fusion | flops 49152 | bytes 327684 | tf_op jit(solution)/shard_map/add | solution.py:158
  48.3 2.7 %collective-permute-start.17 = (f32[128,128]{1,0:T(8,128)S(1)}, f32[128,128]{1,0:T(8,128)S(1)}, u32[]{:S(2)}, u32[]{:S(2)}) collective-permute-start(f32[128,128]{1,0:T(8,128)S(1)} %add_add_fusion), channel_id=1, source_target_pairs={{0,2},{1,3},{2,0},{3,1},{4,6},{5,7},{6,4},{7,5},{8,10},{9,11},{10,... | collective-permute-start | bytes 196616 | tf_op jit(solution)/shard_map/ppermute | solution.py:14
  51.0 1.3 %collective-permute-start.18 = (f32[128,128]{1,0:T(8,128)S(1)}, f32[128,128]{1,0:T(8,128)S(1)}, u32[]{:S(2)}, u32[]{:S(2)}) collective-permute-start(f32[128,128]{1,0:T(8,128)S(1)} %add_add_fusion), channel_id=1, source_target_pairs={{0,3},{1,2},{2,1},{3,0},{4,7},{5,6},{6,5},{7,4},{8,11},{9,10},{10,... | collective-permute-start | bytes 196616 | tf_op jit(solution)/shard_map/ppermute | solution.py:14
  52.3 5.4 %inverse_factor.1 = f32[128,128]{1,0:T(8,128)} custom-call(f32[128,128]{1,0:T(8,128)} %copy-done.7, f32[128,128]{1,0:T(8,128)} %copy-done.8), custom_call_target="tpu_custom_call" | custom-call | flops 6000000000 | bytes 131072 | tf_op jit(solution)/shard_map/inverse_factor/pallas_call | solution.py:97
  57.8 1.3 %fusion.6 = f32[512,128]{1,0:T(8,128)S(1)} fusion(f32[512,128]{1,0:T(8,128)S(1)} %constant_dynamic-update-slice_fusion, f32[128,128]{1,0:T(8,128)} %inverse_factor.1), kind=kOutput, calls=%fused_computation.19 | convolution fusion | flops 100679680 | bytes 589824 | tf_op jit(solution)/shard_map/dot_general | solution.py:18
  59.2 1.5 %collective-permute-start.21 = (bf16[512,128]{1,0:T(8,128)(2,1)S(1)}, bf16[512,128]{1,0:T(8,128)(2,1)S(1)}, u32[]{:S(2)}, u32[]{:S(2)}) collective-permute-start(bf16[512,128]{1,0:T(8,128)(2,1)S(1)} %convert_element_type.22), channel_id=1, source_target_pairs={{0,24},{4,28},{8,16},{12,20},{16,8},{20,12},{24,0},{28,4},{1,25},{... | collective-permute-start | bytes 393224 | tf_op jit(solution)/shard_map/ppermute | solution.py:14
  61.4 1.3 %collective-permute-start.19 = (bf16[512,128]{1,0:T(8,128)(2,1)S(1)}, bf16[512,128]{1,0:T(8,128)(2,1)S(1)}, u32[]{:S(2)}, u32[]{:S(2)}) collective-permute-start(bf16[512,128]{1,0:T(8,128)(2,1)S(1)} %convert_element_type.22), channel_id=1, source_target_pairs={{0,8},{4,12},{8,0},{12,4},{16,24},{20,28},{24,16},{28,20},{1,9},{5... | collective-permute-start | bytes 393224 | tf_op jit(solution)/shard_map/ppermute | solution.py:14
  62.7 2.5 %collective-permute-done.21 = bf16[512,128]{1,0:T(8,128)(2,1)S(1)} collective-permute-done((bf16[512,128]{1,0:T(8,128)(2,1)S(1)}, bf16[512,128]{1,0:T(8,128)(2,1)S(1)}, u32[]{:S(2)}, u32[]{:S(2)}) %collective-permute-start.21) | collective-permute-done | bytes 131104 | tf_op jit(solution)/shard_map/ppermute | solution.py:14
  65.2 1.3 %collective-permute-done.20 = bf16[512,128]{1,0:T(8,128)(2,1)S(1)} collective-permute-done((bf16[512,128]{1,0:T(8,128)(2,1)S(1)}, bf16[512,128]{1,0:T(8,128)(2,1)S(1)}, u32[]{:S(2)}, u32[]{:S(2)}) %collective-permute-start.20) | collective-permute-done | bytes 131104 | tf_op jit(solution)/shard_map/ppermute | solution.py:14
  67.2 0.9 %multiply_reduce_fusion.1 = f32[512]{0:T(512)S(1)} fusion(bf16[512,2048]{1,0:T(8,128)(2,1)S(1)} %copy-done.1, f32[512,128]{1,0:T(8,128)S(1)} %fusion.8, bf16[512,128]{1,0:T(8,128)(2,1)S(1)} %collective-permute-done.21, bf16[512,128]{1,0:T(8,128)(2,1)S(1)} %collective-permute-done.20, bf16[512,128]{1,0:T(8,128)(2,1)S(1)} %collective-permute-done.19, ...), kind=kOutput, calls=%fused_computation.1 | convolution fusion | flops 275840512 | bytes 2885632 | tf_op jit(solution)/shard_map/dot_general | solution.py:184
  68.5 0.9 %multiply_reduce_fusion = f32[512]{0:T(512)S(1)} fusion(bf16[512,2048]{1,0:T(8,128)(2,1)S(1)} %get-tuple-element.17, bf16[2048,128]{1,0:T(8,128)(2,1)S(1)} %collective-permute-done.22, f32[512,128]{1,0:T(8,128)S(1)} %fusion.8), kind=kOutput, calls=%fused_computation | convolution fusion | flops 273743360 | bytes 2885632 | tf_op jit(solution)/shard_map/dot_general | solution.py:184
  (64 shorter events, 10.0 us)
Async XLA Ops:
  0.6 8.2 %collective-permute-start.2 = (bf16[512,128]{1,0:T(8,128)(2,1)}, bf16[512,128]{1,0:T(8,128)(2,1)S(1)}, u32[]{:S(2)}, u32[]{:S(2)}) collective-permute-start(bf16[512,128]{1,0:T(8,128)(2,1)} %param.3), channel_id=1, source_target_pairs={{0,24},{4,28},{8,16},{12,20},{16,8},{20,12},{24,0},{28,4},{1,25},{... | collective-permute-start | bytes 393224 | tf_op jit(solution)/shard_map/ppermute | solution.py:14
  4.6 6.5 %collective-permute-start.1 = (bf16[512,128]{1,0:T(8,128)(2,1)}, bf16[512,128]{1,0:T(8,128)(2,1)S(1)}, u32[]{:S(2)}, u32[]{:S(2)}) collective-permute-start(bf16[512,128]{1,0:T(8,128)(2,1)} %param.3), channel_id=1, source_target_pairs={{0,16},{4,20},{8,24},{12,28},{16,0},{20,4},{24,8},{28,12},{1,17},{... | collective-permute-start | bytes 393224 | tf_op jit(solution)/shard_map/ppermute | solution.py:14
  5.1 6.3 %collective-permute-start = (bf16[512,128]{1,0:T(8,128)(2,1)}, bf16[512,128]{1,0:T(8,128)(2,1)S(1)}, u32[]{:S(2)}, u32[]{:S(2)}) collective-permute-start(bf16[512,128]{1,0:T(8,128)(2,1)} %param.3), channel_id=1, source_target_pairs={{0,8},{4,12},{8,0},{12,4},{16,24},{20,28},{24,16},{28,20},{1,9},{5... | collective-permute-start | bytes 393224 | tf_op jit(solution)/shard_map/ppermute | solution.py:14
  7.9 3.5 %copy-start.6 = (bf16[512,128]{1,0:T(8,128)(2,1)S(1)}, bf16[512,128]{1,0:T(8,128)(2,1)}, u32[]{:S(2)}) copy-start(bf16[512,128]{1,0:T(8,128)(2,1)} %param.3) | copy-start | bytes 393220
  8.5 7.7 %copy-start = (bf16[512,2048]{1,0:T(8,128)(2,1)}, bf16[512,2048]{1,0:T(8,128)(2,1)S(1)}, u32[]{:S(2)}) copy-start(bf16[512,2048]{1,0:T(8,128)(2,1)S(1)} %get-tuple-element.15) | copy-start | bytes 6291460
  11.4 2.0 %collective-permute-start.3 = (bf16[2048,128]{1,0:T(8,128)(2,1)S(1)}, bf16[2048,128]{1,0:T(8,128)(2,1)S(1)}, u32[]{:S(2)}, u32[]{:S(2)}) collective-permute-start(bf16[2048,128]{1,0:T(8,128)(2,1)S(1)} %pad_maximum_fusion.2), channel_id=1, source_target_pairs={{0,4},{4,0},{8,12},{12,8},{16,20},{20,16},{24,28},{28,24},{1,5},{5... | collective-permute-start | bytes 1572872 | tf_op jit(solution)/shard_map/ppermute | solution.py:14
  14.6 1.3 %collective-permute-start.4 = (f32[128,128]{1,0:T(8,128)S(1)}, f32[128,128]{1,0:T(8,128)S(1)}, u32[]{:S(2)}, u32[]{:S(2)}) collective-permute-start(f32[128,128]{1,0:T(8,128)S(1)} %fusion.16), channel_id=1, source_target_pairs={{0,4},{4,0},{8,12},{12,8},{16,20},{20,16},{24,28},{28,24},{1,5},{5... | collective-permute-start | bytes 196616 | tf_op jit(solution)/shard_map/ppermute | solution.py:14
  16.0 2.7 %collective-permute-start.7 = (f32[2048,128]{1,0:T(8,128)S(1)}, f32[2048,128]{1,0:T(8,128)S(1)}, u32[]{:S(2)}, u32[]{:S(2)}) collective-permute-start(f32[2048,128]{1,0:T(8,128)S(1)} %slice_add_fusion.1), channel_id=1, source_target_pairs={{0,4},{4,0},{8,12},{12,8},{16,20},{20,16},{24,28},{28,24},{1,5},{5... | collective-permute-start | bytes 3145736 | tf_op jit(solution)/shard_map/ppermute | solution.py:14
  19.7 14.0 %collective-permute-start.10 = (f32[512,128]{1,0:T(8,128)}, f32[512,128]{1,0:T(8,128)}, u32[]{:S(2)}, u32[]{:S(2)}) collective-permute-start(f32[512,128]{1,0:T(8,128)} %get-tuple-element.36), channel_id=1, source_target_pairs={{0,16},{4,20},{8,24},{12,28},{16,0},{20,4},{24,8},{28,12},{1,17},{... | collective-permute-start | bytes 786440 | tf_op jit(solution)/shard_map/ppermute | solution.py:14
  21.2 12.5 %collective-permute-start.9 = (f32[512,128]{1,0:T(8,128)}, f32[512,128]{1,0:T(8,128)}, u32[]{:S(2)}, u32[]{:S(2)}) collective-permute-start(f32[512,128]{1,0:T(8,128)} %get-tuple-element.37), channel_id=1, source_target_pairs={{0,8},{4,12},{8,0},{12,4},{16,24},{20,28},{24,16},{28,20},{1,9},{5... | collective-permute-start | bytes 786440 | tf_op jit(solution)/shard_map/ppermute | solution.py:14
  21.9 13.3 %collective-permute-start.8 = (f32[512,128]{1,0:T(8,128)}, f32[512,128]{1,0:T(8,128)}, u32[]{:S(2)}, u32[]{:S(2)}) collective-permute-start(f32[512,128]{1,0:T(8,128)} %get-tuple-element.35), channel_id=1, source_target_pairs={{0,24},{4,28},{8,16},{12,20},{16,8},{20,12},{24,0},{28,4},{1,25},{... | collective-permute-start | bytes 786440 | tf_op jit(solution)/shard_map/ppermute | solution.py:14
  23.2 4.3 %collective-permute-start.5 = (f32[128,128]{1,0:T(8,128)S(1)}, f32[128,128]{1,0:T(8,128)S(1)}, u32[]{:S(2)}, u32[]{:S(2)}) collective-permute-start(f32[128,128]{1,0:T(8,128)S(1)} %add.94), channel_id=1, source_target_pairs={{0,1},{1,0},{2,3},{3,2},{4,5},{5,4},{6,7},{7,6},{8,9},{9,8},{10,11... | collective-permute-start | bytes 196616 | tf_op jit(solution)/shard_map/ppermute | solution.py:14
  27.5 5.3 %collective-permute-start.6 = (f32[128,128]{1,0:T(8,128)S(1)}, f32[128,128]{1,0:T(8,128)}, u32[]{:S(2)}, u32[]{:S(2)}) collective-permute-start(f32[128,128]{1,0:T(8,128)S(1)} %add.96), channel_id=1, source_target_pairs={{0,2},{1,3},{2,0},{3,1},{4,6},{5,7},{6,4},{7,5},{8,10},{9,11},{10,... | collective-permute-start | bytes 196616 | tf_op jit(solution)/shard_map/ppermute | solution.py:14
  36.4 1.6 %copy-start.2 = (f32[512,128]{1,0:T(8,128)}, f32[512,128]{1,0:T(8,128)S(1)}, u32[]{:S(2)}) copy-start(f32[512,128]{1,0:T(8,128)S(1)} %fusion.3) | copy-start | bytes 786436
  36.4 6.1 %collective-permute-start.11 = (f32[128,128]{1,0:T(8,128)S(1)}, f32[128,128]{1,0:T(8,128)S(1)}, u32[]{:S(2)}, u32[]{:S(2)}) collective-permute-start(f32[128,128]{1,0:T(8,128)S(1)} %add.97), channel_id=1, source_target_pairs={{0,8},{4,12},{8,0},{12,4},{16,24},{20,28},{24,16},{28,20},{1,9},{5... | collective-permute-start | bytes 196616 | tf_op jit(solution)/shard_map/ppermute | solution.py:14
  38.0 6.1 %collective-permute-start.15 = (f32[128,128]{1,0:T(8,128)S(1)}, f32[128,128]{1,0:T(8,128)S(1)}, u32[]{:S(2)}, u32[]{:S(2)}) collective-permute-start(f32[128,128]{1,0:T(8,128)S(1)} %get-tuple-element.39), channel_id=1, source_target_pairs={{0,3},{1,2},{2,1},{3,0},{4,7},{5,6},{6,5},{7,4},{8,11},{9,10},{10,... | collective-permute-start | bytes 196616 | tf_op jit(solution)/shard_map/ppermute | solution.py:14
  41.7 5.2 %collective-permute-start.14 = (f32[128,128]{1,0:T(8,128)S(1)}, f32[128,128]{1,0:T(8,128)S(1)}, u32[]{:S(2)}, u32[]{:S(2)}) collective-permute-start(f32[128,128]{1,0:T(8,128)S(1)} %get-tuple-element.40), channel_id=1, source_target_pairs={{0,2},{1,3},{2,0},{3,1},{4,6},{5,7},{6,4},{7,5},{8,10},{9,11},{10,... | collective-permute-start | bytes 196616 | tf_op jit(solution)/shard_map/ppermute | solution.py:14
  41.7 5.2 %collective-permute-start.13 = (f32[128,128]{1,0:T(8,128)S(1)}, f32[128,128]{1,0:T(8,128)S(1)}, u32[]{:S(2)}, u32[]{:S(2)}) collective-permute-start(f32[128,128]{1,0:T(8,128)S(1)} %get-tuple-element.38), channel_id=1, source_target_pairs={{0,1},{1,0},{2,3},{3,2},{4,5},{5,4},{6,7},{7,6},{8,9},{9,8},{10,11... | collective-permute-start | bytes 196616 | tf_op jit(solution)/shard_map/ppermute | solution.py:14
  42.5 9.8 %copy-start.7 = (f32[128,128]{1,0:T(8,128)}, f32[128,128]{1,0:T(8,128)S(1)}, u32[]{:S(2)}) copy-start(f32[128,128]{1,0:T(8,128)S(1)} %add.103.gram_ref) | copy-start | bytes 196612
  42.5 5.3 %collective-permute-start.12 = (f32[128,128]{1,0:T(8,128)S(1)}, f32[128,128]{1,0:T(8,128)S(1)}, u32[]{:S(2)}, u32[]{:S(2)}) collective-permute-start(f32[128,128]{1,0:T(8,128)S(1)} %add.103.gram_ref), channel_id=1, source_target_pairs={{0,16},{4,20},{8,24},{12,28},{16,0},{20,4},{24,8},{28,12},{1,17},{... | collective-permute-start | bytes 196616 | tf_op jit(solution)/shard_map/ppermute | solution.py:14
  47.8 4.5 %copy-start.8 = (f32[128,128]{1,0:T(8,128)}, f32[128,128]{1,0:T(8,128)S(1)}, u32[]{:S(2)}) copy-start(f32[128,128]{1,0:T(8,128)S(1)} %collective-permute-done.12.other_ref) | copy-start | bytes 196612
  47.8 9.9 %collective-permute-start.16 = (f32[128,128]{1,0:T(8,128)S(1)}, f32[128,128]{1,0:T(8,128)S(1)}, u32[]{:S(2)}, u32[]{:S(2)}) collective-permute-start(f32[128,128]{1,0:T(8,128)S(1)} %add_add_fusion), channel_id=1, source_target_pairs={{0,1},{1,0},{2,3},{3,2},{4,5},{5,4},{6,7},{7,6},{8,9},{9,8},{10,11... | collective-permute-start | bytes 196616 | tf_op jit(solution)/shard_map/ppermute | solution.py:14
  48.3 9.4 %collective-permute-start.17 = (f32[128,128]{1,0:T(8,128)S(1)}, f32[128,128]{1,0:T(8,128)S(1)}, u32[]{:S(2)}, u32[]{:S(2)}) collective-permute-start(f32[128,128]{1,0:T(8,128)S(1)} %add_add_fusion), channel_id=1, source_target_pairs={{0,2},{1,3},{2,0},{3,1},{4,6},{5,7},{6,4},{7,5},{8,10},{9,11},{10,... | collective-permute-start | bytes 196616 | tf_op jit(solution)/shard_map/ppermute | solution.py:14
  51.0 6.8 %collective-permute-start.18 = (f32[128,128]{1,0:T(8,128)S(1)}, f32[128,128]{1,0:T(8,128)S(1)}, u32[]{:S(2)}, u32[]{:S(2)}) collective-permute-start(f32[128,128]{1,0:T(8,128)S(1)} %add_add_fusion), channel_id=1, source_target_pairs={{0,3},{1,2},{2,1},{3,0},{4,7},{5,6},{6,5},{7,4},{8,11},{9,10},{10,... | collective-permute-start | bytes 196616 | tf_op jit(solution)/shard_map/ppermute | solution.py:14
  57.6 9.0 %copy-start.4 = (f32[128,128]{1,0:T(8,128)S(1)}, f32[128,128]{1,0:T(8,128)}, u32[]{:S(2)}) copy-start(f32[128,128]{1,0:T(8,128)} %inverse_factor.1) | copy-start | bytes 196612
  57.6 9.6 %copy-start.1 = (bf16[512,2048]{1,0:T(8,128)(2,1)S(1)}, bf16[512,2048]{1,0:T(8,128)(2,1)}, u32[]{:S(2)}) copy-start(bf16[512,2048]{1,0:T(8,128)(2,1)} %copy-done) | copy-start | bytes 6291460
  59.1 9.1 %copy-start.3 = (f32[512,128]{1,0:T(8,128)}, f32[512,128]{1,0:T(8,128)S(1)}, u32[]{:S(2)}) copy-start(f32[512,128]{1,0:T(8,128)S(1)} %fusion.6) | copy-start | bytes 786436
  59.2 6.0 %collective-permute-start.21 = (bf16[512,128]{1,0:T(8,128)(2,1)S(1)}, bf16[512,128]{1,0:T(8,128)(2,1)S(1)}, u32[]{:S(2)}, u32[]{:S(2)}) collective-permute-start(bf16[512,128]{1,0:T(8,128)(2,1)S(1)} %convert_element_type.22), channel_id=1, source_target_pairs={{0,24},{4,28},{8,16},{12,20},{16,8},{20,12},{24,0},{28,4},{1,25},{... | collective-permute-start | bytes 393224 | tf_op jit(solution)/shard_map/ppermute | solution.py:14
  60.6 5.9 %collective-permute-start.20 = (bf16[512,128]{1,0:T(8,128)(2,1)S(1)}, bf16[512,128]{1,0:T(8,128)(2,1)S(1)}, u32[]{:S(2)}, u32[]{:S(2)}) collective-permute-start(bf16[512,128]{1,0:T(8,128)(2,1)S(1)} %convert_element_type.22), channel_id=1, source_target_pairs={{0,16},{4,20},{8,24},{12,28},{16,0},{20,4},{24,8},{28,12},{1,17},{... | collective-permute-start | bytes 393224 | tf_op jit(solution)/shard_map/ppermute | solution.py:14
  61.4 5.1 %collective-permute-start.19 = (bf16[512,128]{1,0:T(8,128)(2,1)S(1)}, bf16[512,128]{1,0:T(8,128)(2,1)S(1)}, u32[]{:S(2)}, u32[]{:S(2)}) collective-permute-start(bf16[512,128]{1,0:T(8,128)(2,1)S(1)} %convert_element_type.22), channel_id=1, source_target_pairs={{0,8},{4,12},{8,0},{12,4},{16,24},{20,28},{24,16},{28,20},{1,9},{5... | collective-permute-start | bytes 393224 | tf_op jit(solution)/shard_map/ppermute | solution.py:14
  66.5 2.0 %collective-permute-start.22 = (bf16[2048,128]{1,0:T(8,128)(2,1)S(1)}, bf16[2048,128]{1,0:T(8,128)(2,1)S(1)}, u32[]{:S(2)}, u32[]{:S(2)}) collective-permute-start(bf16[2048,128]{1,0:T(8,128)(2,1)S(1)} %pad_maximum_fusion.3), channel_id=1, source_target_pairs={{0,4},{4,0},{8,12},{12,8},{16,20},{20,16},{24,28},{28,24},{1,5},{5... | collective-permute-start | bytes 1572872 | tf_op jit(solution)/shard_map/ppermute | solution.py:14
  67.2 1.3 %copy-start.5 = (f32[512,128]{1,0:T(8,128)}, f32[512,128]{1,0:T(8,128)S(1)}, u32[]{:S(2)}) copy-start(f32[512,128]{1,0:T(8,128)S(1)} %fusion.8) | copy-start | bytes 786436

commit v5 on v4

--- a/solution.py
+++ b/solution.py
@@ -147,12 +147,16 @@
     gram, odd_pieces = lax.optimization_barrier((gram + flipped(gram, "inner", 1), products(odd_columns)))
     pieces = products(even_columns) + flipped(odd_pieces, "inner", 1)
     pieces = pieces.reshape(inner // 2, piece, rank)
-    gram = gram + flipped(gram, "outer", 1)
-    gram = gram + flipped(gram, "outer", 2)
-    own = pieces[0] + flipped(pieces[3], "inner", 6)+ flipped(pieces[1], "inner", 2)+ flipped(pieces[2], "inner", 4)
+    for level in range(outer.bit_length() - 1):
+        gram = gram + flipped(gram, "outer", 1 << level)
+    own = pieces[0]
+    for mask in [inner - 2, *evens[:-1]]:
+        own = own + flipped(pieces[mask // 2], "inner", mask)
     gram, own = lax.optimization_barrier((gram, own))
-    gram = gram + flipped(gram, "inner", 2)
-    last = flipped(gram, "inner", 4)
+    levels = inner.bit_length() - 1
+    for level in range(1, levels - 1):
+        gram = gram + flipped(gram, "inner", 1 << level)
+    last = flipped(gram, "inner", 1 << (levels - 1))
     share = lax.dynamic_slice_in_dim(own, mine * part, part, 0)
     for mask in range(1, outer):
         share = share + flipped(

time: 70.3 us -> 70.3 us (level)
  no operation moved by 1% of the time
where the time goes in v5:
time: 70.3 us; the launch traced here: 70 us
  starting transfers between devices  27.6 us (39%)
  waiting for transfers between devices  20.6 us (29%)
  matrix products  7.38 us (10%)
  Pallas kernels  5.38 us (8%)
  other arithmetic  4.46 us (6%)
  local copies, waits for them, and re-layouts  3.66 us (5%)
  between operations  0.95 us (1%)
    ppermute x23, starting transfers between devices, flipped(): lax.ppermute(block, axis, [(low, low ^ mask) for low in range(count)])  27.6 us
    ppermute x23, waiting for transfers between devices, flipped(): lax.ppermute(block, axis, [(low, low ^ mask) for low in range(count)])  20.6 us
    pallas_call x1, Pallas kernels, inverse_factor(): pl.pallas_call(factor_kernel, out_shape=jax.ShapeDtypeStruct((n, n), jnp....  5.38 us
    dynamic_slice x1, local copies, waits for them, and re-layouts, columns(): lax.dynamic_slice_in_dim(samples, (me ^ mask) * piece, piece, 1)  2.63 us
    dot_general x3, matrix products, exact_dot(): lax.dot_general(a, b, (contract, ((), ())), precision=lax.Precision.HIGHE...  2.31 us
    dot_general x2, matrix products, errors(): lax.dot_general(basis_low, factor, (((1,), (1,)), ((), ())), preferred_el...  1.88 us
    dot_general x2, matrix products, products(): lax.dot_general(side, both, (((0,), (0,)), ((), ())), preferred_element_t...  1.52 us
  transfers between devices with their start and end apart: 23, of which 14 were waited for; matrix products, arithmetic and copies ran while one was open for 13% of the time, Pallas kernels for 8%

profile of v5, /device:TPU:0, one launch (start us, length us, event | category | flops | bytes accessed | tf_op | source)
XLA Modules:
  0.0 70.0 jit_solution(7460225245319430993)
XLA Ops:
  0.6 4.0 %collective-permute-start.2 = (bf16[512,128]{1,0:T(8,128)(2,1)}, bf16[512,128]{1,0:T(8,128)(2,1)S(1)}, u32[]{:S(2)}, u32[]{:S(2)}) collective-permute-start(bf16[512,128]{1,0:T(8,128)(2,1)} %param.3), channel_id=1, source_target_pairs={{0,24},{4,28},{8,16},{12,20},{16,8},{20,12},{24,0},{28,4},{1,25},{... | collective-permute-start | bytes 393224 | tf_op jit(solution)/shard_map/ppermute | solution.py:14
  5.2 2.6 %constant_dynamic-slice_fusion.6 = (bf16[512,512]{1,0:T(8,128)(2,1)S(1)}, bf16[512,512]{1,0:T(8,128)(2,1)S(1)}, bf16[512,512]{1,0:T(8,128)(2,1)S(1)}, bf16[512,5...) fusion(bf16[512,4096]{1,0:T(8,128)(2,1)} %param.2, ...), kind=kLoop, calls=%fused_computation.36 | loop fusion | bytes 8388640 | tf_op jit(solution)/shard_map/dynamic_slice | solution.py:126
  8.8 2.3 %collective-permute-done.1 = bf16[512,128]{1,0:T(8,128)(2,1)S(1)} collective-permute-done((bf16[512,128]{1,0:T(8,128)(2,1)}, bf16[512,128]{1,0:T(8,128)(2,1)S(1)}, u32[]{:S(2)}, u32[]{:S(2)}) %collective-permute-start.1) | collective-permute-done | bytes 131104 | tf_op jit(solution)/shard_map/ppermute | solution.py:14
  11.5 0.8 %fusion.15 = f32[512,128]{0,1:T(8,128)S(1)} fusion(bf16[512,2048]{1,0:T(8,128)(2,1)S(1)} %get-tuple-element.15, bf16[2048,128]{1,0:T(8,128)(2,1)S(1)} %pad_maximum_fusion.2), kind=kOutput, calls=%fused_computation.45 | convolution fusion | flops 268435456 | bytes 2883584 | tf_op jit(solution)/shard_map/dot_general | solution.py:133
  12.3 1.1 %collective-permute-done.3 = bf16[2048,128]{1,0:T(8,128)(2,1)S(1)} collective-permute-done((bf16[2048,128]{1,0:T(8,128)(2,1)S(1)}, bf16[2048,128]{1,0:T(8,128)(2,1)S(1)}, u32[]{:S(2)}, u32[]{:S(2)}) %collective-permute-start.3) | collective-permute-done | bytes 524320 | tf_op jit(solution)/shard_map/ppermute | solution.py:14
  13.4 0.8 %reduce-precision_convert_fusion = (bf16[512,128]{0,1:T(8,128)(2,1)S(1)}, bf16[512,128]{0,1:T(8,128)(2,1)S(1)}, f32[512,128]{0,1:T(8,128)S(1)}) fusion(f32[512,128]{0,1:T(8,128)S(1)} %fusion.15, bf16[512,2048]{1,0:T(8,128)(2,1)S(1)} %get-tuple-element.17, bf16[2048,128]{1,0:T(8,128)(2,1)S(1)} %collective-permute-done.3), kind=kOutput, calls=%fused_computation.11 | convolution fusion | flops 268763136 | bytes 3407872 | tf_op jit(solution)/shard_map/dot_general | solution.py:134
  17.0 1.7 %collective-permute-done.7 = f32[2048,128]{1,0:T(8,128)S(1)} collective-permute-done((f32[2048,128]{1,0:T(8,128)S(1)}, f32[2048,128]{1,0:T(8,128)S(1)}, u32[]{:S(2)}, u32[]{:S(2)}) %collective-permute-start.7) | collective-permute-done | bytes 1048608 | tf_op jit(solution)/shard_map/ppermute | solution.py:14
  18.8 0.9 %fusion.14 = (f32[512,128]{1,0:T(8,128)}, f32[512,128]{1,0:T(8,128)}, f32[512,128]{1,0:T(8,128)}) fusion(f32[2048,128]{1,0:T(8,128)S(1)} %fusion), kind=kLoop, calls=%fused_computation.44 | loop fusion | bytes 1572864 | tf_op jit(solution)/shard_map/slice | solution.py:154
  19.7 1.5 %collective-permute-start.10 = (f32[512,128]{1,0:T(8,128)}, f32[512,128]{1,0:T(8,128)}, u32[]{:S(2)}, u32[]{:S(2)}) collective-permute-start(f32[512,128]{1,0:T(8,128)} %get-tuple-element.36), channel_id=1, source_target_pairs={{0,16},{4,20},{8,24},{12,28},{16,0},{20,4},{24,8},{28,12},{1,17},{... | collective-permute-start | bytes 786440 | tf_op jit(solution)/shard_map/ppermute | solution.py:14
  21.9 1.3 %collective-permute-start.8 = (f32[512,128]{1,0:T(8,128)}, f32[512,128]{1,0:T(8,128)}, u32[]{:S(2)}, u32[]{:S(2)}) collective-permute-start(f32[512,128]{1,0:T(8,128)} %get-tuple-element.35), channel_id=1, source_target_pairs={{0,24},{4,28},{8,16},{12,20},{16,8},{20,12},{24,0},{28,4},{1,25},{... | collective-permute-start | bytes 786440 | tf_op jit(solution)/shard_map/ppermute | solution.py:14
  23.2 1.6 %collective-permute-start.5 = (f32[128,128]{1,0:T(8,128)S(1)}, f32[128,128]{1,0:T(8,128)S(1)}, u32[]{:S(2)}, u32[]{:S(2)}) collective-permute-start(f32[128,128]{1,0:T(8,128)S(1)} %add.94), channel_id=1, source_target_pairs={{0,1},{1,0},{2,3},{3,2},{4,5},{5,4},{6,7},{7,6},{8,9},{9,8},{10,11... | collective-permute-start | bytes 196616 | tf_op jit(solution)/shard_map/ppermute | solution.py:14
  24.8 2.7 %collective-permute-done.5 = f32[128,128]{1,0:T(8,128)S(1)} collective-permute-done((f32[128,128]{1,0:T(8,128)S(1)}, f32[128,128]{1,0:T(8,128)S(1)}, u32[]{:S(2)}, u32[]{:S(2)}) %collective-permute-start.5) | collective-permute-done | bytes 65568 | tf_op jit(solution)/shard_map/ppermute | solution.py:14
  27.5 2.7 %collective-permute-start.6 = (f32[128,128]{1,0:T(8,128)S(1)}, f32[128,128]{1,0:T(8,128)}, u32[]{:S(2)}, u32[]{:S(2)}) collective-permute-start(f32[128,128]{1,0:T(8,128)S(1)} %add.96), channel_id=1, source_target_pairs={{0,2},{1,3},{2,0},{3,1},{4,6},{5,7},{6,4},{7,5},{8,10},{9,11},{10,... | collective-permute-start | bytes 196616 | tf_op jit(solution)/shard_map/ppermute | solution.py:14
  30.2 2.7 %collective-permute-done.6 = f32[128,128]{1,0:T(8,128)} collective-permute-done((f32[128,128]{1,0:T(8,128)S(1)}, f32[128,128]{1,0:T(8,128)}, u32[]{:S(2)}, u32[]{:S(2)}) %collective-permute-start.6) | collective-permute-done | bytes 65568 | tf_op jit(solution)/shard_map/ppermute | solution.py:14
  32.8 0.8 %add.97 = f32[128,128]{1,0:T(8,128)S(1)} add(f32[128,128]{1,0:T(8,128)S(1)} %add.96, f32[128,128]{1,0:T(8,128)} %collective-permute-done.6) | non-fusion elementwise | flops 16384 | bytes 196608 | tf_op jit(solution)/shard_map/add | solution.py:151
  33.7 1.5 %collective-permute-done.8 = f32[512,128]{1,0:T(8,128)} collective-permute-done((f32[512,128]{1,0:T(8,128)}, f32[512,128]{1,0:T(8,128)}, u32[]{:S(2)}, u32[]{:S(2)}) %collective-permute-start.8) | collective-permute-done | bytes 262176 | tf_op jit(solution)/shard_map/ppermute | solution.py:14
  35.2 1.2 %fusion.3 = f32[512,128]{1,0:T(8,128)S(1)} fusion(f32[512,128]{1,0:T(8,128)} %collective-permute-done.10, f32[512,128]{1,0:T(8,128)} %collective-permute-done.9, f32[512,128]{1,0:T(8,128)} %collective-permute-done.8, f32[2048,128]{1,0:T(8,128)S(1)} %fusion), kind=kLoop, calls=%fused_computation.15 | loop fusion | flops 196608 | bytes 1310720 | tf_op jit(solution)/shard_map/add | solution.py:154
  36.4 1.6 %collective-permute-start.11 = (f32[128,128]{1,0:T(8,128)S(1)}, f32[128,128]{1,0:T(8,128)S(1)}, u32[]{:S(2)}, u32[]{:S(2)}) collective-permute-start(f32[128,128]{1,0:T(8,128)S(1)} %add.97), channel_id=1, source_target_pairs={{0,8},{4,12},{8,0},{12,4},{16,24},{20,28},{24,16},{28,20},{1,9},{5... | collective-permute-start | bytes 196616 | tf_op jit(solution)/shard_map/ppermute | solution.py:14
  38.0 3.7 %collective-permute-start.15 = (f32[128,128]{1,0:T(8,128)S(1)}, f32[128,128]{1,0:T(8,128)S(1)}, u32[]{:S(2)}, u32[]{:S(2)}) collective-permute-start(f32[128,128]{1,0:T(8,128)S(1)} %get-tuple-element.39), channel_id=1, source_target_pairs={{0,3},{1,2},{2,1},{3,0},{4,7},{5,6},{6,5},{7,4},{8,11},{9,10},{10,... | collective-permute-start | bytes 196616 | tf_op jit(solution)/shard_map/ppermute | solution.py:14
  43.2 1.0 %collective-permute-done.15 = f32[128,128]{1,0:T(8,128)S(1)} collective-permute-done((f32[128,128]{1,0:T(8,128)S(1)}, f32[128,128]{1,0:T(8,128)S(1)}, u32[]{:S(2)}, u32[]{:S(2)}) %collective-permute-start.15) | collective-permute-done | bytes 65568 | tf_op jit(solution)/shard_map/ppermute | solution.py:14
  44.2 2.7 %collective-permute-done.14 = f32[128,128]{1,0:T(8,128)S(1)} collective-permute-done((f32[128,128]{1,0:T(8,128)S(1)}, f32[128,128]{1,0:T(8,128)S(1)}, u32[]{:S(2)}, u32[]{:S(2)}) %collective-permute-start.14) | collective-permute-done | bytes 65568 | tf_op jit(solution)/shard_map/ppermute | solution.py:14
  46.9 0.9 %add_add_fusion = f32[128,128]{1,0:T(8,128)S(1)} fusion(f32[128,128]{1,0:T(8,128)S(1)} %collective-permute-done.15, f32[128,128]{1,0:T(8,128)S(1)} %collective-permute-done.14, f32[128,128]{1,0:T(8,128)S(1)} %collective-permute-done.13, f32[512,128]{1,0:T(8,128)} %copy-done.2, s32[]{:T(128)S(6)} %select_n.48), kind=kLoop, calls=%fused_computation.23 | loop fusion | flops 49152 | bytes 327684 | tf_op jit(solution)/shard_map/add | solution.py:162
  48.3 2.7 %collective-permute-start.17 = (f32[128,128]{1,0:T(8,128)S(1)}, f32[128,128]{1,0:T(8,128)S(1)}, u32[]{:S(2)}, u32[]{:S(2)}) collective-permute-start(f32[128,128]{1,0:T(8,128)S(1)} %add_add_fusion), channel_id=1, source_target_pairs={{0,2},{1,3},{2,0},{3,1},{4,6},{5,7},{6,4},{7,5},{8,10},{9,11},{10,... | collective-permute-start | bytes 196616 | tf_op jit(solution)/shard_map/ppermute | solution.py:14
  51.0 1.3 %collective-permute-start.18 = (f32[128,128]{1,0:T(8,128)S(1)}, f32[128,128]{1,0:T(8,128)S(1)}, u32[]{:S(2)}, u32[]{:S(2)}) collective-permute-start(f32[128,128]{1,0:T(8,128)S(1)} %add_add_fusion), channel_id=1, source_target_pairs={{0,3},{1,2},{2,1},{3,0},{4,7},{5,6},{6,5},{7,4},{8,11},{9,10},{10,... | collective-permute-start | bytes 196616 | tf_op jit(solution)/shard_map/ppermute | solution.py:14
  52.3 5.4 %inverse_factor.1 = f32[128,128]{1,0:T(8,128)} custom-call(f32[128,128]{1,0:T(8,128)} %copy-done.7, f32[128,128]{1,0:T(8,128)} %copy-done.8), custom_call_target="tpu_custom_call" | custom-call | flops 6000000000 | bytes 131072 | tf_op jit(solution)/shard_map/inverse_factor/pallas_call | solution.py:97
  57.8 1.3 %fusion.6 = f32[512,128]{1,0:T(8,128)S(1)} fusion(f32[512,128]{1,0:T(8,128)S(1)} %constant_dynamic-update-slice_fusion, f32[128,128]{1,0:T(8,128)} %inverse_factor.1), kind=kOutput, calls=%fused_computation.19 | convolution fusion | flops 100679680 | bytes 589824 | tf_op jit(solution)/shard_map/dot_general | solution.py:18
  59.2 1.5 %collective-permute-start.21 = (bf16[512,128]{1,0:T(8,128)(2,1)S(1)}, bf16[512,128]{1,0:T(8,128)(2,1)S(1)}, u32[]{:S(2)}, u32[]{:S(2)}) collective-permute-start(bf16[512,128]{1,0:T(8,128)(2,1)S(1)} %convert_element_type.22), channel_id=1, source_target_pairs={{0,24},{4,28},{8,16},{12,20},{16,8},{20,12},{24,0},{28,4},{1,25},{... | collective-permute-start | bytes 393224 | tf_op jit(solution)/shard_map/ppermute | solution.py:14
  61.4 1.3 %collective-permute-start.19 = (bf16[512,128]{1,0:T(8,128)(2,1)S(1)}, bf16[512,128]{1,0:T(8,128)(2,1)S(1)}, u32[]{:S(2)}, u32[]{:S(2)}) collective-permute-start(bf16[512,128]{1,0:T(8,128)(2,1)S(1)} %convert_element_type.22), channel_id=1, source_target_pairs={{0,8},{4,12},{8,0},{12,4},{16,24},{20,28},{24,16},{28,20},{1,9},{5... | collective-permute-start | bytes 393224 | tf_op jit(solution)/shard_map/ppermute | solution.py:14
  62.7 2.5 %collective-permute-done.21 = bf16[512,128]{1,0:T(8,128)(2,1)S(1)} collective-permute-done((bf16[512,128]{1,0:T(8,128)(2,1)S(1)}, bf16[512,128]{1,0:T(8,128)(2,1)S(1)}, u32[]{:S(2)}, u32[]{:S(2)}) %collective-permute-start.21) | collective-permute-done | bytes 131104 | tf_op jit(solution)/shard_map/ppermute | solution.py:14
  65.2 1.3 %collective-permute-done.20 = bf16[512,128]{1,0:T(8,128)(2,1)S(1)} collective-permute-done((bf16[512,128]{1,0:T(8,128)(2,1)S(1)}, bf16[512,128]{1,0:T(8,128)(2,1)S(1)}, u32[]{:S(2)}, u32[]{:S(2)}) %collective-permute-start.20) | collective-permute-done | bytes 131104 | tf_op jit(solution)/shard_map/ppermute | solution.py:14
  67.2 0.9 %multiply_reduce_fusion.1 = f32[512]{0:T(512)S(1)} fusion(bf16[512,2048]{1,0:T(8,128)(2,1)S(1)} %copy-done.1, f32[512,128]{1,0:T(8,128)S(1)} %fusion.8, bf16[512,128]{1,0:T(8,128)(2,1)S(1)} %collective-permute-done.21, bf16[512,128]{1,0:T(8,128)(2,1)S(1)} %collective-permute-done.20, bf16[512,128]{1,0:T(8,128)(2,1)S(1)} %collective-permute-done.19, ...), kind=kOutput, calls=%fused_computation.1 | convolution fusion | flops 275840512 | bytes 2885632 | tf_op jit(solution)/shard_map/dot_general | solution.py:188
  68.5 0.9 %multiply_reduce_fusion = f32[512]{0:T(512)S(1)} fusion(bf16[512,2048]{1,0:T(8,128)(2,1)S(1)} %get-tuple-element.17, bf16[2048,128]{1,0:T(8,128)(2,1)S(1)} %collective-permute-done.22, f32[512,128]{1,0:T(8,128)S(1)} %fusion.8), kind=kOutput, calls=%fused_computation | convolution fusion | flops 273743360 | bytes 2885632 | tf_op jit(solution)/shard_map/dot_general | solution.py:188
  (64 shorter events, 10.0 us)
Async XLA Ops:
  0.6 8.2 %collective-permute-start.2 = (bf16[512,128]{1,0:T(8,128)(2,1)}, bf16[512,128]{1,0:T(8,128)(2,1)S(1)}, u32[]{:S(2)}, u32[]{:S(2)}) collective-permute-start(bf16[512,128]{1,0:T(8,128)(2,1)} %param.3), channel_id=1, source_target_pairs={{0,24},{4,28},{8,16},{12,20},{16,8},{20,12},{24,0},{28,4},{1,25},{... | collective-permute-start | bytes 393224 | tf_op jit(solution)/shard_map/ppermute | solution.py:14
  4.6 6.5 %collective-permute-start.1 = (bf16[512,128]{1,0:T(8,128)(2,1)}, bf16[512,128]{1,0:T(8,128)(2,1)S(1)}, u32[]{:S(2)}, u32[]{:S(2)}) collective-permute-start(bf16[512,128]{1,0:T(8,128)(2,1)} %param.3), channel_id=1, source_target_pairs={{0,16},{4,20},{8,24},{12,28},{16,0},{20,4},{24,8},{28,12},{1,17},{... | collective-permute-start | bytes 393224 | tf_op jit(solution)/shard_map/ppermute | solution.py:14
  5.1 6.3 %collective-permute-start = (bf16[512,128]{1,0:T(8,128)(2,1)}, bf16[512,128]{1,0:T(8,128)(2,1)S(1)}, u32[]{:S(2)}, u32[]{:S(2)}) collective-permute-start(bf16[512,128]{1,0:T(8,128)(2,1)} %param.3), channel_id=1, source_target_pairs={{0,8},{4,12},{8,0},{12,4},{16,24},{20,28},{24,16},{28,20},{1,9},{5... | collective-permute-start | bytes 393224 | tf_op jit(solution)/shard_map/ppermute | solution.py:14
  7.9 3.5 %copy-start.6 = (bf16[512,128]{1,0:T(8,128)(2,1)S(1)}, bf16[512,128]{1,0:T(8,128)(2,1)}, u32[]{:S(2)}) copy-start(bf16[512,128]{1,0:T(8,128)(2,1)} %param.3) | copy-start | bytes 393220
  8.5 7.7 %copy-start = (bf16[512,2048]{1,0:T(8,128)(2,1)}, bf16[512,2048]{1,0:T(8,128)(2,1)S(1)}, u32[]{:S(2)}) copy-start(bf16[512,2048]{1,0:T(8,128)(2,1)S(1)} %get-tuple-element.15) | copy-start | bytes 6291460
  11.4 2.0 %collective-permute-start.3 = (bf16[2048,128]{1,0:T(8,128)(2,1)S(1)}, bf16[2048,128]{1,0:T(8,128)(2,1)S(1)}, u32[]{:S(2)}, u32[]{:S(2)}) collective-permute-start(bf16[2048,128]{1,0:T(8,128)(2,1)S(1)} %pad_maximum_fusion.2), channel_id=1, source_target_pairs={{0,4},{4,0},{8,12},{12,8},{16,20},{20,16},{24,28},{28,24},{1,5},{5... | collective-permute-start | bytes 1572872 | tf_op jit(solution)/shard_map/ppermute | solution.py:14
  14.6 1.3 %collective-permute-start.4 = (f32[128,128]{1,0:T(8,128)S(1)}, f32[128,128]{1,0:T(8,128)S(1)}, u32[]{:S(2)}, u32[]{:S(2)}) collective-permute-start(f32[128,128]{1,0:T(8,128)S(1)} %fusion.16), channel_id=1, source_target_pairs={{0,4},{4,0},{8,12},{12,8},{16,20},{20,16},{24,28},{28,24},{1,5},{5... | collective-permute-start | bytes 196616 | tf_op jit(solution)/shard_map/ppermute | solution.py:14
  16.0 2.7 %collective-permute-start.7 = (f32[2048,128]{1,0:T(8,128)S(1)}, f32[2048,128]{1,0:T(8,128)S(1)}, u32[]{:S(2)}, u32[]{:S(2)}) collective-permute-start(f32[2048,128]{1,0:T(8,128)S(1)} %slice_add_fusion.1), channel_id=1, source_target_pairs={{0,4},{4,0},{8,12},{12,8},{16,20},{20,16},{24,28},{28,24},{1,5},{5... | collective-permute-start | bytes 3145736 | tf_op jit(solution)/shard_map/ppermute | solution.py:14
  19.7 14.0 %collective-permute-start.10 = (f32[512,128]{1,0:T(8,128)}, f32[512,128]{1,0:T(8,128)}, u32[]{:S(2)}, u32[]{:S(2)}) collective-permute-start(f32[512,128]{1,0:T(8,128)} %get-tuple-element.36), channel_id=1, source_target_pairs={{0,16},{4,20},{8,24},{12,28},{16,0},{20,4},{24,8},{28,12},{1,17},{... | collective-permute-start | bytes 786440 | tf_op jit(solution)/shard_map/ppermute | solution.py:14
  21.2 12.5 %collective-permute-start.9 = (f32[512,128]{1,0:T(8,128)}, f32[512,128]{1,0:T(8,128)}, u32[]{:S(2)}, u32[]{:S(2)}) collective-permute-start(f32[512,128]{1,0:T(8,128)} %get-tuple-element.37), channel_id=1, source_target_pairs={{0,8},{4,12},{8,0},{12,4},{16,24},{20,28},{24,16},{28,20},{1,9},{5... | collective-permute-start | bytes 786440 | tf_op jit(solution)/shard_map/ppermute | solution.py:14
  21.9 13.3 %collective-permute-start.8 = (f32[512,128]{1,0:T(8,128)}, f32[512,128]{1,0:T(8,128)}, u32[]{:S(2)}, u32[]{:S(2)}) collective-permute-start(f32[512,128]{1,0:T(8,128)} %get-tuple-element.35), channel_id=1, source_target_pairs={{0,24},{4,28},{8,16},{12,20},{16,8},{20,12},{24,0},{28,4},{1,25},{... | collective-permute-start | bytes 786440 | tf_op jit(solution)/shard_map/ppermute | solution.py:14
  23.2 4.3 %collective-permute-start.5 = (f32[128,128]{1,0:T(8,128)S(1)}, f32[128,128]{1,0:T(8,128)S(1)}, u32[]{:S(2)}, u32[]{:S(2)}) collective-permute-start(f32[128,128]{1,0:T(8,128)S(1)} %add.94), channel_id=1, source_target_pairs={{0,1},{1,0},{2,3},{3,2},{4,5},{5,4},{6,7},{7,6},{8,9},{9,8},{10,11... | collective-permute-start | bytes 196616 | tf_op jit(solution)/shard_map/ppermute | solution.py:14
  27.5 5.3 %collective-permute-start.6 = (f32[128,128]{1,0:T(8,128)S(1)}, f32[128,128]{1,0:T(8,128)}, u32[]{:S(2)}, u32[]{:S(2)}) collective-permute-start(f32[128,128]{1,0:T(8,128)S(1)} %add.96), channel_id=1, source_target_pairs={{0,2},{1,3},{2,0},{3,1},{4,6},{5,7},{6,4},{7,5},{8,10},{9,11},{10,... | collective-permute-start | bytes 196616 | tf_op jit(solution)/shard_map/ppermute | solution.py:14
  36.4 1.6 %copy-start.2 = (f32[512,128]{1,0:T(8,128)}, f32[512,128]{1,0:T(8,128)S(1)}, u32[]{:S(2)}) copy-start(f32[512,128]{1,0:T(8,128)S(1)} %fusion.3) | copy-start | bytes 786436
  36.4 6.1 %collective-permute-start.11 = (f32[128,128]{1,0:T(8,128)S(1)}, f32[128,128]{1,0:T(8,128)S(1)}, u32[]{:S(2)}, u32[]{:S(2)}) collective-permute-start(f32[128,128]{1,0:T(8,128)S(1)} %add.97), channel_id=1, source_target_pairs={{0,8},{4,12},{8,0},{12,4},{16,24},{20,28},{24,16},{28,20},{1,9},{5... | collective-permute-start | bytes 196616 | tf_op jit(solution)/shard_map/ppermute | solution.py:14
  38.0 6.1 %collective-permute-start.15 = (f32[128,128]{1,0:T(8,128)S(1)}, f32[128,128]{1,0:T(8,128)S(1)}, u32[]{:S(2)}, u32[]{:S(2)}) collective-permute-start(f32[128,128]{1,0:T(8,128)S(1)} %get-tuple-element.39), channel_id=1, source_target_pairs={{0,3},{1,2},{2,1},{3,0},{4,7},{5,6},{6,5},{7,4},{8,11},{9,10},{10,... | collective-permute-start | bytes 196616 | tf_op jit(solution)/shard_map/ppermute | solution.py:14
  41.7 5.2 %collective-permute-start.14 = (f32[128,128]{1,0:T(8,128)S(1)}, f32[128,128]{1,0:T(8,128)S(1)}, u32[]{:S(2)}, u32[]{:S(2)}) collective-permute-start(f32[128,128]{1,0:T(8,128)S(1)} %get-tuple-element.40), channel_id=1, source_target_pairs={{0,2},{1,3},{2,0},{3,1},{4,6},{5,7},{6,4},{7,5},{8,10},{9,11},{10,... | collective-permute-start | bytes 196616 | tf_op jit(solution)/shard_map/ppermute | solution.py:14
  41.7 5.2 %collective-permute-start.13 = (f32[128,128]{1,0:T(8,128)S(1)}, f32[128,128]{1,0:T(8,128)S(1)}, u32[]{:S(2)}, u32[]{:S(2)}) collective-permute-start(f32[128,128]{1,0:T(8,128)S(1)} %get-tuple-element.38), channel_id=1, source_target_pairs={{0,1},{1,0},{2,3},{3,2},{4,5},{5,4},{6,7},{7,6},{8,9},{9,8},{10,11... | collective-permute-start | bytes 196616 | tf_op jit(solution)/shard_map/ppermute | solution.py:14
  42.5 9.8 %copy-start.7 = (f32[128,128]{1,0:T(8,128)}, f32[128,128]{1,0:T(8,128)S(1)}, u32[]{:S(2)}) copy-start(f32[128,128]{1,0:T(8,128)S(1)} %add.103.gram_ref) | copy-start | bytes 196612
  42.5 5.3 %collective-permute-start.12 = (f32[128,128]{1,0:T(8,128)S(1)}, f32[128,128]{1,0:T(8,128)S(1)}, u32[]{:S(2)}, u32[]{:S(2)}) collective-permute-start(f32[128,128]{1,0:T(8,128)S(1)} %add.103.gram_ref), channel_id=1, source_target_pairs={{0,16},{4,20},{8,24},{12,28},{16,0},{20,4},{24,8},{28,12},{1,17},{... | collective-permute-start | bytes 196616 | tf_op jit(solution)/shard_map/ppermute | solution.py:14
  47.8 4.5 %copy-start.8 = (f32[128,128]{1,0:T(8,128)}, f32[128,128]{1,0:T(8,128)S(1)}, u32[]{:S(2)}) copy-start(f32[128,128]{1,0:T(8,128)S(1)} %collective-permute-done.12.other_ref) | copy-start | bytes 196612
  47.8 9.9 %collective-permute-start.16 = (f32[128,128]{1,0:T(8,128)S(1)}, f32[128,128]{1,0:T(8,128)S(1)}, u32[]{:S(2)}, u32[]{:S(2)}) collective-permute-start(f32[128,128]{1,0:T(8,128)S(1)} %add_add_fusion), channel_id=1, source_target_pairs={{0,1},{1,0},{2,3},{3,2},{4,5},{5,4},{6,7},{7,6},{8,9},{9,8},{10,11... | collective-permute-start | bytes 196616 | tf_op jit(solution)/shard_map/ppermute | solution.py:14
  48.3 9.4 %collective-permute-start.17 = (f32[128,128]{1,0:T(8,128)S(1)}, f32[128,128]{1,0:T(8,128)S(1)}, u32[]{:S(2)}, u32[]{:S(2)}) collective-permute-start(f32[128,128]{1,0:T(8,128)S(1)} %add_add_fusion), channel_id=1, source_target_pairs={{0,2},{1,3},{2,0},{3,1},{4,6},{5,7},{6,4},{7,5},{8,10},{9,11},{10,... | collective-permute-start | bytes 196616 | tf_op jit(solution)/shard_map/ppermute | solution.py:14
  51.0 6.8 %collective-permute-start.18 = (f32[128,128]{1,0:T(8,128)S(1)}, f32[128,128]{1,0:T(8,128)S(1)}, u32[]{:S(2)}, u32[]{:S(2)}) collective-permute-start(f32[128,128]{1,0:T(8,128)S(1)} %add_add_fusion), channel_id=1, source_target_pairs={{0,3},{1,2},{2,1},{3,0},{4,7},{5,6},{6,5},{7,4},{8,11},{9,10},{10,... | collective-permute-start | bytes 196616 | tf_op jit(solution)/shard_map/ppermute | solution.py:14
  57.6 9.0 %copy-start.4 = (f32[128,128]{1,0:T(8,128)S(1)}, f32[128,128]{1,0:T(8,128)}, u32[]{:S(2)}) copy-start(f32[128,128]{1,0:T(8,128)} %inverse_factor.1) | copy-start | bytes 196612
  57.6 9.6 %copy-start.1 = (bf16[512,2048]{1,0:T(8,128)(2,1)S(1)}, bf16[512,2048]{1,0:T(8,128)(2,1)}, u32[]{:S(2)}) copy-start(bf16[512,2048]{1,0:T(8,128)(2,1)} %copy-done) | copy-start | bytes 6291460
  59.1 9.1 %copy-start.3 = (f32[512,128]{1,0:T(8,128)}, f32[512,128]{1,0:T(8,128)S(1)}, u32[]{:S(2)}) copy-start(f32[512,128]{1,0:T(8,128)S(1)} %fusion.6) | copy-start | bytes 786436
  59.2 6.0 %collective-permute-start.21 = (bf16[512,128]{1,0:T(8,128)(2,1)S(1)}, bf16[512,128]{1,0:T(8,128)(2,1)S(1)}, u32[]{:S(2)}, u32[]{:S(2)}) collective-permute-start(bf16[512,128]{1,0:T(8,128)(2,1)S(1)} %convert_element_type.22), channel_id=1, source_target_pairs={{0,24},{4,28},{8,16},{12,20},{16,8},{20,12},{24,0},{28,4},{1,25},{... | collective-permute-start | bytes 393224 | tf_op jit(solution)/shard_map/ppermute | solution.py:14
  60.6 5.9 %collective-permute-start.20 = (bf16[512,128]{1,0:T(8,128)(2,1)S(1)}, bf16[512,128]{1,0:T(8,128)(2,1)S(1)}, u32[]{:S(2)}, u32[]{:S(2)}) collective-permute-start(bf16[512,128]{1,0:T(8,128)(2,1)S(1)} %convert_element_type.22), channel_id=1, source_target_pairs={{0,16},{4,20},{8,24},{12,28},{16,0},{20,4},{24,8},{28,12},{1,17},{... | collective-permute-start | bytes 393224 | tf_op jit(solution)/shard_map/ppermute | solution.py:14
  61.4 5.1 %collective-permute-start.19 = (bf16[512,128]{1,0:T(8,128)(2,1)S(1)}, bf16[512,128]{1,0:T(8,128)(2,1)S(1)}, u32[]{:S(2)}, u32[]{:S(2)}) collective-permute-start(bf16[512,128]{1,0:T(8,128)(2,1)S(1)} %convert_element_type.22), channel_id=1, source_target_pairs={{0,8},{4,12},{8,0},{12,4},{16,24},{20,28},{24,16},{28,20},{1,9},{5... | collective-permute-start | bytes 393224 | tf_op jit(solution)/shard_map/ppermute | solution.py:14
  66.5 2.0 %collective-permute-start.22 = (bf16[2048,128]{1,0:T(8,128)(2,1)S(1)}, bf16[2048,128]{1,0:T(8,128)(2,1)S(1)}, u32[]{:S(2)}, u32[]{:S(2)}) collective-permute-start(bf16[2048,128]{1,0:T(8,128)(2,1)S(1)} %pad_maximum_fusion.3), channel_id=1, source_target_pairs={{0,4},{4,0},{8,12},{12,8},{16,20},{20,16},{24,28},{28,24},{1,5},{5... | collective-permute-start | bytes 1572872 | tf_op jit(solution)/shard_map/ppermute | solution.py:14
  67.2 1.3 %copy-start.5 = (f32[512,128]{1,0:T(8,128)}, f32[512,128]{1,0:T(8,128)S(1)}, u32[]{:S(2)}) copy-start(f32[512,128]{1,0:T(8,128)S(1)} %fusion.8) | copy-start | bytes 786436

commit v6 on v5

--- a/solution.py
+++ b/solution.py
@@ -100,6 +100,7 @@
         out_specs=pl.BlockSpec(memory_space=pltpu.VMEM),
         scratch_shapes=[pltpu.VMEM((n, 2 * n), jnp.float32), pltpu.VMEM((16, 2 * n), jnp.float32)],
         cost_estimate=pl.CostEstimate(flops=6_000_000_000, bytes_accessed=131072, transcendentals=128),
+        compiler_params=pltpu.CompilerParams(vmem_limit_bytes=4 * 1024 * 1024),
         name="inverse_factor",
     )(*grams)
 

time: 70.3 us -> 68.6 us (0.976)
  Pallas kernels: 5.38 us -> 3.9 us
  matrix products: 7.38 us -> 6.42 us
  waiting for transfers between devices: 20.6 us -> 21.4 us
    pallas_call x1, Pallas kernels: 5.38 us -> 3.9 us  [inverse_factor(): pl.pallas_call(factor_kernel, out_shape=jax.ShapeDtypeStruct((n, n), jnp....]
    dot_general x3, matrix products: 2.31 us -> 1.34 us  [exact_dot(): lax.dot_general(a, b, (contract, ((), ())), precision=lax.Precision.HIGHE...]
    ppermute x23, waiting for transfers between devices: 20.6 us -> 21.4 us  [flipped(): lax.ppermute(block, axis, [(low, low ^ mask) for low in range(count)])]
  transfers between devices with their start and end apart: 23 -> 23, of which waited for: 14 -> 15; matrix products, arithmetic and copies ran while one was open for 13% -> 13% of each run, Pallas kernels for 8% -> 6%
where the time goes in v6:
time: 68.6 us; the launch traced here: 68.4 us
  starting transfers between devices  27.6 us (40%)
  waiting for transfers between devices  21.4 us (31%)
  matrix products  6.42 us (9%)
  other arithmetic  4.46 us (7%)
  Pallas kernels  3.9 us (6%)
  local copies, waits for them, and re-layouts  3.64 us (5%)
  between operations  0.92 us (1%)
    ppermute x23, starting transfers between devices, flipped(): lax.ppermute(block, axis, [(low, low ^ mask) for low in range(count)])  27.6 us
    ppermute x23, waiting for transfers between devices, flipped(): lax.ppermute(block, axis, [(low, low ^ mask) for low in range(count)])  21.4 us
    pallas_call x1, Pallas kernels, inverse_factor(): pl.pallas_call(factor_kernel, out_shape=jax.ShapeDtypeStruct((n, n), jnp....  3.9 us
    dynamic_slice x1, local copies, waits for them, and re-layouts, columns(): lax.dynamic_slice_in_dim(samples, (me ^ mask) * piece, piece, 1)  2.63 us
    dot_general x2, matrix products, errors(): lax.dot_general(basis_low, factor, (((1,), (1,)), ((), ())), preferred_el...  1.88 us
    dot_general x2, matrix products, products(): lax.dot_general(side, both, (((0,), (0,)), ((), ())), preferred_element_t...  1.52 us
  transfers between devices with their start and end apart: 23, of which 15 were waited for; matrix products, arithmetic and copies ran while one was open for 13% of the time, Pallas kernels for 6%

profile of v6, /device:TPU:0, one launch (start us, length us, event | category | flops | bytes accessed | tf_op | source)
XLA Modules:
  0.0 68.4 jit_solution(7823578436377018996)
XLA Ops:
  0.6 4.0 %collective-permute-start.2 = (bf16[512,128]{1,0:T(8,128)(2,1)}, bf16[512,128]{1,0:T(8,128)(2,1)S(1)}, u32[]{:S(2)}, u32[]{:S(2)}) collective-permute-start(bf16[512,128]{1,0:T(8,128)(2,1)} %param.3), channel_id=1, source_target_pairs={{0,24},{4,28},{8,16},{12,20},{16,8},{20,12},{24,0},{28,4},{1,25},{... | collective-permute-start | bytes 393224 | tf_op jit(solution)/shard_map/ppermute | solution.py:14
  5.2 2.6 %constant_dynamic-slice_fusion.6 = (bf16[512,512]{1,0:T(8,128)(2,1)S(1)}, bf16[512,512]{1,0:T(8,128)(2,1)S(1)}, bf16[512,512]{1,0:T(8,128)(2,1)S(1)}, bf16[512,5...) fusion(bf16[512,4096]{1,0:T(8,128)(2,1)} %param.2, ...), kind=kLoop, calls=%fused_computation.36 | loop fusion | bytes 8388640 | tf_op jit(solution)/shard_map/dynamic_slice | solution.py:127
  8.8 2.3 %collective-permute-done.1 = bf16[512,128]{1,0:T(8,128)(2,1)S(1)} collective-permute-done((bf16[512,128]{1,0:T(8,128)(2,1)}, bf16[512,128]{1,0:T(8,128)(2,1)S(1)}, u32[]{:S(2)}, u32[]{:S(2)}) %collective-permute-start.1) | collective-permute-done | bytes 131104 | tf_op jit(solution)/shard_map/ppermute | solution.py:14
  11.5 0.8 %fusion.15 = f32[512,128]{0,1:T(8,128)S(1)} fusion(bf16[512,2048]{1,0:T(8,128)(2,1)S(1)} %get-tuple-element.15, bf16[2048,128]{1,0:T(8,128)(2,1)S(1)} %pad_maximum_fusion.2), kind=kOutput, calls=%fused_computation.45 | convolution fusion | flops 268435456 | bytes 2883584 | tf_op jit(solution)/shard_map/dot_general | solution.py:134
  12.3 1.1 %collective-permute-done.3 = bf16[2048,128]{1,0:T(8,128)(2,1)S(1)} collective-permute-done((bf16[2048,128]{1,0:T(8,128)(2,1)S(1)}, bf16[2048,128]{1,0:T(8,128)(2,1)S(1)}, u32[]{:S(2)}, u32[]{:S(2)}) %collective-permute-start.3) | collective-permute-done | bytes 524320 | tf_op jit(solution)/shard_map/ppermute | solution.py:14
  13.4 0.8 %reduce-precision_convert_fusion = (bf16[512,128]{0,1:T(8,128)(2,1)S(1)}, bf16[512,128]{0,1:T(8,128)(2,1)S(1)}, f32[512,128]{0,1:T(8,128)S(1)}) fusion(f32[512,128]{0,1:T(8,128)S(1)} %fusion.15, bf16[512,2048]{1,0:T(8,128)(2,1)S(1)} %get-tuple-element.17, bf16[2048,128]{1,0:T(8,128)(2,1)S(1)} %collective-permute-done.3), kind=kOutput, calls=%fused_computation.11 | convolution fusion | flops 268763136 | bytes 3407872 | tf_op jit(solution)/shard_map/dot_general | solution.py:135
  17.0 1.7 %collective-permute-done.7 = f32[2048,128]{1,0:T(8,128)S(1)} collective-permute-done((f32[2048,128]{1,0:T(8,128)S(1)}, f32[2048,128]{1,0:T(8,128)S(1)}, u32[]{:S(2)}, u32[]{:S(2)}) %collective-permute-start.7) | collective-permute-done | bytes 1048608 | tf_op jit(solution)/shard_map/ppermute | solution.py:14
  18.8 0.9 %fusion.14 = (f32[512,128]{1,0:T(8,128)}, f32[512,128]{1,0:T(8,128)}, f32[512,128]{1,0:T(8,128)}) fusion(f32[2048,128]{1,0:T(8,128)S(1)} %fusion), kind=kLoop, calls=%fused_computation.44 | loop fusion | bytes 1572864 | tf_op jit(solution)/shard_map/slice | solution.py:155
  19.7 1.5 %collective-permute-start.10 = (f32[512,128]{1,0:T(8,128)}, f32[512,128]{1,0:T(8,128)}, u32[]{:S(2)}, u32[]{:S(2)}) collective-permute-start(f32[512,128]{1,0:T(8,128)} %get-tuple-element.36), channel_id=1, source_target_pairs={{0,16},{4,20},{8,24},{12,28},{16,0},{20,4},{24,8},{28,12},{1,17},{... | collective-permute-start | bytes 786440 | tf_op jit(solution)/shard_map/ppermute | solution.py:14
  21.9 1.3 %collective-permute-start.8 = (f32[512,128]{1,0:T(8,128)}, f32[512,128]{1,0:T(8,128)}, u32[]{:S(2)}, u32[]{:S(2)}) collective-permute-start(f32[512,128]{1,0:T(8,128)} %get-tuple-element.35), channel_id=1, source_target_pairs={{0,24},{4,28},{8,16},{12,20},{16,8},{20,12},{24,0},{28,4},{1,25},{... | collective-permute-start | bytes 786440 | tf_op jit(solution)/shard_map/ppermute | solution.py:14
  23.2 1.6 %collective-permute-start.5 = (f32[128,128]{1,0:T(8,128)S(1)}, f32[128,128]{1,0:T(8,128)S(1)}, u32[]{:S(2)}, u32[]{:S(2)}) collective-permute-start(f32[128,128]{1,0:T(8,128)S(1)} %add.94), channel_id=1, source_target_pairs={{0,1},{1,0},{2,3},{3,2},{4,5},{5,4},{6,7},{7,6},{8,9},{9,8},{10,11... | collective-permute-start | bytes 196616 | tf_op jit(solution)/shard_map/ppermute | solution.py:14
  24.8 2.7 %collective-permute-done.5 = f32[128,128]{1,0:T(8,128)S(1)} collective-permute-done((f32[128,128]{1,0:T(8,128)S(1)}, f32[128,128]{1,0:T(8,128)S(1)}, u32[]{:S(2)}, u32[]{:S(2)}) %collective-permute-start.5) | collective-permute-done | bytes 65568 | tf_op jit(solution)/shard_map/ppermute | solution.py:14
  27.5 2.7 %collective-permute-start.6 = (f32[128,128]{1,0:T(8,128)S(1)}, f32[128,128]{1,0:T(8,128)}, u32[]{:S(2)}, u32[]{:S(2)}) collective-permute-start(f32[128,128]{1,0:T(8,128)S(1)} %add.96), channel_id=1, source_target_pairs={{0,2},{1,3},{2,0},{3,1},{4,6},{5,7},{6,4},{7,5},{8,10},{9,11},{10,... | collective-permute-start | bytes 196616 | tf_op jit(solution)/shard_map/ppermute | solution.py:14
  30.2 2.7 %collective-permute-done.6 = f32[128,128]{1,0:T(8,128)} collective-permute-done((f32[128,128]{1,0:T(8,128)S(1)}, f32[128,128]{1,0:T(8,128)}, u32[]{:S(2)}, u32[]{:S(2)}) %collective-permute-start.6) | collective-permute-done | bytes 65568 | tf_op jit(solution)/shard_map/ppermute | solution.py:14
  32.8 0.8 %add.97 = f32[128,128]{1,0:T(8,128)S(1)} add(f32[128,128]{1,0:T(8,128)S(1)} %add.96, f32[128,128]{1,0:T(8,128)} %collective-permute-done.6) | non-fusion elementwise | flops 16384 | bytes 196608 | tf_op jit(solution)/shard_map/add | solution.py:152
  33.7 1.5 %collective-permute-done.8 = f32[512,128]{1,0:T(8,128)} collective-permute-done((f32[512,128]{1,0:T(8,128)}, f32[512,128]{1,0:T(8,128)}, u32[]{:S(2)}, u32[]{:S(2)}) %collective-permute-start.8) | collective-permute-done | bytes 262176 | tf_op jit(solution)/shard_map/ppermute | solution.py:14
  35.2 1.2 %fusion.3 = f32[512,128]{1,0:T(8,128)S(1)} fusion(f32[512,128]{1,0:T(8,128)} %collective-permute-done.10, f32[512,128]{1,0:T(8,128)} %collective-permute-done.9, f32[512,128]{1,0:T(8,128)} %collective-permute-done.8, f32[2048,128]{1,0:T(8,128)S(1)} %fusion), kind=kLoop, calls=%fused_computation.15 | loop fusion | flops 196608 | bytes 1310720 | tf_op jit(solution)/shard_map/add | solution.py:155
  36.4 1.6 %collective-permute-start.11 = (f32[128,128]{1,0:T(8,128)S(1)}, f32[128,128]{1,0:T(8,128)S(1)}, u32[]{:S(2)}, u32[]{:S(2)}) collective-permute-start(f32[128,128]{1,0:T(8,128)S(1)} %add.97), channel_id=1, source_target_pairs={{0,8},{4,12},{8,0},{12,4},{16,24},{20,28},{24,16},{28,20},{1,9},{5... | collective-permute-start | bytes 196616 | tf_op jit(solution)/shard_map/ppermute | solution.py:14
  38.0 3.7 %collective-permute-start.15 = (f32[128,128]{1,0:T(8,128)S(1)}, f32[128,128]{1,0:T(8,128)S(1)}, u32[]{:S(2)}, u32[]{:S(2)}) collective-permute-start(f32[128,128]{1,0:T(8,128)S(1)} %get-tuple-element.39), channel_id=1, source_target_pairs={{0,3},{1,2},{2,1},{3,0},{4,7},{5,6},{6,5},{7,4},{8,11},{9,10},{10,... | collective-permute-start | bytes 196616 | tf_op jit(solution)/shard_map/ppermute | solution.py:14
  43.2 1.0 %collective-permute-done.15 = f32[128,128]{1,0:T(8,128)S(1)} collective-permute-done((f32[128,128]{1,0:T(8,128)S(1)}, f32[128,128]{1,0:T(8,128)S(1)}, u32[]{:S(2)}, u32[]{:S(2)}) %collective-permute-start.15) | collective-permute-done | bytes 65568 | tf_op jit(solution)/shard_map/ppermute | solution.py:14
  44.2 2.7 %collective-permute-done.14 = f32[128,128]{1,0:T(8,128)S(1)} collective-permute-done((f32[128,128]{1,0:T(8,128)S(1)}, f32[128,128]{1,0:T(8,128)S(1)}, u32[]{:S(2)}, u32[]{:S(2)}) %collective-permute-start.14) | collective-permute-done | bytes 65568 | tf_op jit(solution)/shard_map/ppermute | solution.py:14
  46.9 0.9 %add_add_fusion = f32[128,128]{1,0:T(8,128)S(1)} fusion(f32[128,128]{1,0:T(8,128)S(1)} %collective-permute-done.15, f32[128,128]{1,0:T(8,128)S(1)} %collective-permute-done.14, f32[128,128]{1,0:T(8,128)S(1)} %collective-permute-done.13, f32[512,128]{1,0:T(8,128)} %copy-done.2, s32[]{:T(128)S(6)} %select_n.48), kind=kLoop, calls=%fused_computation.23 | loop fusion | flops 49152 | bytes 327684 | tf_op jit(solution)/shard_map/add | solution.py:163
  48.3 2.7 %collective-permute-start.17 = (f32[128,128]{1,0:T(8,128)S(1)}, f32[128,128]{1,0:T(8,128)S(1)}, u32[]{:S(2)}, u32[]{:S(2)}) collective-permute-start(f32[128,128]{1,0:T(8,128)S(1)} %add_add_fusion), channel_id=1, source_target_pairs={{0,2},{1,3},{2,0},{3,1},{4,6},{5,7},{6,4},{7,5},{8,10},{9,11},{10,... | collective-permute-start | bytes 196616 | tf_op jit(solution)/shard_map/ppermute | solution.py:14
  51.0 1.3 %collective-permute-start.18 = (f32[128,128]{1,0:T(8,128)S(1)}, f32[128,128]{1,0:T(8,128)S(1)}, u32[]{:S(2)}, u32[]{:S(2)}) collective-permute-start(f32[128,128]{1,0:T(8,128)S(1)} %add_add_fusion), channel_id=1, source_target_pairs={{0,3},{1,2},{2,1},{3,0},{4,7},{5,6},{6,5},{7,4},{8,11},{9,10},{10,... | collective-permute-start | bytes 196616 | tf_op jit(solution)/shard_map/ppermute | solution.py:14
  52.2 3.9 %inverse_factor.1 = f32[128,128]{1,0:T(8,128)S(1)} custom-call(f32[128,128]{1,0:T(8,128)S(1)} %add.103.gram_ref, f32[128,128]{1,0:T(8,128)S(1)} %collective-permute-done.12.other_ref), custom_call_target="tpu_custom_call" | custom-call | flops 6000000000 | bytes 131072 | tf_op jit(solution)/shard_map/inverse_factor/pallas_call | solution.py:97
  56.3 0.8 %collective-permute-done.18 = f32[128,128]{1,0:T(8,128)S(1)} collective-permute-done((f32[128,128]{1,0:T(8,128)S(1)}, f32[128,128]{1,0:T(8,128)S(1)}, u32[]{:S(2)}, u32[]{:S(2)}) %collective-permute-start.18) | collective-permute-done | bytes 65568 | tf_op jit(solution)/shard_map/ppermute | solution.py:14
  57.5 1.5 %collective-permute-start.21 = (bf16[512,128]{1,0:T(8,128)(2,1)S(1)}, bf16[512,128]{1,0:T(8,128)(2,1)S(1)}, u32[]{:S(2)}, u32[]{:S(2)}) collective-permute-start(bf16[512,128]{1,0:T(8,128)(2,1)S(1)} %convert_element_type.22), channel_id=1, source_target_pairs={{0,24},{4,28},{8,16},{12,20},{16,8},{20,12},{24,0},{28,4},{1,25},{... | collective-permute-start | bytes 393224 | tf_op jit(solution)/shard_map/ppermute | solution.py:14
  59.6 1.4 %collective-permute-start.19 = (bf16[512,128]{1,0:T(8,128)(2,1)S(1)}, bf16[512,128]{1,0:T(8,128)(2,1)S(1)}, u32[]{:S(2)}, u32[]{:S(2)}) collective-permute-start(bf16[512,128]{1,0:T(8,128)(2,1)S(1)} %convert_element_type.22), channel_id=1, source_target_pairs={{0,8},{4,12},{8,0},{12,4},{16,24},{20,28},{24,16},{28,20},{1,9},{5... | collective-permute-start | bytes 393224 | tf_op jit(solution)/shard_map/ppermute | solution.py:14
  61.0 2.5 %collective-permute-done.21 = bf16[512,128]{1,0:T(8,128)(2,1)S(1)} collective-permute-done((bf16[512,128]{1,0:T(8,128)(2,1)S(1)}, bf16[512,128]{1,0:T(8,128)(2,1)S(1)}, u32[]{:S(2)}, u32[]{:S(2)}) %collective-permute-start.21) | collective-permute-done | bytes 131104 | tf_op jit(solution)/shard_map/ppermute | solution.py:14
  63.5 1.3 %collective-permute-done.20 = bf16[512,128]{1,0:T(8,128)(2,1)S(1)} collective-permute-done((bf16[512,128]{1,0:T(8,128)(2,1)S(1)}, bf16[512,128]{1,0:T(8,128)(2,1)S(1)}, u32[]{:S(2)}, u32[]{:S(2)}) %collective-permute-start.20) | collective-permute-done | bytes 131104 | tf_op jit(solution)/shard_map/ppermute | solution.py:14
  65.6 0.9 %multiply_reduce_fusion.1 = f32[512]{0:T(512)S(1)} fusion(bf16[512,2048]{1,0:T(8,128)(2,1)S(1)} %copy-done.1, f32[512,128]{1,0:T(8,128)S(1)} %fusion.8, bf16[512,128]{1,0:T(8,128)(2,1)S(1)} %collective-permute-done.21, bf16[512,128]{1,0:T(8,128)(2,1)S(1)} %collective-permute-done.20, bf16[512,128]{1,0:T(8,128)(2,1)S(1)} %collective-permute-done.19, ...), kind=kOutput, calls=%fused_computation.1 | convolution fusion | flops 275840512 | bytes 2885632 | tf_op jit(solution)/shard_map/dot_general | solution.py:189
  66.8 0.9 %multiply_reduce_fusion = f32[512]{0:T(512)S(1)} fusion(bf16[512,2048]{1,0:T(8,128)(2,1)S(1)} %get-tuple-element.17, bf16[2048,128]{1,0:T(8,128)(2,1)S(1)} %collective-permute-done.22, f32[512,128]{1,0:T(8,128)S(1)} %fusion.8), kind=kOutput, calls=%fused_computation | convolution fusion | flops 273743360 | bytes 2885632 | tf_op jit(solution)/shard_map/dot_general | solution.py:189
  (58 shorter events, 10.3 us)
Async XLA Ops:
  0.6 8.2 %collective-permute-start.2 = (bf16[512,128]{1,0:T(8,128)(2,1)}, bf16[512,128]{1,0:T(8,128)(2,1)S(1)}, u32[]{:S(2)}, u32[]{:S(2)}) collective-permute-start(bf16[512,128]{1,0:T(8,128)(2,1)} %param.3), channel_id=1, source_target_pairs={{0,24},{4,28},{8,16},{12,20},{16,8},{20,12},{24,0},{28,4},{1,25},{... | collective-permute-start | bytes 393224 | tf_op jit(solution)/shard_map/ppermute | solution.py:14
  4.6 6.5 %collective-permute-start.1 = (bf16[512,128]{1,0:T(8,128)(2,1)}, bf16[512,128]{1,0:T(8,128)(2,1)S(1)}, u32[]{:S(2)}, u32[]{:S(2)}) collective-permute-start(bf16[512,128]{1,0:T(8,128)(2,1)} %param.3), channel_id=1, source_target_pairs={{0,16},{4,20},{8,24},{12,28},{16,0},{20,4},{24,8},{28,12},{1,17},{... | collective-permute-start | bytes 393224 | tf_op jit(solution)/shard_map/ppermute | solution.py:14
  5.1 6.3 %collective-permute-start = (bf16[512,128]{1,0:T(8,128)(2,1)}, bf16[512,128]{1,0:T(8,128)(2,1)S(1)}, u32[]{:S(2)}, u32[]{:S(2)}) collective-permute-start(bf16[512,128]{1,0:T(8,128)(2,1)} %param.3), channel_id=1, source_target_pairs={{0,8},{4,12},{8,0},{12,4},{16,24},{20,28},{24,16},{28,20},{1,9},{5... | collective-permute-start | bytes 393224 | tf_op jit(solution)/shard_map/ppermute | solution.py:14
  7.9 3.5 %copy-start.5 = (bf16[512,128]{1,0:T(8,128)(2,1)S(1)}, bf16[512,128]{1,0:T(8,128)(2,1)}, u32[]{:S(2)}) copy-start(bf16[512,128]{1,0:T(8,128)(2,1)} %param.3) | copy-start | bytes 393220
  8.5 7.7 %copy-start = (bf16[512,2048]{1,0:T(8,128)(2,1)}, bf16[512,2048]{1,0:T(8,128)(2,1)S(1)}, u32[]{:S(2)}) copy-start(bf16[512,2048]{1,0:T(8,128)(2,1)S(1)} %get-tuple-element.15) | copy-start | bytes 6291460
  11.4 2.0 %collective-permute-start.3 = (bf16[2048,128]{1,0:T(8,128)(2,1)S(1)}, bf16[2048,128]{1,0:T(8,128)(2,1)S(1)}, u32[]{:S(2)}, u32[]{:S(2)}) collective-permute-start(bf16[2048,128]{1,0:T(8,128)(2,1)S(1)} %pad_maximum_fusion.2), channel_id=1, source_target_pairs={{0,4},{4,0},{8,12},{12,8},{16,20},{20,16},{24,28},{28,24},{1,5},{5... | collective-permute-start | bytes 1572872 | tf_op jit(solution)/shard_map/ppermute | solution.py:14
  14.6 1.3 %collective-permute-start.4 = (f32[128,128]{1,0:T(8,128)S(1)}, f32[128,128]{1,0:T(8,128)S(1)}, u32[]{:S(2)}, u32[]{:S(2)}) collective-permute-start(f32[128,128]{1,0:T(8,128)S(1)} %fusion.16), channel_id=1, source_target_pairs={{0,4},{4,0},{8,12},{12,8},{16,20},{20,16},{24,28},{28,24},{1,5},{5... | collective-permute-start | bytes 196616 | tf_op jit(solution)/shard_map/ppermute | solution.py:14
  16.0 2.7 %collective-permute-start.7 = (f32[2048,128]{1,0:T(8,128)S(1)}, f32[2048,128]{1,0:T(8,128)S(1)}, u32[]{:S(2)}, u32[]{:S(2)}) collective-permute-start(f32[2048,128]{1,0:T(8,128)S(1)} %slice_add_fusion.1), channel_id=1, source_target_pairs={{0,4},{4,0},{8,12},{12,8},{16,20},{20,16},{24,28},{28,24},{1,5},{5... | collective-permute-start | bytes 3145736 | tf_op jit(solution)/shard_map/ppermute | solution.py:14
  19.7 14.0 %collective-permute-start.10 = (f32[512,128]{1,0:T(8,128)}, f32[512,128]{1,0:T(8,128)}, u32[]{:S(2)}, u32[]{:S(2)}) collective-permute-start(f32[512,128]{1,0:T(8,128)} %get-tuple-element.36), channel_id=1, source_target_pairs={{0,16},{4,20},{8,24},{12,28},{16,0},{20,4},{24,8},{28,12},{1,17},{... | collective-permute-start | bytes 786440 | tf_op jit(solution)/shard_map/ppermute | solution.py:14
  21.2 12.5 %collective-permute-start.9 = (f32[512,128]{1,0:T(8,128)}, f32[512,128]{1,0:T(8,128)}, u32[]{:S(2)}, u32[]{:S(2)}) collective-permute-start(f32[512,128]{1,0:T(8,128)} %get-tuple-element.37), channel_id=1, source_target_pairs={{0,8},{4,12},{8,0},{12,4},{16,24},{20,28},{24,16},{28,20},{1,9},{5... | collective-permute-start | bytes 786440 | tf_op jit(solution)/shard_map/ppermute | solution.py:14
  21.9 13.3 %collective-permute-start.8 = (f32[512,128]{1,0:T(8,128)}, f32[512,128]{1,0:T(8,128)}, u32[]{:S(2)}, u32[]{:S(2)}) collective-permute-start(f32[512,128]{1,0:T(8,128)} %get-tuple-element.35), channel_id=1, source_target_pairs={{0,24},{4,28},{8,16},{12,20},{16,8},{20,12},{24,0},{28,4},{1,25},{... | collective-permute-start | bytes 786440 | tf_op jit(solution)/shard_map/ppermute | solution.py:14
  23.2 4.3 %collective-permute-start.5 = (f32[128,128]{1,0:T(8,128)S(1)}, f32[128,128]{1,0:T(8,128)S(1)}, u32[]{:S(2)}, u32[]{:S(2)}) collective-permute-start(f32[128,128]{1,0:T(8,128)S(1)} %add.94), channel_id=1, source_target_pairs={{0,1},{1,0},{2,3},{3,2},{4,5},{5,4},{6,7},{7,6},{8,9},{9,8},{10,11... | collective-permute-start | bytes 196616 | tf_op jit(solution)/shard_map/ppermute | solution.py:14
  27.5 5.3 %collective-permute-start.6 = (f32[128,128]{1,0:T(8,128)S(1)}, f32[128,128]{1,0:T(8,128)}, u32[]{:S(2)}, u32[]{:S(2)}) collective-permute-start(f32[128,128]{1,0:T(8,128)S(1)} %add.96), channel_id=1, source_target_pairs={{0,2},{1,3},{2,0},{3,1},{4,6},{5,7},{6,4},{7,5},{8,10},{9,11},{10,... | collective-permute-start | bytes 196616 | tf_op jit(solution)/shard_map/ppermute | solution.py:14
  36.4 1.6 %copy-start.2 = (f32[512,128]{1,0:T(8,128)}, f32[512,128]{1,0:T(8,128)S(1)}, u32[]{:S(2)}) copy-start(f32[512,128]{1,0:T(8,128)S(1)} %fusion.3) | copy-start | bytes 786436
  36.4 6.1 %collective-permute-start.11 = (f32[128,128]{1,0:T(8,128)S(1)}, f32[128,128]{1,0:T(8,128)S(1)}, u32[]{:S(2)}, u32[]{:S(2)}) collective-permute-start(f32[128,128]{1,0:T(8,128)S(1)} %add.97), channel_id=1, source_target_pairs={{0,8},{4,12},{8,0},{12,4},{16,24},{20,28},{24,16},{28,20},{1,9},{5... | collective-permute-start | bytes 196616 | tf_op jit(solution)/shard_map/ppermute | solution.py:14
  38.0 6.1 %collective-permute-start.15 = (f32[128,128]{1,0:T(8,128)S(1)}, f32[128,128]{1,0:T(8,128)S(1)}, u32[]{:S(2)}, u32[]{:S(2)}) collective-permute-start(f32[128,128]{1,0:T(8,128)S(1)} %get-tuple-element.39), channel_id=1, source_target_pairs={{0,3},{1,2},{2,1},{3,0},{4,7},{5,6},{6,5},{7,4},{8,11},{9,10},{10,... | collective-permute-start | bytes 196616 | tf_op jit(solution)/shard_map/ppermute | solution.py:14
  41.7 5.2 %collective-permute-start.14 = (f32[128,128]{1,0:T(8,128)S(1)}, f32[128,128]{1,0:T(8,128)S(1)}, u32[]{:S(2)}, u32[]{:S(2)}) collective-permute-start(f32[128,128]{1,0:T(8,128)S(1)} %get-tuple-element.40), channel_id=1, source_target_pairs={{0,2},{1,3},{2,0},{3,1},{4,6},{5,7},{6,4},{7,5},{8,10},{9,11},{10,... | collective-permute-start | bytes 196616 | tf_op jit(solution)/shard_map/ppermute | solution.py:14
  41.7 5.2 %collective-permute-start.13 = (f32[128,128]{1,0:T(8,128)S(1)}, f32[128,128]{1,0:T(8,128)S(1)}, u32[]{:S(2)}, u32[]{:S(2)}) collective-permute-start(f32[128,128]{1,0:T(8,128)S(1)} %get-tuple-element.38), channel_id=1, source_target_pairs={{0,1},{1,0},{2,3},{3,2},{4,5},{5,4},{6,7},{7,6},{8,9},{9,8},{10,11... | collective-permute-start | bytes 196616 | tf_op jit(solution)/shard_map/ppermute | solution.py:14
  42.5 5.3 %collective-permute-start.12 = (f32[128,128]{1,0:T(8,128)S(1)}, f32[128,128]{1,0:T(8,128)S(1)}, u32[]{:S(2)}, u32[]{:S(2)}) collective-permute-start(f32[128,128]{1,0:T(8,128)S(1)} %add.103.gram_ref), channel_id=1, source_target_pairs={{0,16},{4,20},{8,24},{12,28},{16,0},{20,4},{24,8},{28,12},{1,17},{... | collective-permute-start | bytes 196616 | tf_op jit(solution)/shard_map/ppermute | solution.py:14
  47.8 8.4 %collective-permute-start.16 = (f32[128,128]{1,0:T(8,128)S(1)}, f32[128,128]{1,0:T(8,128)S(1)}, u32[]{:S(2)}, u32[]{:S(2)}) collective-permute-start(f32[128,128]{1,0:T(8,128)S(1)} %add_add_fusion), channel_id=1, source_target_pairs={{0,1},{1,0},{2,3},{3,2},{4,5},{5,4},{6,7},{7,6},{8,9},{9,8},{10,11... | collective-permute-start | bytes 196616 | tf_op jit(solution)/shard_map/ppermute | solution.py:14
  48.3 7.9 %collective-permute-start.17 = (f32[128,128]{1,0:T(8,128)S(1)}, f32[128,128]{1,0:T(8,128)S(1)}, u32[]{:S(2)}, u32[]{:S(2)}) collective-permute-start(f32[128,128]{1,0:T(8,128)S(1)} %add_add_fusion), channel_id=1, source_target_pairs={{0,2},{1,3},{2,0},{3,1},{4,6},{5,7},{6,4},{7,5},{8,10},{9,11},{10,... | collective-permute-start | bytes 196616 | tf_op jit(solution)/shard_map/ppermute | solution.py:14
  51.0 6.1 %collective-permute-start.18 = (f32[128,128]{1,0:T(8,128)S(1)}, f32[128,128]{1,0:T(8,128)S(1)}, u32[]{:S(2)}, u32[]{:S(2)}) collective-permute-start(f32[128,128]{1,0:T(8,128)S(1)} %add_add_fusion), channel_id=1, source_target_pairs={{0,3},{1,2},{2,1},{3,0},{4,7},{5,6},{6,5},{7,4},{8,11},{9,10},{10,... | collective-permute-start | bytes 196616 | tf_op jit(solution)/shard_map/ppermute | solution.py:14
  56.1 9.4 %copy-start.1 = (bf16[512,2048]{1,0:T(8,128)(2,1)S(1)}, bf16[512,2048]{1,0:T(8,128)(2,1)}, u32[]{:S(2)}) copy-start(bf16[512,2048]{1,0:T(8,128)(2,1)} %copy-done) | copy-start | bytes 6291460
  57.4 9.1 %copy-start.3 = (f32[512,128]{1,0:T(8,128)}, f32[512,128]{1,0:T(8,128)S(1)}, u32[]{:S(2)}) copy-start(f32[512,128]{1,0:T(8,128)S(1)} %fusion.6) | copy-start | bytes 786436
  57.5 6.0 %collective-permute-start.21 = (bf16[512,128]{1,0:T(8,128)(2,1)S(1)}, bf16[512,128]{1,0:T(8,128)(2,1)S(1)}, u32[]{:S(2)}, u32[]{:S(2)}) collective-permute-start(bf16[512,128]{1,0:T(8,128)(2,1)S(1)} %convert_element_type.22), channel_id=1, source_target_pairs={{0,24},{4,28},{8,16},{12,20},{16,8},{20,12},{24,0},{28,4},{1,25},{... | collective-permute-start | bytes 393224 | tf_op jit(solution)/shard_map/ppermute | solution.py:14
  58.9 5.9 %collective-permute-start.20 = (bf16[512,128]{1,0:T(8,128)(2,1)S(1)}, bf16[512,128]{1,0:T(8,128)(2,1)S(1)}, u32[]{:S(2)}, u32[]{:S(2)}) collective-permute-start(bf16[512,128]{1,0:T(8,128)(2,1)S(1)} %convert_element_type.22), channel_id=1, source_target_pairs={{0,16},{4,20},{8,24},{12,28},{16,0},{20,4},{24,8},{28,12},{1,17},{... | collective-permute-start | bytes 393224 | tf_op jit(solution)/shard_map/ppermute | solution.py:14
  59.6 5.2 %collective-permute-start.19 = (bf16[512,128]{1,0:T(8,128)(2,1)S(1)}, bf16[512,128]{1,0:T(8,128)(2,1)S(1)}, u32[]{:S(2)}, u32[]{:S(2)}) collective-permute-start(bf16[512,128]{1,0:T(8,128)(2,1)S(1)} %convert_element_type.22), channel_id=1, source_target_pairs={{0,8},{4,12},{8,0},{12,4},{16,24},{20,28},{24,16},{28,20},{1,9},{5... | collective-permute-start | bytes 393224 | tf_op jit(solution)/shard_map/ppermute | solution.py:14
  64.9 2.0 %collective-permute-start.22 = (bf16[2048,128]{1,0:T(8,128)(2,1)S(1)}, bf16[2048,128]{1,0:T(8,128)(2,1)S(1)}, u32[]{:S(2)}, u32[]{:S(2)}) collective-permute-start(bf16[2048,128]{1,0:T(8,128)(2,1)S(1)} %pad_maximum_fusion.3), channel_id=1, source_target_pairs={{0,4},{4,0},{8,12},{12,8},{16,20},{20,16},{24,28},{28,24},{1,5},{5... | collective-permute-start | bytes 1572872 | tf_op jit(solution)/shard_map/ppermute | solution.py:14
  65.5 1.3 %copy-start.4 = (f32[512,128]{1,0:T(8,128)}, f32[512,128]{1,0:T(8,128)S(1)}, u32[]{:S(2)}) copy-start(f32[512,128]{1,0:T(8,128)S(1)} %fusion.8) | copy-start | bytes 786436

commit v7 on v6

--- a/solution.py
+++ b/solution.py
@@ -144,9 +144,8 @@
         twice = lax.dot_general(side, both, (((0,), (0,)), ((), ())), preferred_element_type=jnp.float32)
         return twice[:, :rank] + twice[:, rank:]
 
-    gram, both = lax.optimization_barrier((gram, both))
-    gram, odd_pieces = lax.optimization_barrier((gram + flipped(gram, "inner", 1), products(odd_columns)))
-    pieces = products(even_columns) + flipped(odd_pieces, "inner", 1)
+    gram = gram + flipped(gram, "inner", 1)
+    pieces = products(even_columns) + flipped(products(odd_columns), "inner", 1)
     pieces = pieces.reshape(inner // 2, piece, rank)
     for level in range(outer.bit_length() - 1):
         gram = gram + flipped(gram, "outer", 1 << level)
@@ -158,16 +157,16 @@
     for level in range(1, levels - 1):
         gram = gram + flipped(gram, "inner", 1 << level)
     last = flipped(gram, "inner", 1 << (levels - 1))
-    share = lax.dynamic_slice_in_dim(own, mine * part, part, 0)
+    parts = [lax.dynamic_slice_in_dim(own, (mine ^ mask) * part, part, 0) for mask in range(outer)]
+    parts = lax.optimization_barrier(parts)
+    share = parts[0]
     for mask in range(1, outer):
-        share = share + flipped(
-            lax.dynamic_slice_in_dim(own, (mine ^ mask) * part, part, 0), "outer", mask
-        )
+        share = share + flipped(parts[mask], "outer", mask)
     gram, last, share = lax.optimization_barrier((gram, last, share))
 
     summed = jnp.zeros((piece, rank), jnp.float32)
     summed = lax.dynamic_update_slice_in_dim(summed, share, mine * part, 0)
-    for mask in range(1, outer):
+    for mask in reversed(range(1, outer)):
         summed = lax.dynamic_update_slice_in_dim(
             summed, flipped(share, "outer", mask), (mine ^ mask) * part, 0
         )

time: 68.6 us -> 66.4 us (0.968)
  other arithmetic: 4.46 us -> 2.76 us
    add x3, other arithmetic: 1 us -> 0.16 us  [the longest x1 0.14 us: local(): pieces = products(even_columns) + flipped(products(odd_columns), 'inner', 1)]
    add x2, other arithmetic: 0.86 us -> 0.02 us  [local(): gram = gram + flipped(gram, 'outer', 1 << level)]
  transfers between devices with their start and end apart: 23 -> 23, of which waited for: 15 -> 15; matrix products, arithmetic and copies ran while one was open for 13% -> 10% of each run, Pallas kernels for 6% -> 6%
where the time goes in v7:
time: 66.4 us; the launch traced here: 66.3 us
  starting transfers between devices  27.5 us (41%)
  waiting for transfers between devices  21.1 us (32%)
  matrix products  6.43 us (10%)
  Pallas kernels  3.9 us (6%)
  local copies, waits for them, and re-layouts  3.62 us (5%)
  other arithmetic  2.76 us (4%)
  between operations  0.93 us (1%)
    ppermute x23, starting transfers between devices, flipped(): lax.ppermute(block, axis, [(low, low ^ mask) for low in range(count)])  27.5 us
    ppermute x23, waiting for transfers between devices, flipped(): lax.ppermute(block, axis, [(low, low ^ mask) for low in range(count)])  21.1 us
    pallas_call x1, Pallas kernels, inverse_factor(): pl.pallas_call(factor_kernel, out_shape=jax.ShapeDtypeStruct((n, n), jnp....  3.9 us
    dynamic_slice x1, local copies, waits for them, and re-layouts, columns(): lax.dynamic_slice_in_dim(samples, (me ^ mask) * piece, piece, 1)  2.63 us
    dot_general x2, matrix products, errors(): lax.dot_general(basis_low, factor, (((1,), (1,)), ((), ())), preferred_el...  1.87 us
    dot_general x2, matrix products, products(): lax.dot_general(side, both, (((0,), (0,)), ((), ())), preferred_element_t...  1.53 us
    dot_general x3, matrix products, exact_dot(): lax.dot_general(a, b, (contract, ((), ())), precision=lax.Precision.HIGHE...  1.34 us
  transfers between devices with their start and end apart: 23, of which 15 were waited for; matrix products, arithmetic and copies ran while one was open for 10% of the time, Pallas kernels for 6%

profile of v7, /device:TPU:0, one launch (start us, length us, event | category | flops | bytes accessed | tf_op | source)
XLA Modules:
  0.0 66.3 jit_solution(17059695384057450383)
XLA Ops:
  0.6 4.0 %collective-permute-start.2 = (bf16[512,128]{1,0:T(8,128)(2,1)}, bf16[512,128]{1,0:T(8,128)(2,1)S(1)}, u32[]{:S(2)}, u32[]{:S(2)}) collective-permute-start(bf16[512,128]{1,0:T(8,128)(2,1)} %param.3), channel_id=1, source_target_pairs={{0,24},{4,28},{8,16},{12,20},{16,8},{20,12},{24,0},{28,4},{1,25},{... | collective-permute-start | bytes 393224 | tf_op jit(solution)/shard_map/ppermute | solution.py:14
  5.2 2.6 %constant_dynamic-slice_fusion.7 = (bf16[512,512]{1,0:T(8,128)(2,1)S(1)}, bf16[512,512]{1,0:T(8,128)(2,1)S(1)}, bf16[512,512]{1,0:T(8,128)(2,1)S(1)}, bf16[512,5...) fusion(bf16[512,4096]{1,0:T(8,128)(2,1)} %param.2, ...), kind=kLoop, calls=%fused_computation.39 | loop fusion | bytes 8388640 | tf_op jit(solution)/shard_map/dynamic_slice | solution.py:127
  8.8 2.3 %collective-permute-done.1 = bf16[512,128]{1,0:T(8,128)(2,1)S(1)} collective-permute-done((bf16[512,128]{1,0:T(8,128)(2,1)}, bf16[512,128]{1,0:T(8,128)(2,1)S(1)}, u32[]{:S(2)}, u32[]{:S(2)}) %collective-permute-start.1) | collective-permute-done | bytes 131104 | tf_op jit(solution)/shard_map/ppermute | solution.py:14
  11.5 0.8 %fusion.19 = f32[512,128]{0,1:T(8,128)S(1)} fusion(bf16[512,2048]{1,0:T(8,128)(2,1)S(1)} %get-tuple-element.15, bf16[2048,128]{1,0:T(8,128)(2,1)S(1)} %pad_maximum_fusion.2), kind=kOutput, calls=%fused_computation.50 | convolution fusion | flops 268435456 | bytes 2883584 | tf_op jit(solution)/shard_map/dot_general | solution.py:134
  12.3 1.1 %collective-permute-done.3 = bf16[2048,128]{1,0:T(8,128)(2,1)S(1)} collective-permute-done((bf16[2048,128]{1,0:T(8,128)(2,1)S(1)}, bf16[2048,128]{1,0:T(8,128)(2,1)S(1)}, u32[]{:S(2)}, u32[]{:S(2)}) %collective-permute-start.3) | collective-permute-done | bytes 524320 | tf_op jit(solution)/shard_map/ppermute | solution.py:14
  13.4 0.8 %reduce-precision_convert_fusion = (bf16[512,128]{0,1:T(8,128)(2,1)S(1)}, bf16[512,128]{0,1:T(8,128)(2,1)S(1)}, f32[512,128]{0,1:T(8,128)S(1)}) fusion(f32[512,128]{0,1:T(8,128)S(1)} %fusion.19, bf16[512,2048]{1,0:T(8,128)(2,1)S(1)} %get-tuple-element.17, bf16[2048,128]{1,0:T(8,128)(2,1)S(1)} %collective-permute-done.3), kind=kOutput, calls=%fused_computation.11 | convolution fusion | flops 268763136 | bytes 3407872 | tf_op jit(solution)/shard_map/dot_general | solution.py:135
  14.2 0.8 %fusion.4 = f32[2048,256]{1,0:T(8,128)S(1)} fusion(bf16[512,2048]{1,0:T(8,128)(2,1)S(1)} %get-tuple-element.17, bf16[512,128]{0,1:T(8,128)(2,1)S(1)} %get-tuple-element.43, bf16[512,128]{0,1:T(8,128)(2,1)S(1)} %get-tuple-element.42), kind=kOutput, calls=%fused_computation.17 | convolution fusion | flops 537395200 | bytes 4456448 | tf_op jit(solution)/shard_map/dot_general | solution.py:144
  15.3 0.8 %fusion.5 = f32[2048,256]{1,0:T(8,128)S(1)} fusion(bf16[512,2048]{1,0:T(8,128)(2,1)S(1)} %get-tuple-element.15, bf16[512,128]{0,1:T(8,128)(2,1)S(1)} %get-tuple-element.43, bf16[512,128]{0,1:T(8,128)(2,1)S(1)} %get-tuple-element.42), kind=kOutput, calls=%fused_computation.18 | convolution fusion | flops 537395200 | bytes 4456448 | tf_op jit(solution)/shard_map/dot_general | solution.py:144
  16.1 1.7 %collective-permute-done.7 = f32[2048,128]{1,0:T(8,128)S(1)} collective-permute-done((f32[2048,128]{1,0:T(8,128)S(1)}, f32[2048,128]{1,0:T(8,128)S(1)}, u32[]{:S(2)}, u32[]{:S(2)}) %collective-permute-start.7) | collective-permute-done | bytes 1048608 | tf_op jit(solution)/shard_map/ppermute | solution.py:14
  18.0 0.9 %fusion.18 = (f32[512,128]{1,0:T(8,128)}, f32[512,128]{1,0:T(8,128)}, f32[512,128]{1,0:T(8,128)}) fusion(f32[2048,128]{1,0:T(8,128)S(1)} %fusion), kind=kLoop, calls=%fused_computation.49 | loop fusion | bytes 1572864 | tf_op jit(solution)/shard_map/slice | solution.py:154
  18.9 1.5 %collective-permute-start.10 = (f32[512,128]{1,0:T(8,128)}, f32[512,128]{1,0:T(8,128)}, u32[]{:S(2)}, u32[]{:S(2)}) collective-permute-start(f32[512,128]{1,0:T(8,128)} %get-tuple-element.36), channel_id=1, source_target_pairs={{0,16},{4,20},{8,24},{12,28},{16,0},{20,4},{24,8},{28,12},{1,17},{... | collective-permute-start | bytes 786440 | tf_op jit(solution)/shard_map/ppermute | solution.py:14
  21.0 1.3 %collective-permute-start.8 = (f32[512,128]{1,0:T(8,128)}, f32[512,128]{1,0:T(8,128)}, u32[]{:S(2)}, u32[]{:S(2)}) collective-permute-start(f32[512,128]{1,0:T(8,128)} %get-tuple-element.35), channel_id=1, source_target_pairs={{0,24},{4,28},{8,16},{12,20},{16,8},{20,12},{24,0},{28,4},{1,25},{... | collective-permute-start | bytes 786440 | tf_op jit(solution)/shard_map/ppermute | solution.py:14
  22.8 1.2 %collective-permute-done.4 = f32[128,128]{1,0:T(8,128)S(1)} collective-permute-done((f32[128,128]{1,0:T(8,128)S(1)}, f32[128,128]{1,0:T(8,128)S(1)}, u32[]{:S(2)}, u32[]{:S(2)}) %collective-permute-start.4) | collective-permute-done | bytes 65568 | tf_op jit(solution)/shard_map/ppermute | solution.py:14
  24.1 1.6 %collective-permute-start.5 = (f32[128,128]{1,0:T(8,128)S(1)}, f32[128,128]{1,0:T(8,128)S(1)}, u32[]{:S(2)}, u32[]{:S(2)}) collective-permute-start(f32[128,128]{1,0:T(8,128)S(1)} %add.94), channel_id=1, source_target_pairs={{0,1},{1,0},{2,3},{3,2},{4,5},{5,4},{6,7},{7,6},{8,9},{9,8},{10,11... | collective-permute-start | bytes 196616 | tf_op jit(solution)/shard_map/ppermute | solution.py:14
  25.7 2.7 %collective-permute-done.5 = f32[128,128]{1,0:T(8,128)S(1)} collective-permute-done((f32[128,128]{1,0:T(8,128)S(1)}, f32[128,128]{1,0:T(8,128)S(1)}, u32[]{:S(2)}, u32[]{:S(2)}) %collective-permute-start.5) | collective-permute-done | bytes 65568 | tf_op jit(solution)/shard_map/ppermute | solution.py:14
  28.4 2.7 %collective-permute-start.6 = (f32[128,128]{1,0:T(8,128)S(1)}, f32[128,128]{1,0:T(8,128)S(1)}, u32[]{:S(2)}, u32[]{:S(2)}) collective-permute-start(f32[128,128]{1,0:T(8,128)S(1)} %add.95), channel_id=1, source_target_pairs={{0,2},{1,3},{2,0},{3,1},{4,6},{5,7},{6,4},{7,5},{8,10},{9,11},{10,... | collective-permute-start | bytes 196616 | tf_op jit(solution)/shard_map/ppermute | solution.py:14
  31.1 2.7 %collective-permute-done.6 = f32[128,128]{1,0:T(8,128)S(1)} collective-permute-done((f32[128,128]{1,0:T(8,128)S(1)}, f32[128,128]{1,0:T(8,128)S(1)}, u32[]{:S(2)}, u32[]{:S(2)}) %collective-permute-start.6) | collective-permute-done | bytes 65568 | tf_op jit(solution)/shard_map/ppermute | solution.py:14
  34.3 1.2 %fusion.3 = f32[512,128]{1,0:T(8,128)S(1)} fusion(f32[512,128]{1,0:T(8,128)} %collective-permute-done.10, f32[512,128]{1,0:T(8,128)} %collective-permute-done.9, f32[512,128]{1,0:T(8,128)} %collective-permute-done.8, f32[2048,128]{1,0:T(8,128)S(1)} %fusion), kind=kLoop, calls=%fused_computation.15 | loop fusion | flops 196608 | bytes 1310720 | tf_op jit(solution)/shard_map/add | solution.py:154
  35.5 1.6 %collective-permute-start.11 = (f32[128,128]{1,0:T(8,128)S(1)}, f32[128,128]{1,0:T(8,128)S(1)}, u32[]{:S(2)}, u32[]{:S(2)}) collective-permute-start(f32[128,128]{1,0:T(8,128)S(1)} %add.96), channel_id=1, source_target_pairs={{0,8},{4,12},{8,0},{12,4},{16,24},{20,28},{24,16},{28,20},{1,9},{5... | collective-permute-start | bytes 196616 | tf_op jit(solution)/shard_map/ppermute | solution.py:14
  37.1 3.7 %collective-permute-start.15 = (f32[128,128]{1,0:T(8,128)S(1)}, f32[128,128]{1,0:T(8,128)S(1)}, u32[]{:S(2)}, u32[]{:S(2)}) collective-permute-start(f32[128,128]{1,0:T(8,128)S(1)} %get-tuple-element.23), channel_id=1, source_target_pairs={{0,3},{1,2},{2,1},{3,0},{4,7},{5,6},{6,5},{7,4},{8,11},{9,10},{10,... | collective-permute-start | bytes 196616 | tf_op jit(solution)/shard_map/ppermute | solution.py:14
  40.8 0.8 %collective-permute-start.13 = (f32[128,128]{1,0:T(8,128)S(1)}, f32[128,128]{1,0:T(8,128)S(1)}, u32[]{:S(2)}, u32[]{:S(2)}) collective-permute-start(f32[128,128]{1,0:T(8,128)S(1)} %get-tuple-element.21), channel_id=1, source_target_pairs={{0,1},{1,0},{2,3},{3,2},{4,5},{5,4},{6,7},{7,6},{8,9},{9,8},{10,11... | collective-permute-start | bytes 196616 | tf_op jit(solution)/shard_map/ppermute | solution.py:14
  42.3 1.0 %collective-permute-done.15 = f32[128,128]{1,0:T(8,128)S(1)} collective-permute-done((f32[128,128]{1,0:T(8,128)S(1)}, f32[128,128]{1,0:T(8,128)S(1)}, u32[]{:S(2)}, u32[]{:S(2)}) %collective-permute-start.15) | collective-permute-done | bytes 65568 | tf_op jit(solution)/shard_map/ppermute | solution.py:14
  43.3 2.7 %collective-permute-done.14 = f32[128,128]{1,0:T(8,128)S(1)} collective-permute-done((f32[128,128]{1,0:T(8,128)S(1)}, f32[128,128]{1,0:T(8,128)S(1)}, u32[]{:S(2)}, u32[]{:S(2)}) %collective-permute-start.14) | collective-permute-done | bytes 65568 | tf_op jit(solution)/shard_map/ppermute | solution.py:14
  46.0 3.5 %collective-permute-start.16 = (f32[128,128]{1,0:T(8,128)S(1)}, f32[128,128]{1,0:T(8,128)S(1)}, u32[]{:S(2)}, u32[]{:S(2)}) collective-permute-start(f32[128,128]{1,0:T(8,128)S(1)} %add_add_fusion), channel_id=1, source_target_pairs={{0,3},{1,2},{2,1},{3,0},{4,7},{5,6},{6,5},{7,4},{8,11},{9,10},{10,... | collective-permute-start | bytes 196616 | tf_op jit(solution)/shard_map/ppermute | solution.py:14
  49.5 1.0 %collective-permute-start.18 = (f32[128,128]{1,0:T(8,128)S(1)}, f32[128,128]{1,0:T(8,128)S(1)}, u32[]{:S(2)}, u32[]{:S(2)}) collective-permute-start(f32[128,128]{1,0:T(8,128)S(1)} %add_add_fusion), channel_id=1, source_target_pairs={{0,1},{1,0},{2,3},{3,2},{4,5},{5,4},{6,7},{7,6},{8,9},{9,8},{10,11... | collective-permute-start | bytes 196616 | tf_op jit(solution)/shard_map/ppermute | solution.py:14
  50.5 3.9 %inverse_factor.1 = f32[128,128]{1,0:T(8,128)S(1)} custom-call(f32[128,128]{1,0:T(8,128)S(1)} %add.103.gram_ref, f32[128,128]{1,0:T(8,128)S(1)} %collective-permute-done.12.other_ref), custom_call_target="tpu_custom_call" | custom-call | flops 6000000000 | bytes 131072 | tf_op jit(solution)/shard_map/inverse_factor/pallas_call | solution.py:97
  55.1 1.5 %collective-permute-start.21 = (bf16[512,128]{1,0:T(8,128)(2,1)S(1)}, bf16[512,128]{1,0:T(8,128)(2,1)S(1)}, u32[]{:S(2)}, u32[]{:S(2)}) collective-permute-start(bf16[512,128]{1,0:T(8,128)(2,1)S(1)} %convert_element_type.22), channel_id=1, source_target_pairs={{0,24},{4,28},{8,16},{12,20},{16,8},{20,12},{24,0},{28,4},{1,25},{... | collective-permute-start | bytes 393224 | tf_op jit(solution)/shard_map/ppermute | solution.py:14
  57.2 1.5 %collective-permute-start.19 = (bf16[512,128]{1,0:T(8,128)(2,1)S(1)}, bf16[512,128]{1,0:T(8,128)(2,1)S(1)}, u32[]{:S(2)}, u32[]{:S(2)}) collective-permute-start(bf16[512,128]{1,0:T(8,128)(2,1)S(1)} %convert_element_type.22), channel_id=1, source_target_pairs={{0,8},{4,12},{8,0},{12,4},{16,24},{20,28},{24,16},{28,20},{1,9},{5... | collective-permute-start | bytes 393224 | tf_op jit(solution)/shard_map/ppermute | solution.py:14
  58.7 2.8 %collective-permute-done.21 = bf16[512,128]{1,0:T(8,128)(2,1)S(1)} collective-permute-done((bf16[512,128]{1,0:T(8,128)(2,1)S(1)}, bf16[512,128]{1,0:T(8,128)(2,1)S(1)}, u32[]{:S(2)}, u32[]{:S(2)}) %collective-permute-start.21) | collective-permute-done | bytes 131104 | tf_op jit(solution)/shard_map/ppermute | solution.py:14
  61.5 1.2 %collective-permute-done.20 = bf16[512,128]{1,0:T(8,128)(2,1)S(1)} collective-permute-done((bf16[512,128]{1,0:T(8,128)(2,1)S(1)}, bf16[512,128]{1,0:T(8,128)(2,1)S(1)}, u32[]{:S(2)}, u32[]{:S(2)}) %collective-permute-start.20) | collective-permute-done | bytes 131104 | tf_op jit(solution)/shard_map/ppermute | solution.py:14
  63.5 0.9 %multiply_reduce_fusion.1 = f32[512]{0:T(512)S(1)} fusion(bf16[512,2048]{1,0:T(8,128)(2,1)S(1)} %copy-done.1, f32[512,128]{1,0:T(8,128)S(1)} %fusion.10, bf16[512,128]{1,0:T(8,128)(2,1)S(1)} %collective-permute-done.21, bf16[512,128]{1,0:T(8,128)(2,1)S(1)} %collective-permute-done.20, bf16[512,128]{1,0:T(8,128)(2,1)S(1)} %collective-permute-done.19, ...), kind=kOutput, calls=%fused_computation.1 | convolution fusion | flops 275840512 | bytes 2885632 | tf_op jit(solution)/shard_map/dot_general | solution.py:188
  64.8 0.9 %multiply_reduce_fusion = f32[512]{0:T(512)S(1)} fusion(bf16[512,2048]{1,0:T(8,128)(2,1)S(1)} %get-tuple-element.17, bf16[2048,128]{1,0:T(8,128)(2,1)S(1)} %collective-permute-done.22, f32[512,128]{1,0:T(8,128)S(1)} %fusion.10), kind=kOutput, calls=%fused_computation | convolution fusion | flops 273743360 | bytes 2885632 | tf_op jit(solution)/shard_map/dot_general | solution.py:188
  (55 shorter events, 7.6 us)
Async XLA Ops:
  0.6 8.2 %collective-permute-start.2 = (bf16[512,128]{1,0:T(8,128)(2,1)}, bf16[512,128]{1,0:T(8,128)(2,1)S(1)}, u32[]{:S(2)}, u32[]{:S(2)}) collective-permute-start(bf16[512,128]{1,0:T(8,128)(2,1)} %param.3), channel_id=1, source_target_pairs={{0,24},{4,28},{8,16},{12,20},{16,8},{20,12},{24,0},{28,4},{1,25},{... | collective-permute-start | bytes 393224 | tf_op jit(solution)/shard_map/ppermute | solution.py:14
  4.6 6.5 %collective-permute-start.1 = (bf16[512,128]{1,0:T(8,128)(2,1)}, bf16[512,128]{1,0:T(8,128)(2,1)S(1)}, u32[]{:S(2)}, u32[]{:S(2)}) collective-permute-start(bf16[512,128]{1,0:T(8,128)(2,1)} %param.3), channel_id=1, source_target_pairs={{0,16},{4,20},{8,24},{12,28},{16,0},{20,4},{24,8},{28,12},{1,17},{... | collective-permute-start | bytes 393224 | tf_op jit(solution)/shard_map/ppermute | solution.py:14
  5.1 6.3 %collective-permute-start = (bf16[512,128]{1,0:T(8,128)(2,1)}, bf16[512,128]{1,0:T(8,128)(2,1)S(1)}, u32[]{:S(2)}, u32[]{:S(2)}) collective-permute-start(bf16[512,128]{1,0:T(8,128)(2,1)} %param.3), channel_id=1, source_target_pairs={{0,8},{4,12},{8,0},{12,4},{16,24},{20,28},{24,16},{28,20},{1,9},{5... | collective-permute-start | bytes 393224 | tf_op jit(solution)/shard_map/ppermute | solution.py:14
  7.9 3.5 %copy-start.4 = (bf16[512,128]{1,0:T(8,128)(2,1)S(1)}, bf16[512,128]{1,0:T(8,128)(2,1)}, u32[]{:S(2)}) copy-start(bf16[512,128]{1,0:T(8,128)(2,1)} %param.3) | copy-start | bytes 393220
  8.5 6.8 %copy-start = (bf16[512,2048]{1,0:T(8,128)(2,1)}, bf16[512,2048]{1,0:T(8,128)(2,1)S(1)}, u32[]{:S(2)}) copy-start(bf16[512,2048]{1,0:T(8,128)(2,1)S(1)} %get-tuple-element.15) | copy-start | bytes 6291460
  11.4 2.0 %collective-permute-start.3 = (bf16[2048,128]{1,0:T(8,128)(2,1)S(1)}, bf16[2048,128]{1,0:T(8,128)(2,1)S(1)}, u32[]{:S(2)}, u32[]{:S(2)}) collective-permute-start(bf16[2048,128]{1,0:T(8,128)(2,1)S(1)} %pad_maximum_fusion.2), channel_id=1, source_target_pairs={{0,4},{4,0},{8,12},{12,8},{16,20},{20,16},{24,28},{28,24},{1,5},{5... | collective-permute-start | bytes 1572872 | tf_op jit(solution)/shard_map/ppermute | solution.py:14
  15.1 2.7 %collective-permute-start.7 = (f32[2048,128]{1,0:T(8,128)S(1)}, f32[2048,128]{1,0:T(8,128)S(1)}, u32[]{:S(2)}, u32[]{:S(2)}) collective-permute-start(f32[2048,128]{1,0:T(8,128)S(1)} %slice_add_fusion), channel_id=1, source_target_pairs={{0,4},{4,0},{8,12},{12,8},{16,20},{20,16},{24,28},{28,24},{1,5},{5... | collective-permute-start | bytes 3145736 | tf_op jit(solution)/shard_map/ppermute | solution.py:14
  18.9 14.9 %collective-permute-start.10 = (f32[512,128]{1,0:T(8,128)}, f32[512,128]{1,0:T(8,128)}, u32[]{:S(2)}, u32[]{:S(2)}) collective-permute-start(f32[512,128]{1,0:T(8,128)} %get-tuple-element.36), channel_id=1, source_target_pairs={{0,16},{4,20},{8,24},{12,28},{16,0},{20,4},{24,8},{28,12},{1,17},{... | collective-permute-start | bytes 786440 | tf_op jit(solution)/shard_map/ppermute | solution.py:14
  20.3 13.5 %collective-permute-start.9 = (f32[512,128]{1,0:T(8,128)}, f32[512,128]{1,0:T(8,128)}, u32[]{:S(2)}, u32[]{:S(2)}) collective-permute-start(f32[512,128]{1,0:T(8,128)} %get-tuple-element.37), channel_id=1, source_target_pairs={{0,8},{4,12},{8,0},{12,4},{16,24},{20,28},{24,16},{28,20},{1,9},{5... | collective-permute-start | bytes 786440 | tf_op jit(solution)/shard_map/ppermute | solution.py:14
  21.0 13.3 %collective-permute-start.8 = (f32[512,128]{1,0:T(8,128)}, f32[512,128]{1,0:T(8,128)}, u32[]{:S(2)}, u32[]{:S(2)}) collective-permute-start(f32[512,128]{1,0:T(8,128)} %get-tuple-element.35), channel_id=1, source_target_pairs={{0,24},{4,28},{8,16},{12,20},{16,8},{20,12},{24,0},{28,4},{1,25},{... | collective-permute-start | bytes 786440 | tf_op jit(solution)/shard_map/ppermute | solution.py:14
  22.7 1.3 %collective-permute-start.4 = (f32[128,128]{1,0:T(8,128)S(1)}, f32[128,128]{1,0:T(8,128)S(1)}, u32[]{:S(2)}, u32[]{:S(2)}) collective-permute-start(f32[128,128]{1,0:T(8,128)S(1)} %fusion.20), channel_id=1, source_target_pairs={{0,4},{4,0},{8,12},{12,8},{16,20},{20,16},{24,28},{28,24},{1,5},{5... | collective-permute-start | bytes 196616 | tf_op jit(solution)/shard_map/ppermute | solution.py:14
  24.1 4.3 %collective-permute-start.5 = (f32[128,128]{1,0:T(8,128)S(1)}, f32[128,128]{1,0:T(8,128)S(1)}, u32[]{:S(2)}, u32[]{:S(2)}) collective-permute-start(f32[128,128]{1,0:T(8,128)S(1)} %add.94), channel_id=1, source_target_pairs={{0,1},{1,0},{2,3},{3,2},{4,5},{5,4},{6,7},{7,6},{8,9},{9,8},{10,11... | collective-permute-start | bytes 196616 | tf_op jit(solution)/shard_map/ppermute | solution.py:14
  28.4 5.4 %collective-permute-start.6 = (f32[128,128]{1,0:T(8,128)S(1)}, f32[128,128]{1,0:T(8,128)S(1)}, u32[]{:S(2)}, u32[]{:S(2)}) collective-permute-start(f32[128,128]{1,0:T(8,128)S(1)} %add.95), channel_id=1, source_target_pairs={{0,2},{1,3},{2,0},{3,1},{4,6},{5,7},{6,4},{7,5},{8,10},{9,11},{10,... | collective-permute-start | bytes 196616 | tf_op jit(solution)/shard_map/ppermute | solution.py:14
  35.5 6.1 %collective-permute-start.11 = (f32[128,128]{1,0:T(8,128)S(1)}, f32[128,128]{1,0:T(8,128)S(1)}, u32[]{:S(2)}, u32[]{:S(2)}) collective-permute-start(f32[128,128]{1,0:T(8,128)S(1)} %add.96), channel_id=1, source_target_pairs={{0,8},{4,12},{8,0},{12,4},{16,24},{20,28},{24,16},{28,20},{1,9},{5... | collective-permute-start | bytes 196616 | tf_op jit(solution)/shard_map/ppermute | solution.py:14
  37.1 6.1 %collective-permute-start.15 = (f32[128,128]{1,0:T(8,128)S(1)}, f32[128,128]{1,0:T(8,128)S(1)}, u32[]{:S(2)}, u32[]{:S(2)}) collective-permute-start(f32[128,128]{1,0:T(8,128)S(1)} %get-tuple-element.23), channel_id=1, source_target_pairs={{0,3},{1,2},{2,1},{3,0},{4,7},{5,6},{6,5},{7,4},{8,11},{9,10},{10,... | collective-permute-start | bytes 196616 | tf_op jit(solution)/shard_map/ppermute | solution.py:14
  40.8 5.2 %collective-permute-start.14 = (f32[128,128]{1,0:T(8,128)S(1)}, f32[128,128]{1,0:T(8,128)S(1)}, u32[]{:S(2)}, u32[]{:S(2)}) collective-permute-start(f32[128,128]{1,0:T(8,128)S(1)} %get-tuple-element.22), channel_id=1, source_target_pairs={{0,2},{1,3},{2,0},{3,1},{4,6},{5,7},{6,4},{7,5},{8,10},{9,11},{10,... | collective-permute-start | bytes 196616 | tf_op jit(solution)/shard_map/ppermute | solution.py:14
  40.8 5.2 %collective-permute-start.13 = (f32[128,128]{1,0:T(8,128)S(1)}, f32[128,128]{1,0:T(8,128)S(1)}, u32[]{:S(2)}, u32[]{:S(2)}) collective-permute-start(f32[128,128]{1,0:T(8,128)S(1)} %get-tuple-element.21), channel_id=1, source_target_pairs={{0,1},{1,0},{2,3},{3,2},{4,5},{5,4},{6,7},{7,6},{8,9},{9,8},{10,11... | collective-permute-start | bytes 196616 | tf_op jit(solution)/shard_map/ppermute | solution.py:14
  41.6 4.4 %collective-permute-start.12 = (f32[128,128]{1,0:T(8,128)S(1)}, f32[128,128]{1,0:T(8,128)S(1)}, u32[]{:S(2)}, u32[]{:S(2)}) collective-permute-start(f32[128,128]{1,0:T(8,128)S(1)} %add.103.gram_ref), channel_id=1, source_target_pairs={{0,16},{4,20},{8,24},{12,28},{16,0},{20,4},{24,8},{28,12},{1,17},{... | collective-permute-start | bytes 196616 | tf_op jit(solution)/shard_map/ppermute | solution.py:14
  46.0 8.4 %collective-permute-start.16 = (f32[128,128]{1,0:T(8,128)S(1)}, f32[128,128]{1,0:T(8,128)S(1)}, u32[]{:S(2)}, u32[]{:S(2)}) collective-permute-start(f32[128,128]{1,0:T(8,128)S(1)} %add_add_fusion), channel_id=1, source_target_pairs={{0,3},{1,2},{2,1},{3,0},{4,7},{5,6},{6,5},{7,4},{8,11},{9,10},{10,... | collective-permute-start | bytes 196616 | tf_op jit(solution)/shard_map/ppermute | solution.py:14
  49.5 5.2 %collective-permute-start.17 = (f32[128,128]{1,0:T(8,128)S(1)}, f32[128,128]{1,0:T(8,128)S(1)}, u32[]{:S(2)}, u32[]{:S(2)}) collective-permute-start(f32[128,128]{1,0:T(8,128)S(1)} %add_add_fusion), channel_id=1, source_target_pairs={{0,2},{1,3},{2,0},{3,1},{4,6},{5,7},{6,4},{7,5},{8,10},{9,11},{10,... | collective-permute-start | bytes 196616 | tf_op jit(solution)/shard_map/ppermute | solution.py:14
  49.5 5.2 %collective-permute-start.18 = (f32[128,128]{1,0:T(8,128)S(1)}, f32[128,128]{1,0:T(8,128)S(1)}, u32[]{:S(2)}, u32[]{:S(2)}) collective-permute-start(f32[128,128]{1,0:T(8,128)S(1)} %add_add_fusion), channel_id=1, source_target_pairs={{0,1},{1,0},{2,3},{3,2},{4,5},{5,4},{6,7},{7,6},{8,9},{9,8},{10,11... | collective-permute-start | bytes 196616 | tf_op jit(solution)/shard_map/ppermute | solution.py:14
  54.4 9.1 %copy-start.1 = (bf16[512,2048]{1,0:T(8,128)(2,1)S(1)}, bf16[512,2048]{1,0:T(8,128)(2,1)}, u32[]{:S(2)}) copy-start(bf16[512,2048]{1,0:T(8,128)(2,1)} %copy-done) | copy-start | bytes 6291460
  55.1 9.3 %copy-start.2 = (f32[512,128]{1,0:T(8,128)}, f32[512,128]{1,0:T(8,128)S(1)}, u32[]{:S(2)}) copy-start(f32[512,128]{1,0:T(8,128)S(1)} %fusion.8) | copy-start | bytes 786436
  55.1 6.3 %collective-permute-start.21 = (bf16[512,128]{1,0:T(8,128)(2,1)S(1)}, bf16[512,128]{1,0:T(8,128)(2,1)S(1)}, u32[]{:S(2)}, u32[]{:S(2)}) collective-permute-start(bf16[512,128]{1,0:T(8,128)(2,1)S(1)} %convert_element_type.22), channel_id=1, source_target_pairs={{0,24},{4,28},{8,16},{12,20},{16,8},{20,12},{24,0},{28,4},{1,25},{... | collective-permute-start | bytes 393224 | tf_op jit(solution)/shard_map/ppermute | solution.py:14
  56.6 6.1 %collective-permute-start.20 = (bf16[512,128]{1,0:T(8,128)(2,1)S(1)}, bf16[512,128]{1,0:T(8,128)(2,1)S(1)}, u32[]{:S(2)}, u32[]{:S(2)}) collective-permute-start(bf16[512,128]{1,0:T(8,128)(2,1)S(1)} %convert_element_type.22), channel_id=1, source_target_pairs={{0,16},{4,20},{8,24},{12,28},{16,0},{20,4},{24,8},{28,12},{1,17},{... | collective-permute-start | bytes 393224 | tf_op jit(solution)/shard_map/ppermute | solution.py:14
  57.2 5.6 %collective-permute-start.19 = (bf16[512,128]{1,0:T(8,128)(2,1)S(1)}, bf16[512,128]{1,0:T(8,128)(2,1)S(1)}, u32[]{:S(2)}, u32[]{:S(2)}) collective-permute-start(bf16[512,128]{1,0:T(8,128)(2,1)S(1)} %convert_element_type.22), channel_id=1, source_target_pairs={{0,8},{4,12},{8,0},{12,4},{16,24},{20,28},{24,16},{28,20},{1,9},{5... | collective-permute-start | bytes 393224 | tf_op jit(solution)/shard_map/ppermute | solution.py:14
  62.8 2.0 %collective-permute-start.22 = (bf16[2048,128]{1,0:T(8,128)(2,1)S(1)}, bf16[2048,128]{1,0:T(8,128)(2,1)S(1)}, u32[]{:S(2)}, u32[]{:S(2)}) collective-permute-start(bf16[2048,128]{1,0:T(8,128)(2,1)S(1)} %pad_maximum_fusion.3), channel_id=1, source_target_pairs={{0,4},{4,0},{8,12},{12,8},{16,20},{20,16},{24,28},{28,24},{1,5},{5... | collective-permute-start | bytes 1572872 | tf_op jit(solution)/shard_map/ppermute | solution.py:14
  63.5 1.3 %copy-start.3 = (f32[512,128]{1,0:T(8,128)}, f32[512,128]{1,0:T(8,128)S(1)}, u32[]{:S(2)}) copy-start(f32[512,128]{1,0:T(8,128)S(1)} %fusion.10) | copy-start | bytes 786436

commit v8 on v7

--- a/solution.py
+++ b/solution.py
@@ -162,7 +162,6 @@
     share = parts[0]
     for mask in range(1, outer):
         share = share + flipped(parts[mask], "outer", mask)
-    gram, last, share = lax.optimization_barrier((gram, last, share))
 
     summed = jnp.zeros((piece, rank), jnp.float32)
     summed = lax.dynamic_update_slice_in_dim(summed, share, mine * part, 0)

time: 66.4 us -> 66 us (level)
  transfers between devices with their start and end apart: 23 -> 23, of which waited for: 15 -> 14; matrix products, arithmetic and copies ran while one was open for 10% -> 10% of each run, Pallas kernels for 6% -> 6%
where the time goes in v8:
time: 66 us; the launch traced here: 65.8 us
  starting transfers between devices  27.5 us (42%)
  waiting for transfers between devices  20.6 us (31%)
  matrix products  6.43 us (10%)
  Pallas kernels  3.9 us (6%)
  local copies, waits for them, and re-layouts  3.62 us (5%)
  other arithmetic  2.76 us (4%)
  between operations  0.92 us (1%)
    ppermute x23, starting transfers between devices, flipped(): lax.ppermute(block, axis, [(low, low ^ mask) for low in range(count)])  27.5 us
    ppermute x23, waiting for transfers between devices, flipped(): lax.ppermute(block, axis, [(low, low ^ mask) for low in range(count)])  20.6 us
    pallas_call x1, Pallas kernels, inverse_factor(): pl.pallas_call(factor_kernel, out_shape=jax.ShapeDtypeStruct((n, n), jnp....  3.9 us
    dynamic_slice x1, local copies, waits for them, and re-layouts, columns(): lax.dynamic_slice_in_dim(samples, (me ^ mask) * piece, piece, 1)  2.63 us
    dot_general x2, matrix products, errors(): lax.dot_general(basis_low, factor, (((1,), (1,)), ((), ())), preferred_el...  1.87 us
    dot_general x2, matrix products, products(): lax.dot_general(side, both, (((0,), (0,)), ((), ())), preferred_element_t...  1.53 us
    dot_general x3, matrix products, exact_dot(): lax.dot_general(a, b, (contract, ((), ())), precision=lax.Precision.HIGHE...  1.34 us
  transfers between devices with their start and end apart: 23, of which 14 were waited for; matrix products, arithmetic and copies ran while one was open for 10% of the time, Pallas kernels for 6%

profile of v8, /device:TPU:0, one launch (start us, length us, event | category | flops | bytes accessed | tf_op | source)
XLA Modules:
  0.0 65.8 jit_solution(3776293986219161420)
XLA Ops:
  0.6 4.0 %collective-permute-start.2 = (bf16[512,128]{1,0:T(8,128)(2,1)}, bf16[512,128]{1,0:T(8,128)(2,1)S(1)}, u32[]{:S(2)}, u32[]{:S(2)}) collective-permute-start(bf16[512,128]{1,0:T(8,128)(2,1)} %param.3), channel_id=1, source_target_pairs={{0,24},{4,28},{8,16},{12,20},{16,8},{20,12},{24,0},{28,4},{1,25},{... | collective-permute-start | bytes 393224 | tf_op jit(solution)/shard_map/ppermute | solution.py:14
  5.2 2.6 %constant_dynamic-slice_fusion.7 = (bf16[512,512]{1,0:T(8,128)(2,1)S(1)}, bf16[512,512]{1,0:T(8,128)(2,1)S(1)}, bf16[512,512]{1,0:T(8,128)(2,1)S(1)}, bf16[512,5...) fusion(bf16[512,4096]{1,0:T(8,128)(2,1)} %param.2, ...), kind=kLoop, calls=%fused_computation.39 | loop fusion | bytes 8388640 | tf_op jit(solution)/shard_map/dynamic_slice | solution.py:127
  8.8 2.3 %collective-permute-done.1 = bf16[512,128]{1,0:T(8,128)(2,1)S(1)} collective-permute-done((bf16[512,128]{1,0:T(8,128)(2,1)}, bf16[512,128]{1,0:T(8,128)(2,1)S(1)}, u32[]{:S(2)}, u32[]{:S(2)}) %collective-permute-start.1) | collective-permute-done | bytes 131104 | tf_op jit(solution)/shard_map/ppermute | solution.py:14
  11.5 0.8 %fusion.19 = f32[512,128]{0,1:T(8,128)S(1)} fusion(bf16[512,2048]{1,0:T(8,128)(2,1)S(1)} %get-tuple-element.12, bf16[2048,128]{1,0:T(8,128)(2,1)S(1)} %pad_maximum_fusion.2), kind=kOutput, calls=%fused_computation.50 | convolution fusion | flops 268435456 | bytes 2883584 | tf_op jit(solution)/shard_map/dot_general | solution.py:134
  12.3 1.1 %collective-permute-done.3 = bf16[2048,128]{1,0:T(8,128)(2,1)S(1)} collective-permute-done((bf16[2048,128]{1,0:T(8,128)(2,1)S(1)}, bf16[2048,128]{1,0:T(8,128)(2,1)S(1)}, u32[]{:S(2)}, u32[]{:S(2)}) %collective-permute-start.3) | collective-permute-done | bytes 524320 | tf_op jit(solution)/shard_map/ppermute | solution.py:14
  13.4 0.8 %reduce-precision_convert_fusion = (bf16[512,128]{0,1:T(8,128)(2,1)S(1)}, bf16[512,128]{0,1:T(8,128)(2,1)S(1)}, f32[512,128]{0,1:T(8,128)S(1)}) fusion(f32[512,128]{0,1:T(8,128)S(1)} %fusion.19, bf16[512,2048]{1,0:T(8,128)(2,1)S(1)} %get-tuple-element.14, bf16[2048,128]{1,0:T(8,128)(2,1)S(1)} %collective-permute-done.3), kind=kOutput, calls=%fused_computation.11 | convolution fusion | flops 268763136 | bytes 3407872 | tf_op jit(solution)/shard_map/dot_general | solution.py:135
  14.2 0.8 %fusion.4 = f32[2048,256]{1,0:T(8,128)S(1)} fusion(bf16[512,2048]{1,0:T(8,128)(2,1)S(1)} %get-tuple-element.14, bf16[512,128]{0,1:T(8,128)(2,1)S(1)} %get-tuple-element.39, bf16[512,128]{0,1:T(8,128)(2,1)S(1)} %get-tuple-element.38), kind=kOutput, calls=%fused_computation.17 | convolution fusion | flops 537395200 | bytes 4456448 | tf_op jit(solution)/shard_map/dot_general | solution.py:144
  15.3 0.8 %fusion.5 = f32[2048,256]{1,0:T(8,128)S(1)} fusion(bf16[512,2048]{1,0:T(8,128)(2,1)S(1)} %get-tuple-element.12, bf16[512,128]{0,1:T(8,128)(2,1)S(1)} %get-tuple-element.39, bf16[512,128]{0,1:T(8,128)(2,1)S(1)} %get-tuple-element.38), kind=kOutput, calls=%fused_computation.18 | convolution fusion | flops 537395200 | bytes 4456448 | tf_op jit(solution)/shard_map/dot_general | solution.py:144
  16.1 1.7 %collective-permute-done.7 = f32[2048,128]{1,0:T(8,128)S(1)} collective-permute-done((f32[2048,128]{1,0:T(8,128)S(1)}, f32[2048,128]{1,0:T(8,128)S(1)}, u32[]{:S(2)}, u32[]{:S(2)}) %collective-permute-start.7) | collective-permute-done | bytes 1048608 | tf_op jit(solution)/shard_map/ppermute | solution.py:14
  18.0 0.9 %fusion.18 = (f32[512,128]{1,0:T(8,128)}, f32[512,128]{1,0:T(8,128)}, f32[512,128]{1,0:T(8,128)}) fusion(f32[2048,128]{1,0:T(8,128)S(1)} %fusion), kind=kLoop, calls=%fused_computation.49 | loop fusion | bytes 1572864 | tf_op jit(solution)/shard_map/slice | solution.py:154
  18.9 1.5 %collective-permute-start.10 = (f32[512,128]{1,0:T(8,128)}, f32[512,128]{1,0:T(8,128)}, u32[]{:S(2)}, u32[]{:S(2)}) collective-permute-start(f32[512,128]{1,0:T(8,128)} %get-tuple-element.32), channel_id=1, source_target_pairs={{0,16},{4,20},{8,24},{12,28},{16,0},{20,4},{24,8},{28,12},{1,17},{... | collective-permute-start | bytes 786440 | tf_op jit(solution)/shard_map/ppermute | solution.py:14
  21.0 1.3 %collective-permute-start.8 = (f32[512,128]{1,0:T(8,128)}, f32[512,128]{1,0:T(8,128)}, u32[]{:S(2)}, u32[]{:S(2)}) collective-permute-start(f32[512,128]{1,0:T(8,128)} %get-tuple-element.31), channel_id=1, source_target_pairs={{0,24},{4,28},{8,16},{12,20},{16,8},{20,12},{24,0},{28,4},{1,25},{... | collective-permute-start | bytes 786440 | tf_op jit(solution)/shard_map/ppermute | solution.py:14
  22.8 1.2 %collective-permute-done.4 = f32[128,128]{1,0:T(8,128)S(1)} collective-permute-done((f32[128,128]{1,0:T(8,128)S(1)}, f32[128,128]{1,0:T(8,128)S(1)}, u32[]{:S(2)}, u32[]{:S(2)}) %collective-permute-start.4) | collective-permute-done | bytes 65568 | tf_op jit(solution)/shard_map/ppermute | solution.py:14
  24.1 1.6 %collective-permute-start.5 = (f32[128,128]{1,0:T(8,128)S(1)}, f32[128,128]{1,0:T(8,128)S(1)}, u32[]{:S(2)}, u32[]{:S(2)}) collective-permute-start(f32[128,128]{1,0:T(8,128)S(1)} %add.94), channel_id=1, source_target_pairs={{0,1},{1,0},{2,3},{3,2},{4,5},{5,4},{6,7},{7,6},{8,9},{9,8},{10,11... | collective-permute-start | bytes 196616 | tf_op jit(solution)/shard_map/ppermute | solution.py:14
  25.7 2.7 %collective-permute-done.5 = f32[128,128]{1,0:T(8,128)S(1)} collective-permute-done((f32[128,128]{1,0:T(8,128)S(1)}, f32[128,128]{1,0:T(8,128)S(1)}, u32[]{:S(2)}, u32[]{:S(2)}) %collective-permute-start.5) | collective-permute-done | bytes 65568 | tf_op jit(solution)/shard_map/ppermute | solution.py:14
  28.4 2.7 %collective-permute-start.6 = (f32[128,128]{1,0:T(8,128)S(1)}, f32[128,128]{1,0:T(8,128)S(1)}, u32[]{:S(2)}, u32[]{:S(2)}) collective-permute-start(f32[128,128]{1,0:T(8,128)S(1)} %add.95), channel_id=1, source_target_pairs={{0,2},{1,3},{2,0},{3,1},{4,6},{5,7},{6,4},{7,5},{8,10},{9,11},{10,... | collective-permute-start | bytes 196616 | tf_op jit(solution)/shard_map/ppermute | solution.py:14
  31.1 2.7 %collective-permute-done.6 = f32[128,128]{1,0:T(8,128)S(1)} collective-permute-done((f32[128,128]{1,0:T(8,128)S(1)}, f32[128,128]{1,0:T(8,128)S(1)}, u32[]{:S(2)}, u32[]{:S(2)}) %collective-permute-start.6) | collective-permute-done | bytes 65568 | tf_op jit(solution)/shard_map/ppermute | solution.py:14
  34.3 1.2 %fusion.3 = f32[512,128]{1,0:T(8,128)S(1)} fusion(f32[512,128]{1,0:T(8,128)} %collective-permute-done.10, f32[512,128]{1,0:T(8,128)} %collective-permute-done.9, f32[512,128]{1,0:T(8,128)} %collective-permute-done.8, f32[2048,128]{1,0:T(8,128)S(1)} %fusion), kind=kLoop, calls=%fused_computation.15 | loop fusion | flops 196608 | bytes 1310720 | tf_op jit(solution)/shard_map/add | solution.py:154
  35.5 1.6 %collective-permute-start.11 = (f32[128,128]{1,0:T(8,128)S(1)}, f32[128,128]{1,0:T(8,128)S(1)}, u32[]{:S(2)}, u32[]{:S(2)}) collective-permute-start(f32[128,128]{1,0:T(8,128)S(1)} %add.96), channel_id=1, source_target_pairs={{0,8},{4,12},{8,0},{12,4},{16,24},{20,28},{24,16},{28,20},{1,9},{5... | collective-permute-start | bytes 196616 | tf_op jit(solution)/shard_map/ppermute | solution.py:14
  37.1 3.7 %collective-permute-start.15 = (f32[128,128]{1,0:T(8,128)S(1)}, f32[128,128]{1,0:T(8,128)S(1)}, u32[]{:S(2)}, u32[]{:S(2)}) collective-permute-start(f32[128,128]{1,0:T(8,128)S(1)} %get-tuple-element.20), channel_id=1, source_target_pairs={{0,3},{1,2},{2,1},{3,0},{4,7},{5,6},{6,5},{7,4},{8,11},{9,10},{10,... | collective-permute-start | bytes 196616 | tf_op jit(solution)/shard_map/ppermute | solution.py:14
  40.8 0.8 %collective-permute-start.13 = (f32[128,128]{1,0:T(8,128)S(1)}, f32[128,128]{1,0:T(8,128)S(1)}, u32[]{:S(2)}, u32[]{:S(2)}) collective-permute-start(f32[128,128]{1,0:T(8,128)S(1)} %get-tuple-element.18), channel_id=1, source_target_pairs={{0,1},{1,0},{2,3},{3,2},{4,5},{5,4},{6,7},{7,6},{8,9},{9,8},{10,11... | collective-permute-start | bytes 196616 | tf_op jit(solution)/shard_map/ppermute | solution.py:14
  42.3 1.0 %collective-permute-done.15 = f32[128,128]{1,0:T(8,128)S(1)} collective-permute-done((f32[128,128]{1,0:T(8,128)S(1)}, f32[128,128]{1,0:T(8,128)S(1)}, u32[]{:S(2)}, u32[]{:S(2)}) %collective-permute-start.15) | collective-permute-done | bytes 65568 | tf_op jit(solution)/shard_map/ppermute | solution.py:14
  43.3 2.7 %collective-permute-done.14 = f32[128,128]{1,0:T(8,128)S(1)} collective-permute-done((f32[128,128]{1,0:T(8,128)S(1)}, f32[128,128]{1,0:T(8,128)S(1)}, u32[]{:S(2)}, u32[]{:S(2)}) %collective-permute-start.14) | collective-permute-done | bytes 65568 | tf_op jit(solution)/shard_map/ppermute | solution.py:14
  46.1 2.2 %collective-permute-start.16 = (f32[128,128]{1,0:T(8,128)S(1)}, f32[128,128]{1,0:T(8,128)S(1)}, u32[]{:S(2)}, u32[]{:S(2)}) collective-permute-start(f32[128,128]{1,0:T(8,128)S(1)} %get-tuple-element.22), channel_id=1, source_target_pairs={{0,3},{1,2},{2,1},{3,0},{4,7},{5,6},{6,5},{7,4},{8,11},{9,10},{10,... | collective-permute-start | bytes 196616 | tf_op jit(solution)/shard_map/ppermute | solution.py:14
  48.2 2.3 %collective-permute-start.18 = (f32[128,128]{1,0:T(8,128)S(1)}, f32[128,128]{1,0:T(8,128)S(1)}, u32[]{:S(2)}, u32[]{:S(2)}) collective-permute-start(f32[128,128]{1,0:T(8,128)S(1)} %get-tuple-element.22), channel_id=1, source_target_pairs={{0,1},{1,0},{2,3},{3,2},{4,5},{5,4},{6,7},{7,6},{8,9},{9,8},{10,11... | collective-permute-start | bytes 196616 | tf_op jit(solution)/shard_map/ppermute | solution.py:14
  50.5 3.9 %inverse_factor.1 = f32[128,128]{1,0:T(8,128)S(1)} custom-call(f32[128,128]{1,0:T(8,128)S(1)} %add.103.gram_ref, f32[128,128]{1,0:T(8,128)S(1)} %collective-permute-done.12.other_ref), custom_call_target="tpu_custom_call" | custom-call | flops 6000000000 | bytes 131072 | tf_op jit(solution)/shard_map/inverse_factor/pallas_call | solution.py:97
  54.9 1.5 %collective-permute-start.21 = (bf16[512,128]{1,0:T(8,128)(2,1)S(1)}, bf16[512,128]{1,0:T(8,128)(2,1)S(1)}, u32[]{:S(2)}, u32[]{:S(2)}) collective-permute-start(bf16[512,128]{1,0:T(8,128)(2,1)S(1)} %convert_element_type.22), channel_id=1, source_target_pairs={{0,24},{4,28},{8,16},{12,20},{16,8},{20,12},{24,0},{28,4},{1,25},{... | collective-permute-start | bytes 393224 | tf_op jit(solution)/shard_map/ppermute | solution.py:14
  57.0 1.5 %collective-permute-start.19 = (bf16[512,128]{1,0:T(8,128)(2,1)S(1)}, bf16[512,128]{1,0:T(8,128)(2,1)S(1)}, u32[]{:S(2)}, u32[]{:S(2)}) collective-permute-start(bf16[512,128]{1,0:T(8,128)(2,1)S(1)} %convert_element_type.22), channel_id=1, source_target_pairs={{0,8},{4,12},{8,0},{12,4},{16,24},{20,28},{24,16},{28,20},{1,9},{5... | collective-permute-start | bytes 393224 | tf_op jit(solution)/shard_map/ppermute | solution.py:14
  58.5 2.5 %collective-permute-done.21 = bf16[512,128]{1,0:T(8,128)(2,1)S(1)} collective-permute-done((bf16[512,128]{1,0:T(8,128)(2,1)S(1)}, bf16[512,128]{1,0:T(8,128)(2,1)S(1)}, u32[]{:S(2)}, u32[]{:S(2)}) %collective-permute-start.21) | collective-permute-done | bytes 131104 | tf_op jit(solution)/shard_map/ppermute | solution.py:14
  61.0 1.3 %collective-permute-done.20 = bf16[512,128]{1,0:T(8,128)(2,1)S(1)} collective-permute-done((bf16[512,128]{1,0:T(8,128)(2,1)S(1)}, bf16[512,128]{1,0:T(8,128)(2,1)S(1)}, u32[]{:S(2)}, u32[]{:S(2)}) %collective-permute-start.20) | collective-permute-done | bytes 131104 | tf_op jit(solution)/shard_map/ppermute | solution.py:14
  63.0 0.9 %multiply_reduce_fusion.1 = f32[512]{0:T(512)S(1)} fusion(bf16[512,2048]{1,0:T(8,128)(2,1)S(1)} %copy-done.1, f32[512,128]{1,0:T(8,128)S(1)} %fusion.10, bf16[512,128]{1,0:T(8,128)(2,1)S(1)} %collective-permute-done.21, bf16[512,128]{1,0:T(8,128)(2,1)S(1)} %collective-permute-done.20, bf16[512,128]{1,0:T(8,128)(2,1)S(1)} %collective-permute-done.19, ...), kind=kOutput, calls=%fused_computation.1 | convolution fusion | flops 275840512 | bytes 2885632 | tf_op jit(solution)/shard_map/dot_general | solution.py:187
  64.3 0.9 %multiply_reduce_fusion = f32[512]{0:T(512)S(1)} fusion(bf16[512,2048]{1,0:T(8,128)(2,1)S(1)} %get-tuple-element.14, bf16[2048,128]{1,0:T(8,128)(2,1)S(1)} %collective-permute-done.22, f32[512,128]{1,0:T(8,128)S(1)} %fusion.10), kind=kOutput, calls=%fused_computation | convolution fusion | flops 273743360 | bytes 2885632 | tf_op jit(solution)/shard_map/dot_general | solution.py:187
  (54 shorter events, 7.4 us)
Async XLA Ops:
  0.6 8.2 %collective-permute-start.2 = (bf16[512,128]{1,0:T(8,128)(2,1)}, bf16[512,128]{1,0:T(8,128)(2,1)S(1)}, u32[]{:S(2)}, u32[]{:S(2)}) collective-permute-start(bf16[512,128]{1,0:T(8,128)(2,1)} %param.3), channel_id=1, source_target_pairs={{0,24},{4,28},{8,16},{12,20},{16,8},{20,12},{24,0},{28,4},{1,25},{... | collective-permute-start | bytes 393224 | tf_op jit(solution)/shard_map/ppermute | solution.py:14
  4.6 6.5 %collective-permute-start.1 = (bf16[512,128]{1,0:T(8,128)(2,1)}, bf16[512,128]{1,0:T(8,128)(2,1)S(1)}, u32[]{:S(2)}, u32[]{:S(2)}) collective-permute-start(bf16[512,128]{1,0:T(8,128)(2,1)} %param.3), channel_id=1, source_target_pairs={{0,16},{4,20},{8,24},{12,28},{16,0},{20,4},{24,8},{28,12},{1,17},{... | collective-permute-start | bytes 393224 | tf_op jit(solution)/shard_map/ppermute | solution.py:14
  5.1 6.3 %collective-permute-start = (bf16[512,128]{1,0:T(8,128)(2,1)}, bf16[512,128]{1,0:T(8,128)(2,1)S(1)}, u32[]{:S(2)}, u32[]{:S(2)}) collective-permute-start(bf16[512,128]{1,0:T(8,128)(2,1)} %param.3), channel_id=1, source_target_pairs={{0,8},{4,12},{8,0},{12,4},{16,24},{20,28},{24,16},{28,20},{1,9},{5... | collective-permute-start | bytes 393224 | tf_op jit(solution)/shard_map/ppermute | solution.py:14
  7.9 3.5 %copy-start.4 = (bf16[512,128]{1,0:T(8,128)(2,1)S(1)}, bf16[512,128]{1,0:T(8,128)(2,1)}, u32[]{:S(2)}) copy-start(bf16[512,128]{1,0:T(8,128)(2,1)} %param.3) | copy-start | bytes 393220
  8.5 6.8 %copy-start = (bf16[512,2048]{1,0:T(8,128)(2,1)}, bf16[512,2048]{1,0:T(8,128)(2,1)S(1)}, u32[]{:S(2)}) copy-start(bf16[512,2048]{1,0:T(8,128)(2,1)S(1)} %get-tuple-element.12) | copy-start | bytes 6291460
  11.4 2.0 %collective-permute-start.3 = (bf16[2048,128]{1,0:T(8,128)(2,1)S(1)}, bf16[2048,128]{1,0:T(8,128)(2,1)S(1)}, u32[]{:S(2)}, u32[]{:S(2)}) collective-permute-start(bf16[2048,128]{1,0:T(8,128)(2,1)S(1)} %pad_maximum_fusion.2), channel_id=1, source_target_pairs={{0,4},{4,0},{8,12},{12,8},{16,20},{20,16},{24,28},{28,24},{1,5},{5... | collective-permute-start | bytes 1572872 | tf_op jit(solution)/shard_map/ppermute | solution.py:14
  15.1 2.7 %collective-permute-start.7 = (f32[2048,128]{1,0:T(8,128)S(1)}, f32[2048,128]{1,0:T(8,128)S(1)}, u32[]{:S(2)}, u32[]{:S(2)}) collective-permute-start(f32[2048,128]{1,0:T(8,128)S(1)} %slice_add_fusion), channel_id=1, source_target_pairs={{0,4},{4,0},{8,12},{12,8},{16,20},{20,16},{24,28},{28,24},{1,5},{5... | collective-permute-start | bytes 3145736 | tf_op jit(solution)/shard_map/ppermute | solution.py:14
  18.9 14.9 %collective-permute-start.10 = (f32[512,128]{1,0:T(8,128)}, f32[512,128]{1,0:T(8,128)}, u32[]{:S(2)}, u32[]{:S(2)}) collective-permute-start(f32[512,128]{1,0:T(8,128)} %get-tuple-element.32), channel_id=1, source_target_pairs={{0,16},{4,20},{8,24},{12,28},{16,0},{20,4},{24,8},{28,12},{1,17},{... | collective-permute-start | bytes 786440 | tf_op jit(solution)/shard_map/ppermute | solution.py:14
  20.3 13.5 %collective-permute-start.9 = (f32[512,128]{1,0:T(8,128)}, f32[512,128]{1,0:T(8,128)}, u32[]{:S(2)}, u32[]{:S(2)}) collective-permute-start(f32[512,128]{1,0:T(8,128)} %get-tuple-element.33), channel_id=1, source_target_pairs={{0,8},{4,12},{8,0},{12,4},{16,24},{20,28},{24,16},{28,20},{1,9},{5... | collective-permute-start | bytes 786440 | tf_op jit(solution)/shard_map/ppermute | solution.py:14
  21.0 13.3 %collective-permute-start.8 = (f32[512,128]{1,0:T(8,128)}, f32[512,128]{1,0:T(8,128)}, u32[]{:S(2)}, u32[]{:S(2)}) collective-permute-start(f32[512,128]{1,0:T(8,128)} %get-tuple-element.31), channel_id=1, source_target_pairs={{0,24},{4,28},{8,16},{12,20},{16,8},{20,12},{24,0},{28,4},{1,25},{... | collective-permute-start | bytes 786440 | tf_op jit(solution)/shard_map/ppermute | solution.py:14
  22.7 1.3 %collective-permute-start.4 = (f32[128,128]{1,0:T(8,128)S(1)}, f32[128,128]{1,0:T(8,128)S(1)}, u32[]{:S(2)}, u32[]{:S(2)}) collective-permute-start(f32[128,128]{1,0:T(8,128)S(1)} %fusion.20), channel_id=1, source_target_pairs={{0,4},{4,0},{8,12},{12,8},{16,20},{20,16},{24,28},{28,24},{1,5},{5... | collective-permute-start | bytes 196616 | tf_op jit(solution)/shard_map/ppermute | solution.py:14
  24.1 4.3 %collective-permute-start.5 = (f32[128,128]{1,0:T(8,128)S(1)}, f32[128,128]{1,0:T(8,128)S(1)}, u32[]{:S(2)}, u32[]{:S(2)}) collective-permute-start(f32[128,128]{1,0:T(8,128)S(1)} %add.94), channel_id=1, source_target_pairs={{0,1},{1,0},{2,3},{3,2},{4,5},{5,4},{6,7},{7,6},{8,9},{9,8},{10,11... | collective-permute-start | bytes 196616 | tf_op jit(solution)/shard_map/ppermute | solution.py:14
  28.4 5.4 %collective-permute-start.6 = (f32[128,128]{1,0:T(8,128)S(1)}, f32[128,128]{1,0:T(8,128)S(1)}, u32[]{:S(2)}, u32[]{:S(2)}) collective-permute-start(f32[128,128]{1,0:T(8,128)S(1)} %add.95), channel_id=1, source_target_pairs={{0,2},{1,3},{2,0},{3,1},{4,6},{5,7},{6,4},{7,5},{8,10},{9,11},{10,... | collective-permute-start | bytes 196616 | tf_op jit(solution)/shard_map/ppermute | solution.py:14
  35.5 6.1 %collective-permute-start.11 = (f32[128,128]{1,0:T(8,128)S(1)}, f32[128,128]{1,0:T(8,128)S(1)}, u32[]{:S(2)}, u32[]{:S(2)}) collective-permute-start(f32[128,128]{1,0:T(8,128)S(1)} %add.96), channel_id=1, source_target_pairs={{0,8},{4,12},{8,0},{12,4},{16,24},{20,28},{24,16},{28,20},{1,9},{5... | collective-permute-start | bytes 196616 | tf_op jit(solution)/shard_map/ppermute | solution.py:14
  37.1 6.1 %collective-permute-start.15 = (f32[128,128]{1,0:T(8,128)S(1)}, f32[128,128]{1,0:T(8,128)S(1)}, u32[]{:S(2)}, u32[]{:S(2)}) collective-permute-start(f32[128,128]{1,0:T(8,128)S(1)} %get-tuple-element.20), channel_id=1, source_target_pairs={{0,3},{1,2},{2,1},{3,0},{4,7},{5,6},{6,5},{7,4},{8,11},{9,10},{10,... | collective-permute-start | bytes 196616 | tf_op jit(solution)/shard_map/ppermute | solution.py:14
  40.8 5.2 %collective-permute-start.14 = (f32[128,128]{1,0:T(8,128)S(1)}, f32[128,128]{1,0:T(8,128)S(1)}, u32[]{:S(2)}, u32[]{:S(2)}) collective-permute-start(f32[128,128]{1,0:T(8,128)S(1)} %get-tuple-element.19), channel_id=1, source_target_pairs={{0,2},{1,3},{2,0},{3,1},{4,6},{5,7},{6,4},{7,5},{8,10},{9,11},{10,... | collective-permute-start | bytes 196616 | tf_op jit(solution)/shard_map/ppermute | solution.py:14
  40.8 5.2 %collective-permute-start.13 = (f32[128,128]{1,0:T(8,128)S(1)}, f32[128,128]{1,0:T(8,128)S(1)}, u32[]{:S(2)}, u32[]{:S(2)}) collective-permute-start(f32[128,128]{1,0:T(8,128)S(1)} %get-tuple-element.18), channel_id=1, source_target_pairs={{0,1},{1,0},{2,3},{3,2},{4,5},{5,4},{6,7},{7,6},{8,9},{9,8},{10,11... | collective-permute-start | bytes 196616 | tf_op jit(solution)/shard_map/ppermute | solution.py:14
  41.6 8.9 %collective-permute-start.12 = (f32[128,128]{1,0:T(8,128)S(1)}, f32[128,128]{1,0:T(8,128)S(1)}, u32[]{:S(2)}, u32[]{:S(2)}) collective-permute-start(f32[128,128]{1,0:T(8,128)S(1)} %add.103.gram_ref), channel_id=1, source_target_pairs={{0,16},{4,20},{8,24},{12,28},{16,0},{20,4},{24,8},{28,12},{1,17},{... | collective-permute-start | bytes 196616 | tf_op jit(solution)/shard_map/ppermute | solution.py:14
  46.1 8.4 %collective-permute-start.16 = (f32[128,128]{1,0:T(8,128)S(1)}, f32[128,128]{1,0:T(8,128)S(1)}, u32[]{:S(2)}, u32[]{:S(2)}) collective-permute-start(f32[128,128]{1,0:T(8,128)S(1)} %get-tuple-element.22), channel_id=1, source_target_pairs={{0,3},{1,2},{2,1},{3,0},{4,7},{5,6},{6,5},{7,4},{8,11},{9,10},{10,... | collective-permute-start | bytes 196616 | tf_op jit(solution)/shard_map/ppermute | solution.py:14
  48.2 6.2 %collective-permute-start.17 = (f32[128,128]{1,0:T(8,128)S(1)}, f32[128,128]{1,0:T(8,128)S(1)}, u32[]{:S(2)}, u32[]{:S(2)}) collective-permute-start(f32[128,128]{1,0:T(8,128)S(1)} %get-tuple-element.22), channel_id=1, source_target_pairs={{0,2},{1,3},{2,0},{3,1},{4,6},{5,7},{6,4},{7,5},{8,10},{9,11},{10,... | collective-permute-start | bytes 196616 | tf_op jit(solution)/shard_map/ppermute | solution.py:14
  48.2 6.3 %collective-permute-start.18 = (f32[128,128]{1,0:T(8,128)S(1)}, f32[128,128]{1,0:T(8,128)S(1)}, u32[]{:S(2)}, u32[]{:S(2)}) collective-permute-start(f32[128,128]{1,0:T(8,128)S(1)} %get-tuple-element.22), channel_id=1, source_target_pairs={{0,1},{1,0},{2,3},{3,2},{4,5},{5,4},{6,7},{7,6},{8,9},{9,8},{10,11... | collective-permute-start | bytes 196616 | tf_op jit(solution)/shard_map/ppermute | solution.py:14
  54.4 8.6 %copy-start.1 = (bf16[512,2048]{1,0:T(8,128)(2,1)S(1)}, bf16[512,2048]{1,0:T(8,128)(2,1)}, u32[]{:S(2)}) copy-start(bf16[512,2048]{1,0:T(8,128)(2,1)} %copy-done) | copy-start | bytes 6291460
  54.9 9.1 %copy-start.2 = (f32[512,128]{1,0:T(8,128)}, f32[512,128]{1,0:T(8,128)S(1)}, u32[]{:S(2)}) copy-start(f32[512,128]{1,0:T(8,128)S(1)} %fusion.8) | copy-start | bytes 786436
  54.9 6.0 %collective-permute-start.21 = (bf16[512,128]{1,0:T(8,128)(2,1)S(1)}, bf16[512,128]{1,0:T(8,128)(2,1)S(1)}, u32[]{:S(2)}, u32[]{:S(2)}) collective-permute-start(bf16[512,128]{1,0:T(8,128)(2,1)S(1)} %convert_element_type.22), channel_id=1, source_target_pairs={{0,24},{4,28},{8,16},{12,20},{16,8},{20,12},{24,0},{28,4},{1,25},{... | collective-permute-start | bytes 393224 | tf_op jit(solution)/shard_map/ppermute | solution.py:14
  56.4 5.9 %collective-permute-start.20 = (bf16[512,128]{1,0:T(8,128)(2,1)S(1)}, bf16[512,128]{1,0:T(8,128)(2,1)S(1)}, u32[]{:S(2)}, u32[]{:S(2)}) collective-permute-start(bf16[512,128]{1,0:T(8,128)(2,1)S(1)} %convert_element_type.22), channel_id=1, source_target_pairs={{0,16},{4,20},{8,24},{12,28},{16,0},{20,4},{24,8},{28,12},{1,17},{... | collective-permute-start | bytes 393224 | tf_op jit(solution)/shard_map/ppermute | solution.py:14
  57.0 5.3 %collective-permute-start.19 = (bf16[512,128]{1,0:T(8,128)(2,1)S(1)}, bf16[512,128]{1,0:T(8,128)(2,1)S(1)}, u32[]{:S(2)}, u32[]{:S(2)}) collective-permute-start(bf16[512,128]{1,0:T(8,128)(2,1)S(1)} %convert_element_type.22), channel_id=1, source_target_pairs={{0,8},{4,12},{8,0},{12,4},{16,24},{20,28},{24,16},{28,20},{1,9},{5... | collective-permute-start | bytes 393224 | tf_op jit(solution)/shard_map/ppermute | solution.py:14
  62.3 2.0 %collective-permute-start.22 = (bf16[2048,128]{1,0:T(8,128)(2,1)S(1)}, bf16[2048,128]{1,0:T(8,128)(2,1)S(1)}, u32[]{:S(2)}, u32[]{:S(2)}) collective-permute-start(bf16[2048,128]{1,0:T(8,128)(2,1)S(1)} %pad_maximum_fusion.3), channel_id=1, source_target_pairs={{0,4},{4,0},{8,12},{12,8},{16,20},{20,16},{24,28},{28,24},{1,5},{5... | collective-permute-start | bytes 1572872 | tf_op jit(solution)/shard_map/ppermute | solution.py:14
  63.0 1.3 %copy-start.3 = (f32[512,128]{1,0:T(8,128)}, f32[512,128]{1,0:T(8,128)S(1)}, u32[]{:S(2)}) copy-start(f32[512,128]{1,0:T(8,128)S(1)} %fusion.10) | copy-start | bytes 786436

commit v9 on v8

--- a/solution.py
+++ b/solution.py
@@ -152,7 +152,6 @@
     own = pieces[0]
     for mask in [inner - 2, *evens[:-1]]:
         own = own + flipped(pieces[mask // 2], "inner", mask)
-    gram, own = lax.optimization_barrier((gram, own))
     levels = inner.bit_length() - 1
     for level in range(1, levels - 1):
         gram = gram + flipped(gram, "inner", 1 << level)

time: 66 us -> 69.2 us (1.048)
  waiting for transfers between devices: 20.6 us -> 23.4 us
    ppermute x23, waiting for transfers between devices: 20.6 us -> 23.4 us  [flipped(): lax.ppermute(block, axis, [(low, low ^ mask) for low in range(count)])]
  transfers between devices with their start and end apart: 23 -> 23, of which waited for: 14 -> 14; matrix products, arithmetic and copies ran while one was open for 10% -> 12% of each run, Pallas kernels for 6% -> 6%
where the time goes in v9:
time: 69.2 us; the launch traced here: 69 us
  starting transfers between devices  28 us (40%)
  waiting for transfers between devices  23.4 us (34%)
  matrix products  6.43 us (9%)
  Pallas kernels  3.9 us (6%)
  local copies, waits for them, and re-layouts  3.63 us (5%)
  other arithmetic  2.77 us (4%)
  between operations  0.89 us (1%)
    ppermute x23, starting transfers between devices, flipped(): lax.ppermute(block, axis, [(low, low ^ mask) for low in range(count)])  28 us
    ppermute x23, waiting for transfers between devices, flipped(): lax.ppermute(block, axis, [(low, low ^ mask) for low in range(count)])  23.4 us
    pallas_call x1, Pallas kernels, inverse_factor(): pl.pallas_call(factor_kernel, out_shape=jax.ShapeDtypeStruct((n, n), jnp....  3.9 us
    dynamic_slice x1, local copies, waits for them, and re-layouts, columns(): lax.dynamic_slice_in_dim(samples, (me ^ mask) * piece, piece, 1)  2.63 us
    dot_general x2, matrix products, errors(): lax.dot_general(basis_low, factor, (((1,), (1,)), ((), ())), preferred_el...  1.87 us
    dot_general x2, matrix products, products(): lax.dot_general(side, both, (((0,), (0,)), ((), ())), preferred_element_t...  1.53 us
  transfers between devices with their start and end apart: 23, of which 14 were waited for; matrix products, arithmetic and copies ran while one was open for 12% of the time, Pallas kernels for 6%

profile of v9, /device:TPU:0, one launch (start us, length us, event | category | flops | bytes accessed | tf_op | source)
XLA Modules:
  0.0 69.0 jit_solution(8191256353417836899)
XLA Ops:
  0.6 4.0 %collective-permute-start.2 = (bf16[512,128]{1,0:T(8,128)(2,1)}, bf16[512,128]{1,0:T(8,128)(2,1)S(1)}, u32[]{:S(2)}, u32[]{:S(2)}) collective-permute-start(bf16[512,128]{1,0:T(8,128)(2,1)} %param.3), channel_id=1, source_target_pairs={{0,24},{4,28},{8,16},{12,20},{16,8},{20,12},{24,0},{28,4},{1,25},{... | collective-permute-start | bytes 393224 | tf_op jit(solution)/shard_map/ppermute | solution.py:14
  5.2 2.6 %constant_dynamic-slice_fusion.7 = (bf16[512,512]{1,0:T(8,128)(2,1)S(1)}, bf16[512,512]{1,0:T(8,128)(2,1)S(1)}, bf16[512,512]{1,0:T(8,128)(2,1)S(1)}, bf16[512,5...) fusion(bf16[512,4096]{1,0:T(8,128)(2,1)} %param.2, ...), kind=kLoop, calls=%fused_computation.39 | loop fusion | bytes 8388640 | tf_op jit(solution)/shard_map/dynamic_slice | solution.py:127
  8.8 2.3 %collective-permute-done.1 = bf16[512,128]{1,0:T(8,128)(2,1)S(1)} collective-permute-done((bf16[512,128]{1,0:T(8,128)(2,1)}, bf16[512,128]{1,0:T(8,128)(2,1)S(1)}, u32[]{:S(2)}, u32[]{:S(2)}) %collective-permute-start.1) | collective-permute-done | bytes 131104 | tf_op jit(solution)/shard_map/ppermute | solution.py:14
  11.5 0.8 %fusion.19 = f32[512,128]{0,1:T(8,128)S(1)} fusion(bf16[512,2048]{1,0:T(8,128)(2,1)S(1)} %get-tuple-element.10, bf16[2048,128]{1,0:T(8,128)(2,1)S(1)} %pad_maximum_fusion.2), kind=kOutput, calls=%fused_computation.50 | convolution fusion | flops 268435456 | bytes 2883584 | tf_op jit(solution)/shard_map/dot_general | solution.py:134
  12.3 1.1 %collective-permute-done.3 = bf16[2048,128]{1,0:T(8,128)(2,1)S(1)} collective-permute-done((bf16[2048,128]{1,0:T(8,128)(2,1)S(1)}, bf16[2048,128]{1,0:T(8,128)(2,1)S(1)}, u32[]{:S(2)}, u32[]{:S(2)}) %collective-permute-start.3) | collective-permute-done | bytes 524320 | tf_op jit(solution)/shard_map/ppermute | solution.py:14
  13.4 0.8 %reduce-precision_convert_fusion = (bf16[512,128]{0,1:T(8,128)(2,1)S(1)}, bf16[512,128]{0,1:T(8,128)(2,1)S(1)}, f32[512,128]{0,1:T(8,128)S(1)}) fusion(f32[512,128]{0,1:T(8,128)S(1)} %fusion.19, bf16[512,2048]{1,0:T(8,128)(2,1)S(1)} %get-tuple-element.12, bf16[2048,128]{1,0:T(8,128)(2,1)S(1)} %collective-permute-done.3), kind=kOutput, calls=%fused_computation.11 | convolution fusion | flops 268763136 | bytes 3407872 | tf_op jit(solution)/shard_map/dot_general | solution.py:135
  14.2 0.8 %fusion.4 = f32[2048,256]{1,0:T(8,128)S(1)} fusion(bf16[512,2048]{1,0:T(8,128)(2,1)S(1)} %get-tuple-element.12, bf16[512,128]{0,1:T(8,128)(2,1)S(1)} %get-tuple-element.35, bf16[512,128]{0,1:T(8,128)(2,1)S(1)} %get-tuple-element.34), kind=kOutput, calls=%fused_computation.17 | convolution fusion | flops 537395200 | bytes 4456448 | tf_op jit(solution)/shard_map/dot_general | solution.py:144
  16.1 1.7 %collective-permute-done.9 = f32[2048,128]{1,0:T(8,128)S(1)} collective-permute-done((f32[2048,128]{1,0:T(8,128)S(1)}, f32[2048,128]{1,0:T(8,128)S(1)}, u32[]{:S(2)}, u32[]{:S(2)}) %collective-permute-start.9) | collective-permute-done | bytes 1048608 | tf_op jit(solution)/shard_map/ppermute | solution.py:14
  18.0 0.9 %fusion.18 = (f32[512,128]{1,0:T(8,128)}, f32[512,128]{1,0:T(8,128)}, f32[512,128]{1,0:T(8,128)}) fusion(f32[2048,128]{1,0:T(8,128)S(1)} %fusion), kind=kLoop, calls=%fused_computation.49 | loop fusion | bytes 1572864 | tf_op jit(solution)/shard_map/slice | solution.py:154
  18.9 1.5 %collective-permute-start.12 = (f32[512,128]{1,0:T(8,128)}, f32[512,128]{1,0:T(8,128)}, u32[]{:S(2)}, u32[]{:S(2)}) collective-permute-start(f32[512,128]{1,0:T(8,128)} %get-tuple-element.28), channel_id=1, source_target_pairs={{0,16},{4,20},{8,24},{12,28},{16,0},{20,4},{24,8},{28,12},{1,17},{... | collective-permute-start | bytes 786440 | tf_op jit(solution)/shard_map/ppermute | solution.py:14
  21.0 1.3 %collective-permute-start.10 = (f32[512,128]{1,0:T(8,128)}, f32[512,128]{1,0:T(8,128)}, u32[]{:S(2)}, u32[]{:S(2)}) collective-permute-start(f32[512,128]{1,0:T(8,128)} %get-tuple-element.27), channel_id=1, source_target_pairs={{0,24},{4,28},{8,16},{12,20},{16,8},{20,12},{24,0},{28,4},{1,25},{... | collective-permute-start | bytes 786440 | tf_op jit(solution)/shard_map/ppermute | solution.py:14
  22.8 1.2 %collective-permute-done.4 = f32[128,128]{1,0:T(8,128)S(1)} collective-permute-done((f32[128,128]{1,0:T(8,128)S(1)}, f32[128,128]{1,0:T(8,128)S(1)}, u32[]{:S(2)}, u32[]{:S(2)}) %collective-permute-start.4) | collective-permute-done | bytes 65568 | tf_op jit(solution)/shard_map/ppermute | solution.py:14
  24.1 1.6 %collective-permute-start.5 = (f32[128,128]{1,0:T(8,128)S(1)}, f32[128,128]{1,0:T(8,128)S(1)}, u32[]{:S(2)}, u32[]{:S(2)}) collective-permute-start(f32[128,128]{1,0:T(8,128)S(1)} %add.94), channel_id=1, source_target_pairs={{0,1},{1,0},{2,3},{3,2},{4,5},{5,4},{6,7},{7,6},{8,9},{9,8},{10,11... | collective-permute-start | bytes 196616 | tf_op jit(solution)/shard_map/ppermute | solution.py:14
  25.7 2.7 %collective-permute-done.5 = f32[128,128]{1,0:T(8,128)S(1)} collective-permute-done((f32[128,128]{1,0:T(8,128)S(1)}, f32[128,128]{1,0:T(8,128)S(1)}, u32[]{:S(2)}, u32[]{:S(2)}) %collective-permute-start.5) | collective-permute-done | bytes 65568 | tf_op jit(solution)/shard_map/ppermute | solution.py:14
  28.4 2.7 %collective-permute-start.6 = (f32[128,128]{1,0:T(8,128)S(1)}, f32[128,128]{1,0:T(8,128)S(1)}, u32[]{:S(2)}, u32[]{:S(2)}) collective-permute-start(f32[128,128]{1,0:T(8,128)S(1)} %add.95), channel_id=1, source_target_pairs={{0,2},{1,3},{2,0},{3,1},{4,6},{5,7},{6,4},{7,5},{8,10},{9,11},{10,... | collective-permute-start | bytes 196616 | tf_op jit(solution)/shard_map/ppermute | solution.py:14
  31.1 2.7 %collective-permute-done.6 = f32[128,128]{1,0:T(8,128)S(1)} collective-permute-done((f32[128,128]{1,0:T(8,128)S(1)}, f32[128,128]{1,0:T(8,128)S(1)}, u32[]{:S(2)}, u32[]{:S(2)}) %collective-permute-start.6) | collective-permute-done | bytes 65568 | tf_op jit(solution)/shard_map/ppermute | solution.py:14
  33.8 1.6 %collective-permute-start.7 = (f32[128,128]{1,0:T(8,128)S(1)}, f32[128,128]{1,0:T(8,128)S(1)}, u32[]{:S(2)}, u32[]{:S(2)}) collective-permute-start(f32[128,128]{1,0:T(8,128)S(1)} %add.96), channel_id=1, source_target_pairs={{0,8},{4,12},{8,0},{12,4},{16,24},{20,28},{24,16},{28,20},{1,9},{5... | collective-permute-start | bytes 196616 | tf_op jit(solution)/shard_map/ppermute | solution.py:14
  35.4 1.2 %fusion.3 = f32[512,128]{1,0:T(8,128)S(1)} fusion(f32[512,128]{1,0:T(8,128)} %collective-permute-done.12, f32[512,128]{1,0:T(8,128)} %collective-permute-done.11, f32[512,128]{1,0:T(8,128)} %collective-permute-done.10, f32[2048,128]{1,0:T(8,128)S(1)} %fusion), kind=kLoop, calls=%fused_computation.15 | loop fusion | flops 196608 | bytes 1310720 | tf_op jit(solution)/shard_map/add | solution.py:154
  36.6 4.1 %collective-permute-start.15 = (f32[128,128]{1,0:T(8,128)S(1)}, f32[128,128]{1,0:T(8,128)S(1)}, u32[]{:S(2)}, u32[]{:S(2)}) collective-permute-start(f32[128,128]{1,0:T(8,128)S(1)} %get-tuple-element.16), channel_id=1, source_target_pairs={{0,3},{1,2},{2,1},{3,0},{4,7},{5,6},{6,5},{7,4},{8,11},{9,10},{10,... | collective-permute-start | bytes 196616 | tf_op jit(solution)/shard_map/ppermute | solution.py:14
  41.4 0.8 %collective-permute-start.8 = (f32[128,128]{1,0:T(8,128)S(1)}, f32[128,128]{1,0:T(8,128)S(1)}, u32[]{:S(2)}, u32[]{:S(2)}) collective-permute-start(f32[128,128]{1,0:T(8,128)S(1)} %add.97.gram_ref), channel_id=1, source_target_pairs={{0,16},{4,20},{8,24},{12,28},{16,0},{20,4},{24,8},{28,12},{1,17},{... | collective-permute-start | bytes 196616 | tf_op jit(solution)/shard_map/ppermute | solution.py:14
  42.2 0.9 %collective-permute-done.15 = f32[128,128]{1,0:T(8,128)S(1)} collective-permute-done((f32[128,128]{1,0:T(8,128)S(1)}, f32[128,128]{1,0:T(8,128)S(1)}, u32[]{:S(2)}, u32[]{:S(2)}) %collective-permute-start.15) | collective-permute-done | bytes 65568 | tf_op jit(solution)/shard_map/ppermute | solution.py:14
  43.1 2.8 %collective-permute-done.14 = f32[128,128]{1,0:T(8,128)S(1)} collective-permute-done((f32[128,128]{1,0:T(8,128)S(1)}, f32[128,128]{1,0:T(8,128)S(1)}, u32[]{:S(2)}, u32[]{:S(2)}) %collective-permute-start.14) | collective-permute-done | bytes 65568 | tf_op jit(solution)/shard_map/ppermute | solution.py:14
  46.0 1.9 %collective-permute-start.16 = (f32[128,128]{1,0:T(8,128)S(1)}, f32[128,128]{1,0:T(8,128)S(1)}, u32[]{:S(2)}, u32[]{:S(2)}) collective-permute-start(f32[128,128]{1,0:T(8,128)S(1)} %get-tuple-element.18), channel_id=1, source_target_pairs={{0,3},{1,2},{2,1},{3,0},{4,7},{5,6},{6,5},{7,4},{8,11},{9,10},{10,... | collective-permute-start | bytes 196616 | tf_op jit(solution)/shard_map/ppermute | solution.py:14
  47.8 3.9 %inverse_factor.1 = f32[128,128]{1,0:T(8,128)S(1)} custom-call(f32[128,128]{1,0:T(8,128)S(1)} %add.97.gram_ref, f32[128,128]{1,0:T(8,128)S(1)} %collective-permute-done.8.other_ref), custom_call_target="tpu_custom_call" | custom-call | flops 6000000000 | bytes 131072 | tf_op jit(solution)/shard_map/inverse_factor/pallas_call | solution.py:97
  52.0 2.3 %collective-permute-start.18 = (f32[128,128]{1,0:T(8,128)S(1)}, f32[128,128]{1,0:T(8,128)S(1)}, u32[]{:S(2)}, u32[]{:S(2)}) collective-permute-start(f32[128,128]{1,0:T(8,128)S(1)} %get-tuple-element.18), channel_id=1, source_target_pairs={{0,1},{1,0},{2,3},{3,2},{4,5},{5,4},{6,7},{7,6},{8,9},{9,8},{10,11... | collective-permute-start | bytes 196616 | tf_op jit(solution)/shard_map/ppermute | solution.py:14
  54.4 3.3 %collective-permute-done.17 = f32[128,128]{1,0:T(8,128)S(1)} collective-permute-done((f32[128,128]{1,0:T(8,128)S(1)}, f32[128,128]{1,0:T(8,128)S(1)}, u32[]{:S(2)}, u32[]{:S(2)}) %collective-permute-start.17) | collective-permute-done | bytes 65568 | tf_op jit(solution)/shard_map/ppermute | solution.py:14
  58.2 1.5 %collective-permute-start.21 = (bf16[512,128]{1,0:T(8,128)(2,1)S(1)}, bf16[512,128]{1,0:T(8,128)(2,1)S(1)}, u32[]{:S(2)}, u32[]{:S(2)}) collective-permute-start(bf16[512,128]{1,0:T(8,128)(2,1)S(1)} %convert_element_type.22), channel_id=1, source_target_pairs={{0,24},{4,28},{8,16},{12,20},{16,8},{20,12},{24,0},{28,4},{1,25},{... | collective-permute-start | bytes 393224 | tf_op jit(solution)/shard_map/ppermute | solution.py:14
  60.3 1.4 %collective-permute-start.19 = (bf16[512,128]{1,0:T(8,128)(2,1)S(1)}, bf16[512,128]{1,0:T(8,128)(2,1)S(1)}, u32[]{:S(2)}, u32[]{:S(2)}) collective-permute-start(bf16[512,128]{1,0:T(8,128)(2,1)S(1)} %convert_element_type.22), channel_id=1, source_target_pairs={{0,8},{4,12},{8,0},{12,4},{16,24},{20,28},{24,16},{28,20},{1,9},{5... | collective-permute-start | bytes 393224 | tf_op jit(solution)/shard_map/ppermute | solution.py:14
  61.7 2.5 %collective-permute-done.21 = bf16[512,128]{1,0:T(8,128)(2,1)S(1)} collective-permute-done((bf16[512,128]{1,0:T(8,128)(2,1)S(1)}, bf16[512,128]{1,0:T(8,128)(2,1)S(1)}, u32[]{:S(2)}, u32[]{:S(2)}) %collective-permute-start.21) | collective-permute-done | bytes 131104 | tf_op jit(solution)/shard_map/ppermute | solution.py:14
  64.2 1.3 %collective-permute-done.20 = bf16[512,128]{1,0:T(8,128)(2,1)S(1)} collective-permute-done((bf16[512,128]{1,0:T(8,128)(2,1)S(1)}, bf16[512,128]{1,0:T(8,128)(2,1)S(1)}, u32[]{:S(2)}, u32[]{:S(2)}) %collective-permute-start.20) | collective-permute-done | bytes 131104 | tf_op jit(solution)/shard_map/ppermute | solution.py:14
  66.2 0.9 %multiply_reduce_fusion.1 = f32[512]{0:T(512)S(1)} fusion(bf16[512,2048]{1,0:T(8,128)(2,1)S(1)} %copy-done.1, f32[512,128]{1,0:T(8,128)S(1)} %fusion.10, bf16[512,128]{1,0:T(8,128)(2,1)S(1)} %collective-permute-done.21, bf16[512,128]{1,0:T(8,128)(2,1)S(1)} %collective-permute-done.20, bf16[512,128]{1,0:T(8,128)(2,1)S(1)} %collective-permute-done.19, ...), kind=kOutput, calls=%fused_computation.1 | convolution fusion | flops 275840512 | bytes 2885632 | tf_op jit(solution)/shard_map/dot_general | solution.py:186
  67.5 0.9 %multiply_reduce_fusion = f32[512]{0:T(512)S(1)} fusion(bf16[512,2048]{1,0:T(8,128)(2,1)S(1)} %get-tuple-element.12, bf16[2048,128]{1,0:T(8,128)(2,1)S(1)} %collective-permute-done.22, f32[512,128]{1,0:T(8,128)S(1)} %fusion.10), kind=kOutput, calls=%fused_computation | convolution fusion | flops 273743360 | bytes 2885632 | tf_op jit(solution)/shard_map/dot_general | solution.py:186
  (54 shorter events, 8.0 us)
Async XLA Ops:
  0.6 8.2 %collective-permute-start.2 = (bf16[512,128]{1,0:T(8,128)(2,1)}, bf16[512,128]{1,0:T(8,128)(2,1)S(1)}, u32[]{:S(2)}, u32[]{:S(2)}) collective-permute-start(bf16[512,128]{1,0:T(8,128)(2,1)} %param.3), channel_id=1, source_target_pairs={{0,24},{4,28},{8,16},{12,20},{16,8},{20,12},{24,0},{28,4},{1,25},{... | collective-permute-start | bytes 393224 | tf_op jit(solution)/shard_map/ppermute | solution.py:14
  4.6 6.5 %collective-permute-start.1 = (bf16[512,128]{1,0:T(8,128)(2,1)}, bf16[512,128]{1,0:T(8,128)(2,1)S(1)}, u32[]{:S(2)}, u32[]{:S(2)}) collective-permute-start(bf16[512,128]{1,0:T(8,128)(2,1)} %param.3), channel_id=1, source_target_pairs={{0,16},{4,20},{8,24},{12,28},{16,0},{20,4},{24,8},{28,12},{1,17},{... | collective-permute-start | bytes 393224 | tf_op jit(solution)/shard_map/ppermute | solution.py:14
  5.1 6.3 %collective-permute-start = (bf16[512,128]{1,0:T(8,128)(2,1)}, bf16[512,128]{1,0:T(8,128)(2,1)S(1)}, u32[]{:S(2)}, u32[]{:S(2)}) collective-permute-start(bf16[512,128]{1,0:T(8,128)(2,1)} %param.3), channel_id=1, source_target_pairs={{0,8},{4,12},{8,0},{12,4},{16,24},{20,28},{24,16},{28,20},{1,9},{5... | collective-permute-start | bytes 393224 | tf_op jit(solution)/shard_map/ppermute | solution.py:14
  7.9 3.5 %copy-start.4 = (bf16[512,128]{1,0:T(8,128)(2,1)S(1)}, bf16[512,128]{1,0:T(8,128)(2,1)}, u32[]{:S(2)}) copy-start(bf16[512,128]{1,0:T(8,128)(2,1)} %param.3) | copy-start | bytes 393220
  8.5 6.8 %copy-start = (bf16[512,2048]{1,0:T(8,128)(2,1)}, bf16[512,2048]{1,0:T(8,128)(2,1)S(1)}, u32[]{:S(2)}) copy-start(bf16[512,2048]{1,0:T(8,128)(2,1)S(1)} %get-tuple-element.10) | copy-start | bytes 6291460
  11.4 2.0 %collective-permute-start.3 = (bf16[2048,128]{1,0:T(8,128)(2,1)S(1)}, bf16[2048,128]{1,0:T(8,128)(2,1)S(1)}, u32[]{:S(2)}, u32[]{:S(2)}) collective-permute-start(bf16[2048,128]{1,0:T(8,128)(2,1)S(1)} %pad_maximum_fusion.2), channel_id=1, source_target_pairs={{0,4},{4,0},{8,12},{12,8},{16,20},{20,16},{24,28},{28,24},{1,5},{5... | collective-permute-start | bytes 1572872 | tf_op jit(solution)/shard_map/ppermute | solution.py:14
  15.1 2.7 %collective-permute-start.9 = (f32[2048,128]{1,0:T(8,128)S(1)}, f32[2048,128]{1,0:T(8,128)S(1)}, u32[]{:S(2)}, u32[]{:S(2)}) collective-permute-start(f32[2048,128]{1,0:T(8,128)S(1)} %slice_add_fusion), channel_id=1, source_target_pairs={{0,4},{4,0},{8,12},{12,8},{16,20},{20,16},{24,28},{28,24},{1,5},{5... | collective-permute-start | bytes 3145736 | tf_op jit(solution)/shard_map/ppermute | solution.py:14
  18.9 16.6 %collective-permute-start.12 = (f32[512,128]{1,0:T(8,128)}, f32[512,128]{1,0:T(8,128)}, u32[]{:S(2)}, u32[]{:S(2)}) collective-permute-start(f32[512,128]{1,0:T(8,128)} %get-tuple-element.28), channel_id=1, source_target_pairs={{0,16},{4,20},{8,24},{12,28},{16,0},{20,4},{24,8},{28,12},{1,17},{... | collective-permute-start | bytes 786440 | tf_op jit(solution)/shard_map/ppermute | solution.py:14
  20.3 15.1 %collective-permute-start.11 = (f32[512,128]{1,0:T(8,128)}, f32[512,128]{1,0:T(8,128)}, u32[]{:S(2)}, u32[]{:S(2)}) collective-permute-start(f32[512,128]{1,0:T(8,128)} %get-tuple-element.29), channel_id=1, source_target_pairs={{0,8},{4,12},{8,0},{12,4},{16,24},{20,28},{24,16},{28,20},{1,9},{5... | collective-permute-start | bytes 786440 | tf_op jit(solution)/shard_map/ppermute | solution.py:14
  21.0 14.4 %collective-permute-start.10 = (f32[512,128]{1,0:T(8,128)}, f32[512,128]{1,0:T(8,128)}, u32[]{:S(2)}, u32[]{:S(2)}) collective-permute-start(f32[512,128]{1,0:T(8,128)} %get-tuple-element.27), channel_id=1, source_target_pairs={{0,24},{4,28},{8,16},{12,20},{16,8},{20,12},{24,0},{28,4},{1,25},{... | collective-permute-start | bytes 786440 | tf_op jit(solution)/shard_map/ppermute | solution.py:14
  22.7 1.3 %collective-permute-start.4 = (f32[128,128]{1,0:T(8,128)S(1)}, f32[128,128]{1,0:T(8,128)S(1)}, u32[]{:S(2)}, u32[]{:S(2)}) collective-permute-start(f32[128,128]{1,0:T(8,128)S(1)} %fusion.20), channel_id=1, source_target_pairs={{0,4},{4,0},{8,12},{12,8},{16,20},{20,16},{24,28},{28,24},{1,5},{5... | collective-permute-start | bytes 196616 | tf_op jit(solution)/shard_map/ppermute | solution.py:14
  24.1 4.3 %collective-permute-start.5 = (f32[128,128]{1,0:T(8,128)S(1)}, f32[128,128]{1,0:T(8,128)S(1)}, u32[]{:S(2)}, u32[]{:S(2)}) collective-permute-start(f32[128,128]{1,0:T(8,128)S(1)} %add.94), channel_id=1, source_target_pairs={{0,1},{1,0},{2,3},{3,2},{4,5},{5,4},{6,7},{7,6},{8,9},{9,8},{10,11... | collective-permute-start | bytes 196616 | tf_op jit(solution)/shard_map/ppermute | solution.py:14
  28.4 5.4 %collective-permute-start.6 = (f32[128,128]{1,0:T(8,128)S(1)}, f32[128,128]{1,0:T(8,128)S(1)}, u32[]{:S(2)}, u32[]{:S(2)}) collective-permute-start(f32[128,128]{1,0:T(8,128)S(1)} %add.95), channel_id=1, source_target_pairs={{0,2},{1,3},{2,0},{3,1},{4,6},{5,7},{6,4},{7,5},{8,10},{9,11},{10,... | collective-permute-start | bytes 196616 | tf_op jit(solution)/shard_map/ppermute | solution.py:14
  33.8 7.6 %collective-permute-start.7 = (f32[128,128]{1,0:T(8,128)S(1)}, f32[128,128]{1,0:T(8,128)S(1)}, u32[]{:S(2)}, u32[]{:S(2)}) collective-permute-start(f32[128,128]{1,0:T(8,128)S(1)} %add.96), channel_id=1, source_target_pairs={{0,8},{4,12},{8,0},{12,4},{16,24},{20,28},{24,16},{28,20},{1,9},{5... | collective-permute-start | bytes 196616 | tf_op jit(solution)/shard_map/ppermute | solution.py:14
  36.6 6.4 %collective-permute-start.15 = (f32[128,128]{1,0:T(8,128)S(1)}, f32[128,128]{1,0:T(8,128)S(1)}, u32[]{:S(2)}, u32[]{:S(2)}) collective-permute-start(f32[128,128]{1,0:T(8,128)S(1)} %get-tuple-element.16), channel_id=1, source_target_pairs={{0,3},{1,2},{2,1},{3,0},{4,7},{5,6},{6,5},{7,4},{8,11},{9,10},{10,... | collective-permute-start | bytes 196616 | tf_op jit(solution)/shard_map/ppermute | solution.py:14
  40.7 5.2 %collective-permute-start.14 = (f32[128,128]{1,0:T(8,128)S(1)}, f32[128,128]{1,0:T(8,128)S(1)}, u32[]{:S(2)}, u32[]{:S(2)}) collective-permute-start(f32[128,128]{1,0:T(8,128)S(1)} %get-tuple-element.15), channel_id=1, source_target_pairs={{0,2},{1,3},{2,0},{3,1},{4,6},{5,7},{6,4},{7,5},{8,10},{9,11},{10,... | collective-permute-start | bytes 196616 | tf_op jit(solution)/shard_map/ppermute | solution.py:14
  40.7 5.2 %collective-permute-start.13 = (f32[128,128]{1,0:T(8,128)S(1)}, f32[128,128]{1,0:T(8,128)S(1)}, u32[]{:S(2)}, u32[]{:S(2)}) collective-permute-start(f32[128,128]{1,0:T(8,128)S(1)} %get-tuple-element.14), channel_id=1, source_target_pairs={{0,1},{1,0},{2,3},{3,2},{4,5},{5,4},{6,7},{7,6},{8,9},{9,8},{10,11... | collective-permute-start | bytes 196616 | tf_op jit(solution)/shard_map/ppermute | solution.py:14
  41.4 6.4 %collective-permute-start.8 = (f32[128,128]{1,0:T(8,128)S(1)}, f32[128,128]{1,0:T(8,128)S(1)}, u32[]{:S(2)}, u32[]{:S(2)}) collective-permute-start(f32[128,128]{1,0:T(8,128)S(1)} %add.97.gram_ref), channel_id=1, source_target_pairs={{0,16},{4,20},{8,24},{12,28},{16,0},{20,4},{24,8},{28,12},{1,17},{... | collective-permute-start | bytes 196616 | tf_op jit(solution)/shard_map/ppermute | solution.py:14
  46.0 8.4 %collective-permute-start.16 = (f32[128,128]{1,0:T(8,128)S(1)}, f32[128,128]{1,0:T(8,128)S(1)}, u32[]{:S(2)}, u32[]{:S(2)}) collective-permute-start(f32[128,128]{1,0:T(8,128)S(1)} %get-tuple-element.18), channel_id=1, source_target_pairs={{0,3},{1,2},{2,1},{3,0},{4,7},{5,6},{6,5},{7,4},{8,11},{9,10},{10,... | collective-permute-start | bytes 196616 | tf_op jit(solution)/shard_map/ppermute | solution.py:14
  51.7 14.5 %copy-start.1 = (bf16[512,2048]{1,0:T(8,128)(2,1)S(1)}, bf16[512,2048]{1,0:T(8,128)(2,1)}, u32[]{:S(2)}) copy-start(bf16[512,2048]{1,0:T(8,128)(2,1)} %copy-done) | copy-start | bytes 6291460
  51.8 5.9 %collective-permute-start.17 = (f32[128,128]{1,0:T(8,128)S(1)}, f32[128,128]{1,0:T(8,128)S(1)}, u32[]{:S(2)}, u32[]{:S(2)}) collective-permute-start(f32[128,128]{1,0:T(8,128)S(1)} %get-tuple-element.18), channel_id=1, source_target_pairs={{0,2},{1,3},{2,0},{3,1},{4,6},{5,7},{6,4},{7,5},{8,10},{9,11},{10,... | collective-permute-start | bytes 196616 | tf_op jit(solution)/shard_map/ppermute | solution.py:14
  52.0 5.7 %collective-permute-start.18 = (f32[128,128]{1,0:T(8,128)S(1)}, f32[128,128]{1,0:T(8,128)S(1)}, u32[]{:S(2)}, u32[]{:S(2)}) collective-permute-start(f32[128,128]{1,0:T(8,128)S(1)} %get-tuple-element.18), channel_id=1, source_target_pairs={{0,1},{1,0},{2,3},{3,2},{4,5},{5,4},{6,7},{7,6},{8,9},{9,8},{10,11... | collective-permute-start | bytes 196616 | tf_op jit(solution)/shard_map/ppermute | solution.py:14
  58.1 9.1 %copy-start.2 = (f32[512,128]{1,0:T(8,128)}, f32[512,128]{1,0:T(8,128)S(1)}, u32[]{:S(2)}) copy-start(f32[512,128]{1,0:T(8,128)S(1)} %fusion.8) | copy-start | bytes 786436
  58.2 6.0 %collective-permute-start.21 = (bf16[512,128]{1,0:T(8,128)(2,1)S(1)}, bf16[512,128]{1,0:T(8,128)(2,1)S(1)}, u32[]{:S(2)}, u32[]{:S(2)}) collective-permute-start(bf16[512,128]{1,0:T(8,128)(2,1)S(1)} %convert_element_type.22), channel_id=1, source_target_pairs={{0,24},{4,28},{8,16},{12,20},{16,8},{20,12},{24,0},{28,4},{1,25},{... | collective-permute-start | bytes 393224 | tf_op jit(solution)/shard_map/ppermute | solution.py:14
  59.6 5.9 %collective-permute-start.20 = (bf16[512,128]{1,0:T(8,128)(2,1)S(1)}, bf16[512,128]{1,0:T(8,128)(2,1)S(1)}, u32[]{:S(2)}, u32[]{:S(2)}) collective-permute-start(bf16[512,128]{1,0:T(8,128)(2,1)S(1)} %convert_element_type.22), channel_id=1, source_target_pairs={{0,16},{4,20},{8,24},{12,28},{16,0},{20,4},{24,8},{28,12},{1,17},{... | collective-permute-start | bytes 393224 | tf_op jit(solution)/shard_map/ppermute | solution.py:14
  60.3 5.2 %collective-permute-start.19 = (bf16[512,128]{1,0:T(8,128)(2,1)S(1)}, bf16[512,128]{1,0:T(8,128)(2,1)S(1)}, u32[]{:S(2)}, u32[]{:S(2)}) collective-permute-start(bf16[512,128]{1,0:T(8,128)(2,1)S(1)} %convert_element_type.22), channel_id=1, source_target_pairs={{0,8},{4,12},{8,0},{12,4},{16,24},{20,28},{24,16},{28,20},{1,9},{5... | collective-permute-start | bytes 393224 | tf_op jit(solution)/shard_map/ppermute | solution.py:14
  65.5 2.0 %collective-permute-start.22 = (bf16[2048,128]{1,0:T(8,128)(2,1)S(1)}, bf16[2048,128]{1,0:T(8,128)(2,1)S(1)}, u32[]{:S(2)}, u32[]{:S(2)}) collective-permute-start(bf16[2048,128]{1,0:T(8,128)(2,1)S(1)} %pad_maximum_fusion.3), channel_id=1, source_target_pairs={{0,4},{4,0},{8,12},{12,8},{16,20},{20,16},{24,28},{28,24},{1,5},{5... | collective-permute-start | bytes 1572872 | tf_op jit(solution)/shard_map/ppermute | solution.py:14
  66.2 1.3 %copy-start.3 = (f32[512,128]{1,0:T(8,128)}, f32[512,128]{1,0:T(8,128)S(1)}, u32[]{:S(2)}) copy-start(f32[512,128]{1,0:T(8,128)S(1)} %fusion.10) | copy-start | bytes 786436
